TPU v7x, 32 devices: a whole 2x2x4 slice. The times are simulated.
32 devices in a mesh: seq: 8 (over z, x), tp: 4 (over y, core).
Axes of the slice: x: 2, y: 2, z: 4, core: 2. Of those that a mesh axis runs over, the one named last changes fastest.
Arguments:
- hidden_in: bfloat16 [4096, 2048], P(('seq', 'tp')), may hold values from -6 to 6
- lengths: int32 [8], replicated, may hold values from 1 to 3869, as said below
- ln1_gain: float32 [2048], replicated, may hold values from 0.25 to 1.75
- ln1_bias: float32 [2048], replicated, may hold values from -3 to 3
- w_query: bfloat16 [2048, 2048], P(None, 'tp'), may hold values from -0.125 to 0.125
- b_query: float32 [2048], P('tp'), may hold values from -3 to 3
- w_kv: bfloat16 [2048, 256], replicated, may hold values from -0.125 to 0.125
- b_value: float32 [128], replicated, may hold values from -0.12 to 0.12
- w_out: bfloat16 [2048, 2048], P('tp'), may hold values from -3 to 3
- b_out: float32 [2048], replicated, may hold values from -3 to 3
- ln2_gain: float32 [2048], replicated, may hold values from 0.25 to 1.75
- ln2_bias: float32 [2048], replicated, may hold values from -3 to 3
- w_fc: bfloat16 [2048, 8192], P(None, 'tp'), may hold values from -0.125 to 0.125
- b_fc: float32 [8192], P('tp'), may hold values from -3 to 3
- w_proj: bfloat16 [8192, 2048], P('tp'), may hold values from -0.0625 to 0.0625
- b_proj: float32 [2048], replicated, may hold values from -3 to 3
- grad_out: bfloat16 [4096, 2048], P(('seq', 'tp')), may hold values from -6 to 6
Outputs:
- layer_out: bfloat16 [4096, 2048], P(('seq', 'tp'))
- grad_in: float32 [4096, 2048], P(('seq', 'tp'))
- grad_ln1_gain: float32 [2048], replicated
- grad_ln1_bias: float32 [2048], replicated
- grad_w_query: float32 [2048, 2048], P('seq', 'tp')
- grad_b_query: float32 [2048], P('tp')
- grad_w_kv: float32 [2048, 256], replicated
- grad_b_value: float32 [128], replicated
- grad_w_out: float32 [2048, 2048], P('tp', 'seq')
- grad_b_out: float32 [2048], replicated
- grad_ln2_gain: float32 [2048], replicated
- grad_ln2_bias: float32 [2048], replicated
- grad_w_fc: float32 [2048, 8192], P('seq', 'tp')
- grad_b_fc: float32 [8192], P('tp')
- grad_w_proj: float32 [8192, 2048], P('tp', 'seq')
- grad_b_proj: float32 [2048], replicated
Inputs may be any that keep to these rules, and one draw needn't show every extreme that they name: The 8 document lengths of the window, in order, sum to 4096. All but one are short, at most max(1, 64); they come in pairs whose two lengths add to max(1, 64) + 1, with one more of (max(1, 64) + 1) // 2 when (7) is odd, in an order drawn from the seed. The remaining one, at a place drawn from the seed, takes the rest of the window, so it begins within the first 512 tokens and ends within the last 512.
All inputs are finite; a program needn't handle non-finite values.
Results may differ from a plain program's by a relative error of at most 0.025.
Values may be sent and summed in bfloat16 or wider, within the bound.
No kernel may reach another device: no remote copies, remote signals or barrier semaphores. Data moves between devices by JAX's collectives and lax.ppermute only.
A program may use at most 192 MiB of HBM per device.

v0:
```python
import math

import jax
import jax.numpy as jnp
from jax import lax
from jax.sharding import PartitionSpec as P

EPS = 1e-05
NEG = -1e30


def layer_norm(features, gain, shift):
    centered = features - jnp.mean(features, axis=-1, keepdims=True)
    variance = jnp.mean(centered * centered, axis=-1, keepdims=True)
    return centered * lax.rsqrt(variance + EPS) * gain + shift


def gelu_tanh(values):
    return jax.nn.gelu(values, approximate=True)


def segment_ids(lengths, length_all):
    doc_ends = jnp.cumsum(lengths)
    places = jnp.arange(length_all, dtype=jnp.int32)
    return jnp.sum((doc_ends[None, :] <= places[:, None]).astype(jnp.int32), axis=1)


def pair_mask(segments, query_first, query_count, key_first, key_count):
    query_place = query_first + jnp.arange(query_count, dtype=jnp.int32)
    key_place = key_first + jnp.arange(key_count, dtype=jnp.int32)
    query_seg = lax.dynamic_slice_in_dim(segments, query_first, query_count)
    key_seg = lax.dynamic_slice_in_dim(segments, key_first, key_count)
    return (key_place[None, :] <= query_place[:, None]) & (key_seg[None, :] == query_seg[:, None])


def block_needed(segments, query_first, query_count, key_first, key_count):
    first_seg = lax.dynamic_index_in_dim(segments, query_first, keepdims=False)
    last_seg = lax.dynamic_index_in_dim(segments, key_first + key_count - 1, keepdims=False)
    return (key_first <= query_first + query_count - 1) & (last_seg >= first_seg)


def masked_scores(queries, key_block, allowed, scaling):
    head_dim = queries.shape[2]
    raw_scores = jnp.einsum(
        "qhd,kd->qhk", queries, key_block[:, :head_dim], preferred_element_type=jnp.float32
    )
    return jnp.where(allowed[:, None, :], raw_scores * scaling, NEG)


def key_values(normed, w_kv, b_value):
    bias_row = jnp.concatenate([jnp.zeros_like(b_value), b_value])
    return (jnp.dot(normed, w_kv, preferred_element_type=jnp.float32) + bias_row).astype(
        jnp.bfloat16
    )


def attention_stats(queries, kv_all, segments, query_first, scaling):
    row_count, head_count, head_dim = queries.shape
    width = math.gcd(kv_all.shape[0], 1024)

    def visit(block_index, carried):
        key_first = block_index * width

        def update(carried):
            running_max, running_sum = carried
            key_block = lax.dynamic_slice_in_dim(kv_all, key_first, width, 0)
            allowed = pair_mask(segments, query_first, row_count, key_first, width)
            scores = masked_scores(queries, key_block, allowed, scaling)
            new_max = jnp.maximum(running_max, jnp.max(scores, axis=-1))
            weights = jnp.where(allowed[:, None, :], jnp.exp(scores - new_max[..., None]), 0.0)
            return (
                new_max,
                running_sum * jnp.exp(running_max - new_max) + jnp.sum(weights, axis=-1),
            )

        live = block_needed(segments, query_first, row_count, key_first, width)
        return lax.cond(live, update, lambda kept: kept, carried)

    start_state = (
        jnp.full((row_count, head_count), NEG, jnp.float32),
        jnp.zeros((row_count, head_count), jnp.float32),
    )
    running_max, running_sum = lax.fori_loop(0, kv_all.shape[0] // width, visit, start_state)
    return running_max + jnp.log(running_sum)


def attention_output(queries, kv_all, segments, query_first, scaling, log_norm):
    row_count, head_count, head_dim = queries.shape
    width = math.gcd(kv_all.shape[0], 1024)

    def visit(block_index, accumulated):
        key_first = block_index * width

        def update(accumulated):
            key_block = lax.dynamic_slice_in_dim(kv_all, key_first, width, 0)
            allowed = pair_mask(segments, query_first, row_count, key_first, width)
            scores = masked_scores(queries, key_block, allowed, scaling)
            weights = jnp.where(
                allowed[:, None, :], jnp.exp(scores - log_norm[..., None]), 0.0
            ).astype(jnp.bfloat16)
            return accumulated + jnp.einsum(
                "qhk,kd->qhd", weights, key_block[:, head_dim:], preferred_element_type=jnp.float32
            )

        live = block_needed(segments, query_first, row_count, key_first, width)
        return lax.cond(live, update, lambda kept: kept, accumulated)

    return lax.fori_loop(
        0,
        kv_all.shape[0] // width,
        visit,
        jnp.zeros((row_count, head_count, head_dim), jnp.float32),
    )


def attention_grads(queries, kv_all, segments, query_first, scaling, log_norm, out_grads, delta):
    row_count, head_count, head_dim = queries.shape
    total = kv_all.shape[0]
    width = math.gcd(total, 1024)

    def visit(block_index, carried):
        key_first = block_index * width

        def update(carried):
            query_acc, pair_acc = carried
            key_block = lax.dynamic_slice_in_dim(kv_all, key_first, width, 0)
            allowed = pair_mask(segments, query_first, row_count, key_first, width)
            scores = masked_scores(queries, key_block, allowed, scaling)
            weights = jnp.where(allowed[:, None, :], jnp.exp(scores - log_norm[..., None]), 0.0)
            weight_grads = jnp.einsum(
                "qhd,kd->qhk",
                out_grads,
                key_block[:, head_dim:],
                preferred_element_type=jnp.float32,
            )
            score_grads = (weights * (weight_grads - delta[..., None]) * scaling).astype(
                jnp.bfloat16
            )
            query_acc = query_acc + jnp.einsum(
                "qhk,kd->qhd",
                score_grads,
                key_block[:, :head_dim],
                preferred_element_type=jnp.float32,
            )
            key_grads = jnp.einsum(
                "qhk,qhd->kd", score_grads, queries, preferred_element_type=jnp.float32
            )
            value_grads = jnp.einsum(
                "qhk,qhd->kd",
                weights.astype(jnp.bfloat16),
                out_grads,
                preferred_element_type=jnp.float32,
            )
            joined = jnp.concatenate([key_grads, value_grads], axis=1)
            return (query_acc, lax.dynamic_update_slice_in_dim(pair_acc, joined, key_first, 0))

        live = block_needed(segments, query_first, row_count, key_first, width)
        return lax.cond(live, update, lambda kept: kept, carried)

    start_state = (
        jnp.zeros((row_count, head_count, head_dim), jnp.float32),
        jnp.zeros((total, 2 * head_dim), jnp.float32),
    )
    return lax.fori_loop(0, total // width, visit, start_state)


def spread_rows(normed):
    return lax.all_gather(normed, "tp", axis=0, tiled=True)


def merge_rows(partial_value):
    return lax.psum_scatter(
        partial_value.astype(jnp.bfloat16), "tp", scatter_dimension=0, tiled=True
    ).astype(jnp.float32)


def spread_grads(grad_rows):
    return lax.all_gather(grad_rows, "tp", axis=0, tiled=True)


def merge_grads(partial_value):
    return lax.psum_scatter(
        partial_value.astype(jnp.bfloat16), "tp", scatter_dimension=0, tiled=True
    ).astype(jnp.float32)


def row_weight_grads(gathered, column_grads):
    return lax.psum_scatter(
        jnp.einsum("rk,rf->kf", gathered, column_grads, preferred_element_type=jnp.float32).astype(
            jnp.bfloat16
        ),
        "seq",
        scatter_dimension=0,
        tiled=True,
    ).astype(jnp.float32)


def column_weight_grads(partial_value):
    return lax.psum_scatter(
        partial_value.astype(jnp.bfloat16), "seq", scatter_dimension=1, tiled=True
    ).astype(jnp.float32)


def body(
    hidden_in,
    lengths,
    ln1_gain,
    ln1_bias,
    w_query,
    b_query,
    w_kv,
    b_value,
    w_out,
    b_out,
    ln2_gain,
    ln2_bias,
    w_fc,
    b_fc,
    w_proj,
    b_proj,
    grad_out,
):
    seq_count = lax.axis_size("seq")
    tp_count = lax.axis_size("tp")
    group_rows = hidden_in.shape[0] * tp_count
    window = group_rows * seq_count
    head_dim = b_value.shape[0]
    local_heads = w_query.shape[1] // head_dim
    scaling = head_dim ** (-0.5)
    query_first = lax.axis_index("seq") * group_rows
    segments = segment_ids(lengths, window)
    residual = hidden_in.astype(jnp.float32)
    normed_one = layer_norm(residual, ln1_gain, ln1_bias).astype(jnp.bfloat16)
    gathered_one = spread_rows(normed_one)
    query_flat = (
        jnp.dot(gathered_one, w_query, preferred_element_type=jnp.float32) + b_query
    ).astype(jnp.bfloat16)
    queries = query_flat.reshape(group_rows, local_heads, head_dim)
    kv_all = lax.all_gather(
        key_values(normed_one, w_kv, b_value), ("seq", "tp"), axis=0, tiled=True
    )
    log_norm = attention_stats(queries, kv_all, segments, query_first, scaling)
    attended_full = attention_output(queries, kv_all, segments, query_first, scaling, log_norm)
    attended = attended_full.astype(jnp.bfloat16).reshape(group_rows, local_heads * head_dim)
    middle = (
        residual + merge_rows(jnp.dot(attended, w_out, preferred_element_type=jnp.float32)) + b_out
    )
    normed_two = layer_norm(middle, ln2_gain, ln2_bias).astype(jnp.bfloat16)
    gathered_two = spread_rows(normed_two)
    pre_act = jnp.dot(gathered_two, w_fc, preferred_element_type=jnp.float32) + b_fc
    activated_full, gelu_back = jax.vjp(gelu_tanh, pre_act)
    activated = activated_full.astype(jnp.bfloat16)
    mlp_sum = merge_rows(jnp.dot(activated, w_proj, preferred_element_type=jnp.float32))
    layer_out = (middle + mlp_sum + b_proj).astype(jnp.bfloat16)
    upstream = grad_out.astype(jnp.float32)
    grad_bias_proj = jnp.sum(upstream, axis=0)
    mlp_grads = spread_grads(upstream.astype(jnp.bfloat16))
    act_grads = jnp.einsum("rd,fd->rf", mlp_grads, w_proj, preferred_element_type=jnp.float32)
    pre_grads = gelu_back(act_grads)[0]
    grad_bias_fc = jnp.sum(pre_grads, axis=0)
    pre_low = pre_grads.astype(jnp.bfloat16)
    grad_proj_part = jnp.einsum(
        "rf,rd->fd", activated, mlp_grads, preferred_element_type=jnp.float32
    )
    grad_fc = row_weight_grads(gathered_two, pre_low)
    normed_two_grads = merge_grads(
        jnp.einsum("rf,df->rd", pre_low, w_fc, preferred_element_type=jnp.float32)
    )
    ln_two_back = jax.vjp(layer_norm, middle, ln2_gain, ln2_bias)[1]
    middle_from_norm, grad_gain_two, grad_bias_two = ln_two_back(normed_two_grads)
    middle_grads = upstream + middle_from_norm
    grad_bias_out = jnp.sum(middle_grads, axis=0)
    attention_grads_rows = spread_grads(middle_grads.astype(jnp.bfloat16))
    grad_proj = column_weight_grads(grad_proj_part)
    attended_grads = jnp.einsum(
        "rd,ed->re", attention_grads_rows, w_out, preferred_element_type=jnp.float32
    ).astype(jnp.bfloat16)
    grad_out_part = jnp.einsum(
        "re,rd->ed", attended, attention_grads_rows, preferred_element_type=jnp.float32
    )
    out_grads = attended_grads.reshape(group_rows, local_heads, head_dim)
    delta = jnp.sum(out_grads.astype(jnp.float32) * attended_full, axis=-1)
    query_grads, pair_partial = attention_grads(
        queries, kv_all, segments, query_first, scaling, log_norm, out_grads, delta
    )
    query_grads_flat = query_grads.reshape(group_rows, local_heads * head_dim)
    grad_bias_query = jnp.sum(query_grads_flat, axis=0)
    query_low = query_grads_flat.astype(jnp.bfloat16)
    grad_query = row_weight_grads(gathered_one, query_low)
    group_pair_grads = lax.psum_scatter(
        pair_partial.astype(jnp.bfloat16), "seq", scatter_dimension=0, tiled=True
    )
    pair_grads = lax.psum_scatter(group_pair_grads, "tp", scatter_dimension=0, tiled=True).astype(
        jnp.float32
    )
    grad_bias_value = jnp.sum(pair_grads[:, head_dim:], axis=0)
    pair_low = pair_grads.astype(jnp.bfloat16)
    grad_kv_part = jnp.einsum("rk,re->ke", normed_one, pair_low, preferred_element_type=jnp.float32)
    normed_one_grads = merge_grads(
        jnp.einsum("re,ke->rk", query_low, w_query, preferred_element_type=jnp.float32)
    )
    normed_one_grads = normed_one_grads + jnp.einsum(
        "re,ke->rk", pair_low, w_kv, preferred_element_type=jnp.float32
    )
    ln_one_back = jax.vjp(layer_norm, residual, ln1_gain, ln1_bias)[1]
    input_from_norm, grad_gain_one, grad_bias_one = ln_one_back(normed_one_grads)
    grad_in = middle_grads + input_from_norm
    grad_out_weight = column_weight_grads(grad_out_part)
    shared = lax.psum(
        (
            grad_kv_part,
            grad_gain_one,
            grad_bias_one,
            grad_bias_out,
            grad_gain_two,
            grad_bias_two,
            grad_bias_proj,
            grad_bias_value,
        ),
        ("seq", "tp"),
    )
    split = lax.psum((grad_bias_query, grad_bias_fc), "seq")
    return (
        layer_out,
        grad_in,
        shared[1],
        shared[2],
        grad_query,
        split[0],
        shared[0],
        shared[7],
        grad_out_weight,
        shared[3],
        shared[4],
        shared[5],
        grad_fc,
        split[1],
        grad_proj,
        shared[6],
    )


def solution(mesh):
    placed = (
        P(("seq", "tp"), None),
        P(),
        P(),
        P(),
        P(None, "tp"),
        P("tp"),
        P(),
        P(),
        P("tp", None),
        P(),
        P(),
        P(),
        P(None, "tp"),
        P("tp"),
        P("tp", None),
        P(),
        P(("seq", "tp"), None),
    )
    return jax.shard_map(
        body,
        mesh=mesh,
        in_specs=placed,
        out_specs=(
            P(("seq", "tp"), None),
            P(("seq", "tp"), None),
            P(),
            P(),
            P("seq", "tp"),
            P("tp"),
            P(),
            P(),
            P("tp", "seq"),
            P(),
            P(),
            P(),
            P("seq", "tp"),
            P("tp"),
            P("tp", "seq"),
            P(),
        ),
        check_vma=False,
    )
```

profile of v0, /device:TPU:0, one launch (start us, length us, event | category | flops | bytes accessed | tf_op | source)
XLA Modules:
  0.0 1170.5 jit_solution(6155522578404734806)
XLA Ops:
  16.3 21.4 %all-gather.8.cloned.1.call-done = bf16[512,2048]{1,0:T(8,128)(2,1)} async-done(((bf16[128,2048]{1,0:T(8,128)(2,1)}), bf16[512,2048]{1,0:T(8,128)(2,1)}) %all-gather.8.cloned.1.call-update) | async-done | bytes 2097168 | tf_op jit(solution)/shard_map/all_gather | solution.py:168
  41.5 56.1 %all-gather.6.cloned.1.call-done = bf16[4096,256]{1,0:T(8,128)(2,1)} async-done(((bf16[128,256]{1,0:T(8,128)(2,1)}), bf16[4096,256]{1,0:T(8,128)(2,1)}) %all-gather.6.cloned.1.call-update) | async-done | bytes 2097168 | tf_op jit(solution)/shard_map/all_gather | solution.py:239
  97.6 13.4 %while.61 = (s32[]{:T(128)}, f32[512,4]{0,1:T(4,128)S(1)}, f32[512,4]{0,1:T(4,128)S(1)}, s32[]{:T(128)}, s32[4096]{0:T(1024)S(1)}, /*index=5*/s32[1]{0:T(128)}, ...) while((s32[]{:T(128)}, f32[512,4]{0,1:T(4,128)S(1)}, ...), condition=%wide.region_9.10_spmd, body=%wide.region_4.9_spmd.sunk | while | flops 555226624 | bytes 19274140 | solution.py:83
  99.5 5.6 conditional.6
  112.0 15.4 %while.62 = (s32[]{:T(128)}, f32[512,4,128]{2,0,1:T(8,128)}, s32[]{:T(128)}, s32[4096]{0:T(1024)S(1)}, s32[1]{0:T(128)}, /*index=5*/s32[]{:T(128)}, bf16[4096,25...) while((s32[]{:T(128)}, f32[512,4,128]{2,0,1:T(8,128)}, ...), condition=%wide.region_13.14_spmd, body=%wide.region_10.13_spmd.sunk | while | flops 1086064128 | bytes 4235141 | solution.py:108
  113.9 7.7 conditional.7
  115.5 6.0 fusion.12
  134.9 69.9 %reduce-scatter.13.cloned.1.call-done = bf16[128,2048]{1,0:T(8,128)(2,1)} async-done(((bf16[512,2048]{1,0:T(8,128)(2,1)}), bf16[128,2048]{1,0:T(8,128)(2,1)}) %reduce-scatter.13.cloned.1.call-update) | async-done | bytes 524304 | tf_op jit(solution)/shard_map/reduce_scatter | solution.py:172
  210.4 22.1 %all-gather.10.cloned.1.call-done = bf16[512,2048]{1,0:T(8,128)(2,1)} async-done(((bf16[128,2048]{1,0:T(8,128)(2,1)}), bf16[512,2048]{1,0:T(8,128)(2,1)}) %all-gather.10.cloned.1.call-update) | async-done | bytes 2097168 | tf_op jit(solution)/shard_map/all_gather | solution.py:168
  232.5 10.5 fusion.74
  243.0 13.6 %all-gather.12.cloned.1.call-done = bf16[512,2048]{1,0:T(8,128)(2,1)} async-done(((bf16[128,2048]{1,0:T(8,128)(2,1)}), bf16[512,2048]{1,0:T(8,128)(2,1)}) %all-gather.12.cloned.1.call-update) | async-done | bytes 2097168 | tf_op jit(solution)/shard_map/all_gather | solution.py:178
  256.6 12.7 %fusion.71 = (f32[2048]{0:T(1024)}, bf16[512,2048]{1,0:T(8,128)(2,1)S(1)}) fusion(f32[512,2048]{1,0:T(8,128)} %fusion.74, f32[2048]{0:T(1024)S(1)} %copy-done.20, bf16[512,2048]{1,0:T(8,128)(2,1)} %all-gather.12.cloned.1.call-done, bf16[2048,2048]{1,0:T(8,128)(2,1)} %param.43), kind=kOutput, calls=%fused_computation.128 | convolution fusion | flops 4318033920 | bytes 16793600 | tf_op jit(solution)/shard_map/rd,fd->rf/dot_general | solution.py:258
  270.6 9.3 convolution_convert_fusion.5
  280.0 12.3 %reduce-scatter.15.cloned.1.call-start = ((), (), s32[]{:S(2)}) async-start(), calls=%async_computation.14 | async-start | bytes 2621440 | tf_op jit(solution)/shard_map/reduce_scatter | solution.py:172
  292.3 11.0 convolution_convert_fusion.6
  303.4 8.2 reduce-scatter.17.cloned.1.call-done
  315.1 31.0 %reduce-scatter.15.cloned.1.call-done = bf16[128,2048]{1,0:T(8,128)(2,1)} async-done(((bf16[512,2048]{1,0:T(8,128)(2,1)}), bf16[128,2048]{1,0:T(8,128)(2,1)}) %reduce-scatter.15.cloned.1.call-update) | async-done | bytes 524304 | tf_op jit(solution)/shard_map/reduce_scatter | solution.py:172
  351.2 22.7 %all-gather.14.cloned.1.call-done = bf16[512,2048]{1,0:T(8,128)(2,1)} async-done(((bf16[128,2048]{1,0:T(8,128)(2,1)}), bf16[512,2048]{1,0:T(8,128)(2,1)}) %all-gather.14.cloned.1.call-update) | async-done | bytes 2097168 | tf_op jit(solution)/shard_map/all_gather | solution.py:178
  379.5 22.9 %while.63 = (s32[]{:T(128)}, f32[512,4,128]{2,0,1:T(8,128)S(1)}, bf16[4096,256]{0,1:T(8,128)(2,1)}, s32[]{:T(128)}, s32[4096]{0:T(1024)S(1)}, /*index=5*/s32[1]{...) while((s32[]{:T(128)}, f32[512,4,128]{2,0,1:T(8,128)S(1)}, ...), condition=%wide.region_25.26_spmd, body=%wide.region_22.25_spmd.sunk | while | flops 2714502656 | bytes 48028164 | solution.py:164
  381.4 15.2 %conditional.8 = ((f32[512,4,128]{2,0,1:T(8,128)S(1)}, bf16[4096,256]{0,1:T(8,128)(2,1)})) conditional(s32[]{:T(128)} %convert_element_type.318, (f32[512,4,128]{2,0,1:T(8,128)S(1)}, bf16[4096,256]{0,1:T(8,128)(2,1)}) %tuple.194, (s32[]{:T(128)}, s32[]{:T(128)}, s32[4096]{0:T(1024)S(1)}, bf16[4096,256]{1,0:T(8,128)(2,1)}, ...), branch_computations={%region_23.23_spmd, %region_24.24_spmd} | conditional | flops 2714502656 | bytes 48027816 | solution.py:158
  411.5 104.9 %reduce-scatter.21.cloned.1.call-done = bf16[512,256]{0,1:T(8,128)(2,1)} async-done(((bf16[4096,256]{0,1:T(8,128)(2,1)}), bf16[512,256]{0,1:T(8,128)(2,1)}) %reduce-scatter.21.cloned.1.call-update) | async-done | bytes 262160 | tf_op jit(solution)/shard_map/reduce_scatter | solution.py:290
  522.7 11.5 convolution_convert_fusion
  534.2 10.0 convolution_convert_fusion.1
  544.9 35.6 %all-reduce.2 = (f32[512]{0:T(512)}, f32[2048]{0:T(1024)}) all-reduce(f32[512]{0:T(512)S(1)} %bitcast.123, f32[2048]{0:T(1024)S(1)} %copy-done.15), channel_id=1, replica_groups=mesh['seq'=8,'tp'=4] {'seq'}, use_global_device_ids=true, to_apply=%region_37.38 | all-reduce | flops 2560 | bytes 20480 | tf_op jit(solution)/shard_map/psum | solution.py:322
  580.6 7.0 reduce-scatter.23.cloned.1.call-done
  589.4 69.8 %reduce-scatter.25.cloned.1.call-done = bf16[512,256]{1,0:T(8,128)(2,1)} async-done(((bf16[512,2048]{1,0:T(8,128)(2,1)}), bf16[512,256]{1,0:T(8,128)(2,1)}) %reduce-scatter.25.cloned.1.call-update) | async-done | bytes 262160 | tf_op jit(solution)/shard_map/reduce_scatter | solution.py:199
  661.0 19.9 %reduce-scatter.31.cloned.1.call-done = bf16[128,256]{1,0:T(8,128)(2,1)} async-done(((bf16[512,256]{1,0:T(8,128)(2,1)}), bf16[128,256]{1,0:T(8,128)(2,1)}) %reduce-scatter.31.cloned.1.call-update) | async-done | bytes 65552
  681.7 33.7 %reduce-scatter.19.cloned.1.call-done = bf16[128,2048]{1,0:T(8,128)(2,1)} async-done(((bf16[512,2048]{1,0:T(8,128)(2,1)}), bf16[128,2048]{1,0:T(8,128)(2,1)}) %reduce-scatter.19.cloned.1.call-update) | async-done | bytes 524304 | tf_op jit(solution)/shard_map/reduce_scatter | solution.py:182
  720.7 44.3 %all-reduce.1 = (f32[2048]{0:T(1024)}, f32[2048]{0:T(1024)}, f32[128]{0:T(128)}, f32[2048]{0:T(1024)}, f32[2048]{0:T(1024)}, /*index=5*/f32[2048]{0:T(1024)}, f32[2048]{0:T(1024)}) all-reduce(f32[2048]{0:T(1024)S(1)} %get-tuple-element.1195, f32[2048]{0:T(1024)S(1)} %get-tuple-element.1197, ...), channel_id=1, replica_groups=mesh['seq'=8,'tp'=4] {'seq','tp'}, use_global_device_ids=true, to_apply=%region_32.33 | all-reduce | flops 12416 | bytes 99328 | tf_op jit(solution)/shard_map/psum | solution.py:309
  766.4 103.2 %reduce-scatter.29.cloned.1.call-done = bf16[2048,256]{1,0:T(8,128)(2,1)} async-done(((bf16[2048,2048]{1,0:T(8,128)(2,1)}), bf16[2048,256]{1,0:T(8,128)(2,1)}) %reduce-scatter.29.cloned.1.call-update) | async-done | bytes 1048592 | tf_op jit(solution)/shard_map/reduce_scatter | solution.py:199
  872.4 148.6 %reduce-scatter.27.cloned.1.call-done = bf16[256,2048]{1,0:T(8,128)(2,1)} async-done(((bf16[2048,2048]{1,0:T(8,128)(2,1)}), bf16[256,2048]{1,0:T(8,128)(2,1)}) %reduce-scatter.27.cloned.1.call-update) | async-done | bytes 1048592 | tf_op jit(solution)/shard_map/reduce_scatter | solution.py:188
  1023.9 136.7 %all-reduce.5.cloned.1.call-done = f32[2048,256]{1,0:T(8,128)} async-done(((f32[2048,256]{1,0:T(8,128)}), f32[2048,256]{1,0:T(8,128)}) %all-reduce.5.cloned.1.call-update) | async-done | bytes 2097168 | tf_op jit(solution)/shard_map/psum | solution.py:309
  (181 shorter events, 107.6 us)
Async XLA Ops:
  7.2 124.8 %copy-start = (bf16[512,2048]{1,0:T(8,128)(2,1)S(1)}, bf16[512,2048]{1,0:T(8,128)(2,1)}, u32[]{:S(2)}) copy-start(bf16[512,2048]{1,0:T(8,128)(2,1)} %param.37) | copy-start | bytes 6291460
  7.2 8.2 copy-start.22
  7.2 30.5 %copy-start.21 = (f32[512]{0:T(512)S(1)}, f32[512]{0:T(512)}, u32[]{:S(2)}) copy-start(f32[512]{0:T(512)} %param.34) | copy-start | bytes 6148
  7.2 30.5 %all-gather.8.cloned.1.call-start = ((), (), s32[]{:S(2)}) async-start(), calls=%async_computation.11 | async-start | bytes 2621440 | tf_op jit(solution)/shard_map/all_gather | solution.py:168
  12.3 85.3 %all-gather.6.cloned.1.call-start = ((), (), s32[]{:S(2)}) async-start(), calls=%async_computation.10 | async-start | bytes 2162688 | tf_op jit(solution)/shard_map/all_gather | solution.py:239
  15.3 189.5 %reduce-scatter.13.cloned.1.call-start = ((), (), s32[]{:S(2)}) async-start(), calls=%async_computation.12 | async-start | bytes 2621440 | tf_op jit(solution)/shard_map/reduce_scatter | solution.py:172
  131.2 73.7 %copy-start.2 = (bf16[128,2048]{1,0:T(8,128)(2,1)S(1)}, bf16[128,2048]{1,0:T(8,128)(2,1)}, u32[]{:S(2)}) copy-start(bf16[128,2048]{1,0:T(8,128)(2,1)} %param.29) | copy-start | bytes 1572868
  131.2 73.6 %copy-start.8 = (f32[2048]{0:T(1024)S(1)}, f32[2048]{0:T(1024)}, u32[]{:S(2)}) copy-start(f32[2048]{0:T(1024)} %param.38) | copy-start | bytes 24580
  132.0 75.6 %copy-start.9 = (f32[2048]{0:T(1024)S(1)}, f32[2048]{0:T(1024)}, u32[]{:S(2)}) copy-start(f32[2048]{0:T(1024)} %param.39) | copy-start | bytes 24580
  132.0 75.6 %copy-start.13 = (f32[2048]{0:T(1024)S(1)}, f32[2048]{0:T(1024)}, u32[]{:S(2)}) copy-start(f32[2048]{0:T(1024)} %param.40) | copy-start | bytes 24580
  134.6 97.9 %all-gather.10.cloned.1.call-start = ((), (), s32[]{:S(2)}) async-start(), calls=%async_computation.13 | async-start | bytes 2621440 | tf_op jit(solution)/shard_map/all_gather | solution.py:168
  209.8 46.8 %all-gather.12.cloned.1.call-start = ((), (), s32[]{:S(2)}) async-start(), calls=%async_computation.15 | async-start | bytes 2621440 | tf_op jit(solution)/shard_map/all_gather | solution.py:178
  210.4 46.3 %copy-start.20 = (f32[2048]{0:T(1024)S(1)}, f32[2048]{0:T(1024)}, u32[]{:S(2)}) copy-start(f32[2048]{0:T(1024)} %param.42) | copy-start | bytes 24580
  210.4 101.2 %reduce-scatter.17.cloned.1.call-start = ((), (), s32[]{:S(2)}) async-start(), calls=%async_computation.16 | async-start | bytes 2621440 | tf_op jit(solution)/shard_map/reduce_scatter | solution.py:182
  280.0 66.2 %reduce-scatter.15.cloned.1.call-start = ((), (), s32[]{:S(2)}) async-start(), calls=%async_computation.14 | async-start | bytes 2621440 | tf_op jit(solution)/shard_map/reduce_scatter | solution.py:172
  303.3 42.9 %copy-start.14 = (f32[2048]{0:T(1024)S(1)}, f32[2048]{0:T(1024)}, u32[]{:S(2)}) copy-start(f32[2048]{0:T(1024)} %param.44) | copy-start | bytes 24580
  303.3 70.6 %all-gather.14.cloned.1.call-start = ((), (), s32[]{:S(2)}) async-start(), calls=%async_computation.17 | async-start | bytes 2621440 | tf_op jit(solution)/shard_map/all_gather | solution.py:178
  351.2 165.3 %reduce-scatter.21.cloned.1.call-start = ((), (), s32[]{:S(2)}) async-start(), calls=%async_computation.19 | async-start | bytes 2359296 | tf_op jit(solution)/shard_map/reduce_scatter | solution.py:290
  402.5 185.2 %reduce-scatter.23.cloned.1.call-start = ((), (), s32[]{:S(2)}) async-start(), calls=%async_computation.20 | async-start | bytes 2359296 | tf_op jit(solution)/shard_map/reduce_scatter | solution.py:188
  407.0 252.1 %reduce-scatter.25.cloned.1.call-start = ((), (), s32[]{:S(2)}) async-start(), calls=%async_computation.22 | async-start | bytes 2359296 | tf_op jit(solution)/shard_map/reduce_scatter | solution.py:199
  411.3 269.5 %reduce-scatter.31.cloned.1.call-start = ((), (), s32[]{:S(2)}) async-start(), calls=%async_computation.25 | async-start | bytes 327680
  518.3 197.1 %reduce-scatter.19.cloned.1.call-start = ((), (), s32[]{:S(2)}) async-start(), calls=%async_computation.18 | async-start | bytes 2621440 | tf_op jit(solution)/shard_map/reduce_scatter | solution.py:182
  522.6 347.0 %reduce-scatter.29.cloned.1.call-start = ((), (), s32[]{:S(2)}) async-start(), calls=%async_computation.24 | async-start | bytes 9437184 | tf_op jit(solution)/shard_map/reduce_scatter | solution.py:199
  534.2 486.9 %reduce-scatter.27.cloned.1.call-start = ((), (), s32[]{:S(2)}) async-start(), calls=%async_computation.23 | async-start | bytes 9437184 | tf_op jit(solution)/shard_map/reduce_scatter | solution.py:188
  544.2 171.1 %copy-start.10 = (f32[2048]{0:T(1024)S(1)}, f32[2048]{0:T(1024)}, u32[]{:S(2)}) copy-start(f32[2048]{0:T(1024)} %param.31) | copy-start | bytes 24580
  544.2 171.1 %copy-start.12 = (f32[128]{0:T(128)S(1)}, f32[128]{0:T(128)}, u32[]{:S(2)}) copy-start(f32[128]{0:T(128)} %copy-done.11) | copy-start | bytes 1540
  544.3 173.1 %copy-start.19 = (f32[128]{0:T(128)S(1)}, f32[128]{0:T(128)}, u32[]{:S(2)}) copy-start(f32[128]{0:T(128)} %copy-done.18) | copy-start | bytes 1540
  544.3 173.1 %copy-start.5 = (bf16[128,2048]{1,0:T(8,128)(2,1)S(1)}, bf16[128,2048]{1,0:T(8,128)(2,1)}, u32[]{:S(2)}) copy-start(bf16[128,2048]{1,0:T(8,128)(2,1)} %fusion.55) | copy-start | bytes 1572868
  544.3 616.2 %all-reduce.5.cloned.1.call-start = ((), (), s32[]{:S(2)}) async-start(), calls=%async_computation.21 | async-start | bytes 4194304 | tf_op jit(solution)/shard_map/psum | solution.py:309
  661.0 59.2 %copy-start.17 = (f32[128]{0:T(128)S(1)}, f32[128]{0:T(128)}, u32[]{:S(2)}) copy-start(f32[128]{0:T(128)} %copy-done.16) | copy-start | bytes 1540
  681.7 83.3 %copy-start.4 = (f32[128,2048]{1,0:T(8,128)S(1)}, f32[128,2048]{1,0:T(8,128)}, u32[]{:S(2)}) copy-start(f32[128,2048]{1,0:T(8,128)} %copy-done.3) | copy-start | bytes 3145732
  869.6 294.0 %copy-start.1 = (bf16[512,2048]{1,0:T(8,128)(2,1)S(1)}, bf16[512,2048]{1,0:T(8,128)(2,1)}, u32[]{:S(2)}) copy-start(bf16[512,2048]{1,0:T(8,128)(2,1)} %param.37) | copy-start | bytes 6291460
  (9 other events, 26.8 us)
Sparse Core Ops, SparseCore 0:
  12.4 25.2 all-gather.7
  41.1 56.3 all-gather.5
  134.7 70.0 reduce-scatter.12
  209.9 22.5 all-gather.9
  234.0 22.5 all-gather.11
  280.1 31.4 reduce-scatter.16
  314.7 31.4 reduce-scatter.14
  351.3 22.5 all-gather.13
  402.6 113.8 reduce-scatter.20
  520.9 66.7 reduce-scatter.22
  592.1 66.9 reduce-scatter.24
  661.6 19.1 reduce-scatter.30
  683.9 31.4 reduce-scatter.18
  719.3 150.2 reduce-scatter.28
  873.1 147.9 reduce-scatter.26
  1027.7 132.7 all-reduce.4
where the time goes:
time: 1180 us; the launch traced here: 1170 us
  waiting for transfers between devices  870 us (74%)
  matrix products  117 us (10%)
  blocking collectives  80 us (7%)
  other arithmetic  36.5 us (3%)
  local copies, waits for them, and re-layouts  23.6 us (2%)
  loops' own time  16.2 us (1%)
  between operations  14.7 us (1%)
  starting transfers between devices  13.4 us (1%)
    reduce_scatter x2, waiting for transfers between devices, column_weight_grads(): lax.psum_scatter(partial_value.astype(jnp.bfloat16), 'seq', scatter_dimen...  173 us
    reduce_scatter x2, waiting for transfers between devices, row_weight_grads(): lax.psum_scatter(jnp.einsum('rk,rf->kf', gathered, column_grads, preferre...  156 us
    psum x1, waiting for transfers between devices, body(): lax.psum((grad_kv_part, grad_gain_one, grad_bias_one, grad_bias_out, grad...  137 us
    reduce_scatter x1, waiting for transfers between devices, body(): lax.psum_scatter(pair_partial.astype(jnp.bfloat16), 'seq', scatter_dimens...  105 us
    reduce_scatter x2, waiting for transfers between devices, merge_rows(): lax.psum_scatter(partial_value.astype(jnp.bfloat16), 'tp', scatter_dimens...  101 us
    all_gather x1, waiting for transfers between devices, body(): lax.all_gather(key_values(normed_one, w_kv, b_value), ('seq', 'tp'), axis...  56.1 us
    psum x1, blocking collectives, body(): lax.psum((grad_kv_part, grad_gain_one, grad_bias_one, grad_bias_out, grad...  44.3 us
    all_gather x2, waiting for transfers between devices, spread_rows(): return lax.all_gather(normed, 'tp', axis=0, tiled=True)  43.5 us
  transfers between devices with their start and end apart: 16, of which 16 were waited for; matrix products, arithmetic and copies ran while one was open for 7% of the time, Pallas kernels for 0%

commit v1 on v0

v1 whole, which is shorter than its diff:
```python
import functools
import math

import jax
import jax.numpy as jnp
from jax import lax
from jax.experimental import pallas as pl
from jax.experimental.pallas import tpu as pltpu
from jax.sharding import PartitionSpec as P

EPS = 1e-05
NEG = -1e30
LOG2E = math.log2(math.e)
VMEM_LIMIT = 60 * 1024 * 1024
LIGHT = pl.CostEstimate(flops=1024, bytes_accessed=1024, transcendentals=0)
NT = (((1,), (1,)), ((), ()))


def dot(left, right):
    return jnp.dot(left, right, preferred_element_type=jnp.float32)


def dot_nt(left, right):
    return lax.dot_general(left, right, NT, preferred_element_type=jnp.float32)


def tie(value, *deps):
    return lax.optimization_barrier((value, *deps))[0]


def struct(shape, dtype):
    return jax.ShapeDtypeStruct(shape, dtype)


def swap(value, axis, bit):
    count = lax.axis_size(axis)
    return lax.ppermute(value, axis, [(j, j ^ bit) for j in range(count)])


def gather_rows(own):
    beside = swap(own, "tp", 1)
    across = swap(own, "tp", 2)
    return own, beside, across, swap(across, "tp", 1)


def gather_other(own, first, second):
    across = swap(tie(own, first), "tp", 2)
    return own, swap(tie(own, first), "tp", 1), across, swap(tie(across, second), "tp", 1)


def call(kernel, outs, *args):
    return pl.pallas_call(
        kernel,
        out_shape=outs,
        compiler_params=pltpu.CompilerParams(vmem_limit_bytes=VMEM_LIMIT),
        cost_estimate=LIGHT,
    )(*args)


def total(*refs):
    return sum(ref[...].astype(jnp.float32) for ref in refs)


def add_kernel(*refs):
    refs[-1][...] = total(*refs[:-1]).astype(jnp.bfloat16)


def add_low(*values):
    return call(add_kernel, struct(values[0].shape, jnp.bfloat16), *values)


def split_kernel(meta, keep_in, got_in, send_ref, keep_ref):
    both = total(keep_in, got_in).astype(jnp.bfloat16)

    @pl.when(pl.program_id(1) == 0)
    def _():
        send_ref[...] = both

    @pl.when(pl.program_id(1) == 1)
    def _():
        keep_ref[...] = both


def halves_kernel(side, keep, got, mine, theirs):
    half = mine.shape[1]
    both = total(keep, got).astype(jnp.bfloat16)
    low, high = both[:, :half], both[:, half:]
    mine[...] = jnp.where(side[0] == 0, low, high)
    theirs[...] = jnp.where(side[0] == 0, high, low)


def split_add(side, keep, got):
    parts, rows, columns = keep.shape
    block = pl.BlockSpec((1, rows, columns), lambda m, s, meta: (2 * m + (meta[0] + 1 - s) % 2, 0, 0))
    half = struct((parts // 2, rows, columns), jnp.bfloat16)
    return pl.pallas_call(
        split_kernel,
        grid_spec=pltpu.PrefetchScalarGridSpec(
            num_scalar_prefetch=1,
            grid=(parts // 2, 2),
            in_specs=[block, block],
            out_specs=[pl.BlockSpec((1, rows, columns), lambda m, s, meta: (m, 0, 0))] * 2,
        ),
        out_shape=[half, half],
        compiler_params=pltpu.CompilerParams(vmem_limit_bytes=VMEM_LIMIT),
        cost_estimate=LIGHT,
    )(jnp.stack([side]).astype(jnp.int32), keep, got)


def line_bits():
    bit = 2
    while bit < lax.axis_size("seq"):
        yield bit
        bit *= 2


def column_halves(value):
    side = lax.axis_index("seq") % 2
    half = value.shape[1] // 2
    keep = lax.dynamic_slice_in_dim(value, side * half, half, 1)
    send = lax.dynamic_slice_in_dim(value, (1 - side) * half, half, 1)
    return keep, send


def sum_over(value, axis):
    bit = 1
    while bit < lax.axis_size(axis):
        value = value + swap(value, axis, bit)
        bit *= 2
    return value


def normalized(features):
    centered = features - jnp.mean(features, axis=-1, keepdims=True)
    variance = jnp.mean(centered * centered, axis=-1, keepdims=True)
    scale = lax.rsqrt(variance + EPS)
    return centered * scale, scale


def norm_back(features, gain, grads):
    normed, scale = normalized(features)
    scaled = grads * gain
    mean = jnp.mean(scaled, axis=-1, keepdims=True)
    along = jnp.mean(scaled * normed, axis=-1, keepdims=True)
    over_rows = lambda value: jnp.sum(value, axis=0, keepdims=True)
    return scale * (scaled - mean - normed * along), over_rows(grads * normed), over_rows(grads)


def first_kernel(in_ref, gain, shift, w_ref, bias, norm_ref, key_ref, value_ref):
    normed, _ = normalized(in_ref[...].astype(jnp.float32))
    low = (normed * gain[...] + shift[...]).astype(jnp.bfloat16)
    norm_ref[...] = low
    pairs = dot(low, w_ref[...])
    hd = key_ref.shape[1]
    key_ref[...] = pairs[:, :hd].astype(jnp.bfloat16)
    value_ref[...] = (pairs[:, hd:] + bias[...]).astype(jnp.bfloat16)


def query_kernel(r0, r1, r2, r3, w_ref, bias, out_ref):
    rows = jnp.concatenate([r0[...], r1[...], r2[...], r3[...]], axis=0)
    out_ref[...] = (dot(rows, w_ref[...]) + bias[...]).astype(jnp.bfloat16)


def project_kernel(first, form, value_ref, w_ref, out0, out1):
    size = out0.shape[0]
    result = form(value_ref[first * size : (first + 2) * size, :], w_ref[...]).astype(jnp.bfloat16)
    out0[...] = result[:size]
    out1[...] = result[size:]


def middle_kernel(in_ref, p0, p1, p2, bias, gain, shift, middle_ref, norm_ref):
    middle = total(in_ref, p0, p1, p2) + bias[...]
    middle_ref[...] = middle
    normed, _ = normalized(middle)
    norm_ref[...] = (normed * gain[...] + shift[...]).astype(jnp.bfloat16)


def middle_back_kernel(middle_ref, p0, p1, p2, up_ref, gain, grads_ref, low_ref, sums_ref):
    upstream = up_ref[...].astype(jnp.float32)
    back, for_gain, for_shift = norm_back(middle_ref[...], gain[...], total(p0, p1, p2))
    grads = upstream + back
    grads_ref[...] = grads
    low_ref[...] = grads.astype(jnp.bfloat16)
    sums_ref[0:1] = jnp.sum(upstream, axis=0, keepdims=True)
    sums_ref[1:2] = for_gain
    sums_ref[2:3] = for_shift
    sums_ref[3:4] = jnp.sum(grads, axis=0, keepdims=True)


def attended_grads_kernel(r0, r1, r2, r3, w_ref, out_ref):
    rows = jnp.concatenate([r0[...], r1[...], r2[...], r3[...]], axis=0)
    out_ref[...] = dot_nt(rows, w_ref[...]).astype(jnp.bfloat16)


def layer_kernel(middle_ref, p0, p1, p2, bias, out_ref):
    out_ref[...] = (total(middle_ref, p0, p1, p2) + bias[...]).astype(jnp.bfloat16)


def last_kernel(in_ref, p0, p1, p2, pairs_ref, w_ref, middle_ref, gain, grads_ref, sums_ref, value_ref):
    hd = value_ref.shape[1]
    grads = total(p0, p1, p2) + dot_nt(pairs_ref[...], w_ref[...])
    back, for_gain, for_shift = norm_back(in_ref[...].astype(jnp.float32), gain[...], grads)
    grads_ref[...] = middle_ref[...] + back
    sums_ref[0:1] = for_gain
    sums_ref[1:2] = for_shift
    value_ref[...] = jnp.sum(pairs_ref[:, hd:].astype(jnp.float32), axis=0, keepdims=True)


def turned(own_ref, other_ref, scratch):
    half = own_ref.shape[0]
    scratch[:, :half] = own_ref[...].T
    scratch[:, half:] = other_ref[...].T


def weight_kernel(meta, *refs):
    lefts, own_ref, other_ref = refs[:8], refs[8], refs[9]
    send_ref, keep_ref, scratch = refs[10:]

    @pl.when((pl.program_id(0) == 0) & (pl.program_id(1) == 0))
    def _():
        turned(own_ref, other_ref, scratch)

    rows = jnp.concatenate([ref[...] for ref in lefts], axis=0)
    part = dot(scratch[...], rows).astype(jnp.bfloat16)

    @pl.when(pl.program_id(1) == 0)
    def _():
        send_ref[0] = part

    @pl.when(pl.program_id(1) == 1)
    def _():
        keep_ref[0] = part


def weight_grads(blocks, lowest, own, piece, other):
    count, columns = other.shape
    size, dim = blocks[0].shape
    parts = lax.axis_size("seq") // 2
    tile = dim // parts
    block = pl.BlockSpec((size, tile), lambda m, s, meta: (0, 2 * m + (meta[0] + 1 - s) % 2))
    half = struct((parts // 2, columns, tile), jnp.bfloat16)
    return pl.pallas_call(
        weight_kernel,
        grid_spec=pltpu.PrefetchScalarGridSpec(
            num_scalar_prefetch=1,
            grid=(parts // 2, 2),
            in_specs=[block] * 8
            + [
                pl.BlockSpec((count, columns), lambda m, s, meta: (0, piece)),
                pl.BlockSpec((count, columns), lambda m, s, meta: (0, 0)),
            ],
            out_specs=[pl.BlockSpec((1, columns, tile), lambda m, s, meta: (m, 0, 0))] * 2,
            scratch_shapes=[pltpu.VMEM((columns, 2 * count), jnp.bfloat16)],
        ),
        out_shape=[half, half],
        compiler_params=pltpu.CompilerParams(vmem_limit_bytes=VMEM_LIMIT),
        cost_estimate=LIGHT,
    )(lowest, *blocks, own, other)


def slab_kernel(meta, *refs):
    lefts, own_ref, other_ref, out_ref, scratch = refs[:8], *refs[8:]
    turned(own_ref, other_ref, scratch)
    rows = jnp.concatenate([ref[...] for ref in lefts], axis=0)
    out_ref[...] = dot(scratch[...], rows).astype(jnp.bfloat16)


def slab_grads(blocks, slab, own, other, parts):
    count, columns = own.shape
    size, dim = blocks[0].shape
    tile = dim // parts
    block = pl.BlockSpec((size, tile), lambda m, meta: (0, meta[0]))
    fixed = pl.BlockSpec((count, columns), lambda m, meta: (0, 0))
    return pl.pallas_call(
        slab_kernel,
        grid_spec=pltpu.PrefetchScalarGridSpec(
            num_scalar_prefetch=1,
            grid=(1,),
            in_specs=[block] * 8 + [fixed, fixed],
            out_specs=pl.BlockSpec((columns, tile), lambda m, meta: (0, 0)),
            scratch_shapes=[pltpu.VMEM((columns, 2 * count), jnp.bfloat16)],
        ),
        out_shape=struct((columns, tile), jnp.bfloat16),
        compiler_params=pltpu.CompilerParams(vmem_limit_bytes=VMEM_LIMIT),
        cost_estimate=LIGHT,
    )(slab, *blocks, own, other)


ANYWHERE = pl.BlockSpec(memory_space=pl.ANY)


def mlp_kernel(tiles, aliased, meta, x0, x1, g0, g1, fc_ref, proj_ref, bias_ref, *refs):
    (a0, a1, ak, l0, l1, lk, m0, m1, t0, t1, sum_ref, x_ref, g_ref, macc, tacc) = refs[aliased:]
    step = pl.program_id(0)
    size = x0.shape[0]

    @pl.when(step == 0)
    def _():
        x_ref[:size] = x0[...]
        x_ref[size:] = x1[...]
        g_ref[:size] = g0[...]
        g_ref[size:] = g1[...]

    values = dot(x_ref[...], fc_ref[...]) + bias_ref[...]
    grads = dot_nt(g_ref[...], proj_ref[...])
    root = math.sqrt(2 / math.pi)
    square = values * values
    bend = jnp.tanh(root * values * (1 + 0.044715 * square))
    half = 0.5 * (1 + bend)
    slope = half + 0.5 * root * values * (1 - bend * bend) * (1 + 3 * 0.044715 * square)
    activated = (values * half).astype(jnp.bfloat16)
    grads = grads * slope
    sum_ref[...] = jnp.sum(grads, axis=0, keepdims=True)
    low = grads.astype(jnp.bfloat16)

    @pl.when(step == 0)
    def _():
        macc[...] = jnp.zeros_like(macc)
        tacc[...] = jnp.zeros_like(tacc)

    chunk = macc.shape[1] // 4
    for c in range(4):
        cut = slice(c * chunk, (c + 1) * chunk)
        macc[:, cut] += dot(activated, proj_ref[:, cut])
        tacc[:, cut] += dot_nt(low, fc_ref[cut, :])

    @pl.when(step < tiles // 4)
    def _():
        a0[...] = activated
        l0[...] = low

    @pl.when((step >= tiles // 4) & (step < tiles // 2))
    def _():
        a1[...] = activated
        l1[...] = low

    @pl.when(step >= tiles // 2)
    def _():
        ak[...] = activated
        lk[...] = low

    @pl.when(step == tiles - 1)
    def _():
        f = macc[...].astype(jnp.bfloat16)
        b = tacc[...].astype(jnp.bfloat16)
        m0[...] = f[:size]
        m1[...] = f[size:]
        t0[...] = b[:size]
        t1[...] = b[size:]


def mlp(blocks, ups, side, first, w_fc, w_proj, b_fc, before=()):
    size, dim = blocks[0].shape
    hidden = w_fc.shape[1]
    tiles = 4
    width = hidden // tiles
    tile = lambda n, meta: ((n // (tiles // 2)) ^ (1 - meta[0])) * (tiles // 2) + n % (tiles // 2)
    within = lambda n, start, count: jnp.clip(n - start, 0, count - 1)
    fixed = pl.BlockSpec((size, dim), lambda n, meta: (0, 0))
    columns = lambda start, count: pl.BlockSpec(
        (2 * size, width), lambda n, meta: (first // 2, within(n, start, count))
    )
    spread = [columns(0, tiles // 4), columns(tiles // 4, tiles // 4), columns(tiles // 2, tiles // 2)] * 2
    shapes = [struct((4 * size, hidden // 4), jnp.bfloat16)] * 2 + [struct((4 * size, hidden // 2), jnp.bfloat16)]
    rows = struct((size, dim), jnp.bfloat16)
    return pl.pallas_call(
        functools.partial(mlp_kernel, tiles, len(before)),
        grid_spec=pltpu.PrefetchScalarGridSpec(
            num_scalar_prefetch=1,
            grid=(tiles,),
            in_specs=[fixed] * 4
            + [
                pl.BlockSpec((dim, width), lambda n, meta: (0, tile(n, meta))),
                pl.BlockSpec((width, dim), lambda n, meta: (tile(n, meta), 0)),
                pl.BlockSpec((1, width), lambda n, meta: (0, tile(n, meta))),
            ]
            + [ANYWHERE] * len(before),
            out_specs=spread + [fixed] * 4 + [pl.BlockSpec((1, width), lambda n, meta: (0, tile(n, meta)))],
            scratch_shapes=[pltpu.VMEM((2 * size, dim), jnp.bfloat16)] * 2 + [pltpu.VMEM((2 * size, dim), jnp.float32)] * 2,
        ),
        out_shape=shapes * 2 + [rows] * 4 + [struct((1, hidden), jnp.float32)],
        input_output_aliases={8 + j: j for j in range(len(before))},
        compiler_params=pltpu.CompilerParams(vmem_limit_bytes=VMEM_LIMIT),
        cost_estimate=LIGHT,
    )(side, *blocks, *ups, w_fc, w_proj, b_fc[None, :], *before)


def allowed_pairs(slot, masks_ref, rows_ref, keys_ref):
    place = keys_ref[...] + masks_ref[2, slot]
    return (place <= rows_ref[0:1, :]) & (place >= rows_ref[1:2, :])


def when_live(meta, slot, visit):
    @pl.when((meta[0, slot] == 1) & (meta[1, slot] == 0))
    def _():
        visit(True)

    @pl.when((meta[0, slot] == 1) & (meta[1, slot] == 1))
    def _():
        visit(False)


def forward_kernel(heads, meta, q_ref, *refs):
    key_refs, value_refs = refs[:4], refs[4:8]
    rows_ref, keys_ref, out_ref, norm_ref, m_ref, l_ref, acc_ref = refs[8:]
    hd = q_ref.shape[1] // heads
    scale = hd ** (-0.5) * LOG2E
    slots = key_refs[0].shape[0]

    def visit(slot, masked, exact):
        keys = jnp.concatenate([ref[slot] for ref in key_refs], axis=0)
        values_t = jnp.concatenate([ref[slot] for ref in value_refs], axis=0).T
        if masked:
            allowed = allowed_pairs(slot, meta, rows_ref, keys_ref)
        for h in range(heads):
            scores = dot_nt(keys, q_ref[:, h * hd : (h + 1) * hd]) * scale
            if masked:
                scores = jnp.where(allowed, scores, NEG)
            top = m_ref[h : h + 1, :]
            if exact:
                new = jnp.maximum(top, jnp.max(scores, axis=0, keepdims=True))
                decay = jnp.exp2(top - new)
                m_ref[h : h + 1, :] = new
                l_ref[h : h + 1, :] = l_ref[h : h + 1, :] * decay
                acc_ref[h] = acc_ref[h] * decay
                top = new
            weights = jnp.exp2(scores - top)
            l_ref[h : h + 1, :] += jnp.sum(weights, axis=0, keepdims=True)
            acc_ref[h] += dot(values_t, weights.astype(jnp.bfloat16))

    def run(exact):
        m_ref[...] = jnp.full_like(m_ref, NEG)
        l_ref[...] = jnp.zeros_like(l_ref)
        acc_ref[...] = jnp.zeros_like(acc_ref)
        visit(0, True, True)

        def body(slot, carry):
            when_live(meta, slot, lambda masked: visit(slot, masked, exact))
            return carry

        lax.fori_loop(1, slots, body, 0)

    run(False)

    @pl.when(jnp.logical_not(jnp.max(l_ref[...]) < 2.0**100))
    def _():
        run(True)

    norm_ref[...] = m_ref[...] + jnp.log2(l_ref[...])
    for h in range(heads):
        result = acc_ref[h] / l_ref[h : h + 1, :]
        out_ref[:, h * hd : (h + 1) * hd] = result.T.astype(jnp.bfloat16)


def backward_visit(heads, slot, meta, q_ref, key_refs, value_refs, rows_ref, keys_ref, norm_ref, up_ref, delta_ref, dq_acc, d_refs):
    hd = q_ref.shape[1] // heads
    part = key_refs[0].shape[1]
    scale = hd ** (-0.5)

    def visit(masked):
        keys = jnp.concatenate([ref[0] for ref in key_refs], axis=0)
        values = jnp.concatenate([ref[0] for ref in value_refs], axis=0)
        keys_t = keys.T
        if masked:
            allowed = allowed_pairs(slot, meta, rows_ref, keys_ref)
        dk = dv = None
        for h in range(heads):
            q = q_ref[:, h * hd : (h + 1) * hd]
            up = up_ref[:, h * hd : (h + 1) * hd]
            weights = jnp.exp2(dot_nt(keys, q) * (scale * LOG2E) - norm_ref[h : h + 1, :])
            if masked:
                weights = jnp.where(allowed, weights, 0.0)
            grads = dot_nt(values, up)
            score_grads = (weights * (grads - delta_ref[h : h + 1, :])).astype(jnp.bfloat16)
            dv_h = dot(weights.astype(jnp.bfloat16), up)
            dk_h = dot(score_grads, q)
            dv = dv_h if dv is None else dv + dv_h
            dk = dk_h if dk is None else dk + dk_h
            dq_acc[h] = dq_acc[h] + dot(keys_t, score_grads)
        for index, ref in enumerate(d_refs):
            part_rows = slice(index * part, (index + 1) * part)
            ref[0, :, :hd] = (dk[part_rows] * scale).astype(jnp.bfloat16)
            ref[0, :, hd:] = dv[part_rows].astype(jnp.bfloat16)

    @pl.when(meta[0, slot] == 0)
    def _():
        for ref in d_refs:
            ref[...] = jnp.zeros_like(ref)

    when_live(meta, slot, visit)


def backward_first_kernel(heads, first, meta, q_ref, *refs):
    key_refs, value_refs = refs[:4], refs[4:8]
    rows_ref, keys_ref, norm_ref, up_ref, att_ref, acc_ref, delta_ref = refs[8:15]
    d_refs = refs[15:19]
    hd = q_ref.shape[1] // heads

    @pl.when(pl.program_id(0) == 0)
    def _():
        acc_ref[...] = jnp.zeros_like(acc_ref)
        for h in range(heads):
            cols = slice(h * hd, (h + 1) * hd)
            both = att_ref[:, cols].astype(jnp.float32) * up_ref[:, cols].astype(jnp.float32)
            delta_ref[h : h + 1, :] = jnp.sum(both.T, axis=0, keepdims=True)

    slot = pl.program_id(0) + first
    backward_visit(heads, slot, meta, q_ref, key_refs, value_refs, rows_ref, keys_ref, norm_ref, up_ref, delta_ref, acc_ref, d_refs)


def backward_last_kernel(heads, first, meta, q_ref, *refs):
    key_refs, value_refs = refs[:4], refs[4:8]
    rows_ref, keys_ref, norm_ref, up_ref, start_ref, delta_ref, dq_ref, bias_ref = refs[8:16]
    d_refs = refs[16:20]
    acc_ref = refs[20]
    hd = q_ref.shape[1] // heads

    @pl.when(pl.program_id(0) == 0)
    def _():
        acc_ref[...] = start_ref[...]

    slot = pl.program_id(0) + first
    backward_visit(heads, slot, meta, q_ref, key_refs, value_refs, rows_ref, keys_ref, norm_ref, up_ref, delta_ref, acc_ref, d_refs)

    @pl.when(pl.program_id(0) == pl.num_programs(0) - 1)
    def _():
        for h in range(heads):
            result = (acc_ref[h] * hd ** (-0.5)).T
            bias_ref[:, h * hd : (h + 1) * hd] = jnp.sum(result, axis=0, keepdims=True)
            dq_ref[:, h * hd : (h + 1) * hd] = result.astype(jnp.bfloat16)


def whole(value):
    return pl.BlockSpec(value.shape, lambda step, meta: (0,) * len(value.shape))


def attention_call(kernel, meta, first, steps, slots, queries, keys, values, extra, outs, scratch, passes):
    rows, width = queries.shape
    part, hd = keys[0].shape[1:]
    block = lambda columns, start: pl.BlockSpec((slots // steps, part, columns), lambda step, meta: (step + start, 0, 0))
    heads = width // hd
    return pl.pallas_call(
        kernel,
        grid_spec=pltpu.PrefetchScalarGridSpec(
            num_scalar_prefetch=1,
            grid=(steps,),
            in_specs=[whole(queries)] + [block(hd, first)] * 8 + [whole(value) for value in extra],
            out_specs=[block(2 * hd, 0) if out.shape == (slots, part, 2 * hd) else whole(out) for out in outs],
            scratch_shapes=scratch,
        ),
        out_shape=outs,
        compiler_params=pltpu.CompilerParams(vmem_limit_bytes=VMEM_LIMIT),
        cost_estimate=LIGHT,
    )(meta, queries, *keys, *values, *extra)


def attention_forward(queries, keys, values, meta, rows_info, keys_info, heads):
    rows, width = queries.shape
    return attention_call(
        functools.partial(forward_kernel, heads), meta, 0, 1, keys[0].shape[0], queries, keys, values,
        [rows_info, keys_info],
        [struct((rows, width), jnp.bfloat16), struct((heads, rows), jnp.float32)],
        [
            pltpu.VMEM((heads, rows), jnp.float32),
            pltpu.VMEM((heads, rows), jnp.float32),
            pltpu.VMEM((heads, width // heads, rows), jnp.float32),
        ],
        2,
    )


def backward_calls(queries, keys, values, meta, rows_info, keys_info, norm, attended, upstream, heads):
    rows, width = queries.shape
    hd = width // heads
    n, part = keys[0].shape[:2]
    half = n // 2
    grads = [struct((half, part, 2 * hd), jnp.bfloat16)] * 4
    shared = [rows_info, keys_info, norm, upstream]

    def first(*deps):
        return attention_call(
            functools.partial(backward_first_kernel, heads, half), meta, half, half, half, tie(queries, *deps),
            keys, values, shared + [attended],
            [struct((heads, hd, rows), jnp.float32), struct((heads, rows), jnp.float32)] + grads,
            [], 5,
        )

    def last(start, delta, *deps):
        return attention_call(
            functools.partial(backward_last_kernel, heads, 0), meta, 0, half, half, tie(queries, *deps),
            keys, values, shared + [start, delta],
            [struct((rows, width), jnp.bfloat16), struct((1, width), jnp.float32)] + grads,
            [pltpu.VMEM((heads, hd, rows), jnp.float32)], 5,
        )

    return first, last


def gather_slots(own, bits, axis):
    found = {0: own}
    for bit in bits:
        masks = sorted(found)
        stacked = jnp.stack([found[m] for m in masks])
        got = swap(stacked, axis, bit)
        found.update({m ^ bit: got[j] for j, m in enumerate(masks)})
    return found


def body(
    hidden_in, lengths, ln1_gain, ln1_bias, w_query, b_query, w_kv, b_value, w_out, b_out,
    ln2_gain, ln2_bias, w_fc, b_fc, w_proj, b_proj, grad_out,
):
    seq_count = lax.axis_size("seq")
    tp_count = lax.axis_size("tp")
    seq_index = lax.axis_index("seq")
    tp_index = lax.axis_index("tp")
    own_rows, dim = hidden_in.shape
    group_rows = own_rows * tp_count
    head_dim = b_value.shape[0]
    heads = w_query.shape[1] // head_dim
    joined = lambda *blocks: jnp.concatenate(blocks, axis=0)
    seq_bits = [1 << j for j in range(seq_count.bit_length() - 1)]

    order = jnp.stack([tp_index, tp_index ^ 1, tp_index ^ 2, tp_index ^ 3]).astype(jnp.int32)
    inside = (order[:, None] * own_rows + jnp.arange(own_rows, dtype=jnp.int32)[None, :]).reshape(-1)
    group_first = seq_index * group_rows
    doc_ends = jnp.cumsum(lengths)
    begins = jnp.max(
        jnp.where(doc_ends[None, :] <= (inside + group_first)[:, None], doc_ends[None, :], 0), axis=1
    )
    rows_info = jnp.stack([inside, begins - group_first])
    keys_info = inside[:, None]
    slot_group = seq_index ^ jnp.arange(seq_count, dtype=jnp.int32)
    key_first = slot_group * group_rows
    live = (slot_group <= seq_index) & (key_first + group_rows > jnp.min(begins))
    clear = (slot_group < seq_index) & (key_first >= jnp.max(begins))
    meta = jnp.stack([live, clear, key_first - group_first]).astype(jnp.int32)
    side = seq_index % 2
    scalar = lambda value: jnp.stack([value]).astype(jnp.int32)
    lowest, slab, side_scalar = scalar((seq_index // 2) % 2), scalar(2 * tp_index + side), scalar(side)
    beside = lambda value: swap(value, "seq", 1)

    row = lambda vector: vector[None, :]
    rows_low = struct((own_rows, dim), jnp.bfloat16)
    rows_wide = struct((own_rows, dim), jnp.float32)
    narrow = struct((own_rows, head_dim), jnp.bfloat16)
    normed_one, key_own, value_own = call(
        first_kernel, [rows_low, narrow, narrow], hidden_in, row(ln1_gain), row(ln1_bias), w_kv, row(b_value)
    )
    key_slots = gather_slots(key_own, seq_bits[::-1], "seq")
    key_stack = jnp.stack([key_slots[m] for m in range(seq_count)])
    value_two = jnp.stack([value_own, swap(value_own, "tp", 2)])
    value_slots = gather_slots(value_two, seq_bits[::-1], "seq")
    value_two = jnp.stack([value_slots[m] for m in range(seq_count)], axis=1)
    value_beside = swap(value_two, "tp", 1)
    values = [value_two[0], value_beside[0], value_two[1], value_beside[1]]
    blocks_one = gather_rows(normed_one)
    queries = call(
        query_kernel, struct((group_rows, heads * head_dim), jnp.bfloat16), *blocks_one, w_query, row(b_query)
    )
    key_across = tie(swap(key_stack, "tp", 2), queries)
    keys = [key_stack, swap(key_stack, "tp", 1), key_across, swap(key_across, "tp", 1)]
    up_other, one_other = beside(grad_out), beside(normed_one)
    ups_own = gather_rows(tie(grad_out, queries))
    attended, norm = attention_forward(queries, keys, values, meta, rows_info, keys_info, heads)

    def project(value, weight, form):
        far = call(functools.partial(project_kernel, 2, form), [rows_low] * 2, value, weight)
        near = call(functools.partial(project_kernel, 0, form), [rows_low] * 2, tie(value, far[0]), weight)
        return (*near, *far)

    def scatter(own, beside, across, opposite, *deps):
        over = add_low(tie(across, *deps), swap(opposite, "tp", 1))
        return own, swap(beside, "tp", 1), over, swap(over, "tp", 2)

    att0, att1, _, att2 = scatter(*project(attended, w_out, dot))
    middle, normed_two = call(
        middle_kernel, [rows_wide, rows_low], hidden_in, att0, att1, att2, row(b_out), row(ln2_gain), row(ln2_bias)
    )

    two_beside, two_across = swap(normed_two, "tp", 1), swap(normed_two, "tp", 2)
    two_other = beside(normed_two)
    *kept, mlp0, mlp1, two0, two1, sum_near = mlp(
        (normed_two, two_beside), ups_own[:2], side_scalar, 0, w_fc, w_proj, b_fc
    )
    two_across = tie(two_across, two0)
    two_opposite = swap(two_across, "tp", 1)
    *kept, mlp2, mlp3, two2, two3, sum_far = mlp(
        (two_across, two_opposite), ups_own[2:], side_scalar, 2, w_fc, w_proj, b_fc, kept
    )
    act_send0, act_send1, act_keep, low_send0, low_send1, low_keep = kept

    line = list(line_bits())
    line_side = lambda bit: (seq_index // bit) % 2

    def start_sum(blocks, keep, piece, other):
        send, kept = weight_grads(blocks, lowest, keep, piece, other)
        return kept, swap(send, "seq", line[0]), line[1:]

    def step_sum(state, *deps):
        keep, got, bits = state
        if not bits:
            return state
        keep = tie(keep, *deps)
        send, kept = split_add(line_side(bits[0]), keep, got)
        return kept, swap(send, "seq", bits[0]), bits[1:]

    def finish_sum(state, *deps):
        while state[2]:
            state = step_sum(state)
        keep, got = tie(state[0][0], *deps), state[1][0]
        half = keep.shape[1] // 2
        return pl.pallas_call(
            halves_kernel,
            in_specs=[pl.BlockSpec(memory_space=pltpu.SMEM), pl.BlockSpec(keep.shape), pl.BlockSpec(keep.shape)],
            out_shape=[struct((keep.shape[0], half), jnp.bfloat16)] * 2,
            compiler_params=pltpu.CompilerParams(vmem_limit_bytes=VMEM_LIMIT),
            cost_estimate=LIGHT,
        )(side_scalar, keep, got)

    def exchange(*halves):
        mine, theirs = joined(*[half[0] for half in halves]), beside(joined(*[half[1] for half in halves]))
        low_first = jnp.where(side == 0, mine, theirs)
        high = jnp.where(side == 0, theirs, mine)
        return joined(low_first, high).astype(jnp.float32)

    act_other0 = beside(act_send0)
    two_sum0, two_sum1, two_over, two_sum2 = scatter(two0, two1, two2, two3)
    ups = ups_own + gather_other(up_other, two0, two_over)
    sum_p0 = start_sum(ups, tie(act_keep, two_over), 0, act_other0)
    act_other1 = beside(tie(act_send1, sum_p0[0]))
    middle_grads, middle_low, sums_two = call(
        middle_back_kernel,
        [rows_wide, rows_low, struct((4, dim), jnp.float32)],
        middle, tie(two_sum0, sum_p0[0]), two_sum1, two_sum2, grad_out, row(ln2_gain),
    )
    mid_beside, mid_across = swap(middle_low, "tp", 1), swap(middle_low, "tp", 2)
    sum_p1 = start_sum(ups, tie(act_keep, middle_low), 1, act_other1)
    low_other0 = beside(tie(low_send0, sum_p1[0]))

    mid_across = tie(mid_across, sum_p1[0])
    mid_opposite = swap(mid_across, "tp", 1)
    mids_own = (middle_low, mid_beside, mid_across, mid_opposite)
    attended_grads = call(
        attended_grads_kernel, struct(attended.shape, jnp.bfloat16), *mids_own, w_out
    )
    mlp_sum0, mlp_sum1, _, mlp_sum2 = scatter(mlp0, mlp1, mlp2, mlp3, attended_grads)
    sum_p0 = step_sum(sum_p0, attended_grads)
    att_keep, att_send = column_halves(attended)

    back = backward_calls(queries, keys, values, meta, rows_info, keys_info, norm, attended, attended_grads, heads)
    start, delta, *kv_far = back[0](sum_p0[0])
    low_other1 = beside(tie(low_send1, start))
    mid_other = beside(tie(middle_low, start))
    far0, far1, far_over, far2 = scatter(*kv_far, start)
    twos = (normed_two, two_beside, two_across, two_opposite) + gather_other(two_other, attended_grads, start)
    sum_f0 = start_sum(twos, tie(low_keep, far_over), 0, low_other0)
    sum_p1 = step_sum(sum_p1, sum_f0[0])
    query_low, bias_query, *kv_near = back[1](start, delta, sum_p1[0])

    one = project(query_low, w_query, dot_nt)
    dq_keep, dq_send = column_halves(query_low)
    dq_other = beside(dq_send)
    att_other = beside(tie(att_send, query_low))
    near0, near1, near_over, near2 = scatter(*kv_near, one[0])
    one0, one1, one_over, one2 = scatter(*one, near_over)
    far_sum = add_low(tie(far0, one_over), far1, far2)
    far_there = swap(far_sum, "seq", seq_count // 2)
    sum_f1 = start_sum(twos, tie(low_keep, far_sum), 1, low_other1)
    done_p0 = finish_sum(sum_p0, sum_f1[0])
    kv_slots = add_low(tie(near0, done_p0[0]), near1, near2, far_there)
    sum_f0 = step_sum(sum_f0, kv_slots)
    ones = blocks_one + gather_other(one_other, start, kv_slots)
    sum_q = start_sum(ones, tie(dq_keep, sum_f0[0]), 0, dq_other)
    for bit in seq_bits[-2::-1]:
        kv_slots = add_low(tie(kv_slots[:bit], sum_q[0]), swap(kv_slots[bit:], "seq", bit))
    kv_low = kv_slots[0]
    kv_group = joined(*gather_rows(kv_low))
    kv_beside = beside(kv_group)
    grad_in, sums_one, sums_value = call(
        last_kernel,
        [rows_wide, struct((2, dim), jnp.float32), struct((1, head_dim), jnp.float32)],
        hidden_in, one0, one1, one2, kv_low, w_kv, middle_grads, row(ln1_gain),
    )
    mids = mids_own + gather_other(mid_other, far_sum, sums_value)
    sum_o = start_sum(mids, tie(att_keep, sums_value), 0, att_other)
    done_p1 = finish_sum(sum_p1, sum_o[0])
    sum_f1 = step_sum(sum_f1, done_p1[0])
    layer_out = call(layer_kernel, rows_low, tie(middle, sum_f1[0]), mlp_sum0, mlp_sum1, mlp_sum2, row(b_proj))

    vectors = [sums_two.reshape(-1), sums_one.reshape(-1), sums_value[0]]
    split = [bias_query[0], (sum_near + sum_far)[0]]
    vectors = jnp.concatenate(vectors + split).reshape(-1, 128)
    vectors = sum_over(vectors, "seq").reshape(-1)
    count = 6 * dim + head_dim
    shared = sum_over(vectors[:count].reshape(-1, 128), "tp").reshape(-1)
    split = vectors[count:]
    queries_width = bias_query.shape[1]

    part_kv = slab_grads(ones, slab, tie(kv_group, sum_f1[0]), kv_beside, 2 * tp_count)
    for bit in seq_bits[1:]:
        part_kv = add_low(part_kv, swap(part_kv, "seq", bit))
    got = beside(part_kv)
    half_kv = jnp.where(side == 0, jnp.stack([part_kv, got]), jnp.stack([got, part_kv]))
    quarters = gather_rows(half_kv)
    grad_kv = jnp.concatenate(
        [
            jnp.where(tp_index == j, quarters[0], jnp.where(tp_index == j ^ 1, quarters[1], jnp.where(tp_index == j ^ 2, quarters[2], quarters[3])))
            for j in range(tp_count)
        ]
    )
    grad_kv = jnp.swapaxes(grad_kv.astype(jnp.float32), 1, 2).reshape(dim, 2 * head_dim)

    grad_proj = exchange(done_p0, done_p1)
    sum_q = step_sum(sum_q, part_kv)
    sum_o = step_sum(sum_o, sum_q[0])
    done_f0 = finish_sum(sum_f0, sum_o[0])
    done_f1 = finish_sum(sum_f1, done_f0[0])
    done_q = finish_sum(sum_q, done_f1[0])
    done_o = finish_sum(sum_o, done_q[0])
    grad_fc = exchange(done_f0, done_f1).T
    grad_query = exchange(done_q).T
    grad_out_weight = exchange(done_o)
    return (
        layer_out,
        grad_in,
        shared[4 * dim : 5 * dim],
        shared[5 * dim : 6 * dim],
        grad_query,
        split[:queries_width],
        grad_kv,
        shared[6 * dim :],
        grad_out_weight,
        shared[3 * dim : 4 * dim],
        shared[dim : 2 * dim],
        shared[2 * dim : 3 * dim],
        grad_fc,
        split[queries_width:],
        grad_proj,
        shared[:dim],
    )


def solution(mesh):
    placed = (
        P(("seq", "tp"), None), P(), P(), P(), P(None, "tp"), P("tp"), P(), P(), P("tp", None),
        P(), P(), P(), P(None, "tp"), P("tp"), P("tp", None), P(), P(("seq", "tp"), None),
    )
    returned = (
        P(("seq", "tp"), None), P(("seq", "tp"), None), P(), P(), P("seq", "tp"), P("tp"), P(), P(),
        P("tp", "seq"), P(), P(), P(), P("seq", "tp"), P("tp"), P("tp", "seq"), P(),
    )
    return jax.shard_map(body, mesh=mesh, in_specs=placed, out_specs=returned, check_vma=False)
```

time: 1180 us -> 506 us (0.43)
  waiting for transfers between devices: 870 us -> 140 us
  Pallas kernels: 0 us -> 187 us
  matrix products: 117 us -> 0 us
  starting transfers between devices: 13.4 us -> 119 us
  blocking collectives: 80 us -> 0 us
  other arithmetic: 36.5 us -> 14.6 us
  loops' own time: 16.2 us -> 0 us
  between operations: 14.7 us -> 1.85 us
    reduce_scatter x9 -> x0, waiting for transfers between devices: 576 us -> none  [the longest x2 173 us: column_weight_grads(): lax.psum_scatter(partial_value.astype(jnp.bfloat16), 'seq', scatter_dimen...]
    pallas_call x0 -> x47, Pallas kernels: none -> 187 us  [the longest x23 62 us: call(): pl.pallas_call(kernel, out_shape=outs, compiler_params=pltpu.CompilerPara...]
    ppermute x0 -> x97, waiting for transfers between devices: none -> 140 us  [swap(): return lax.ppermute(value, axis, [(j, j ^ bit) for j in range(count)])]
    psum x1 -> x0, waiting for transfers between devices: 137 us -> none  [body(): lax.psum((grad_kv_part, grad_gain_one, grad_bias_one, grad_bias_out, grad...]
    all_gather x5 -> x0, waiting for transfers between devices: 136 us -> none  [the longest x1 56.1 us: body(): lax.all_gather(key_values(normed_one, w_kv, b_value), ('seq', 'tp'), axis...]
    ppermute x0 -> x97, starting transfers between devices: none -> 119 us  [swap(): return lax.ppermute(value, axis, [(j, j ^ bit) for j in range(count)])]
    dot_general x22 -> x0, matrix products: 117 us -> none  [the longest x2 14.3 us: row_weight_grads(): jnp.einsum('rk,rf->kf', gathered, column_grads, preferred_element_type=jn...]
    psum x2 -> x0, blocking collectives: 80 us -> none  [the longest x1 44.3 us: body(): lax.psum((grad_kv_part, grad_gain_one, grad_bias_one, grad_bias_out, grad...]
  transfers between devices with their start and end apart: 16 -> 97, of which waited for: 16 -> 30; matrix products, arithmetic and copies ran while one was open for 7% -> 6% of each run, Pallas kernels for 0% -> 32%
where the time goes in v1:
time: 506 us; the launch traced here: 497 us
  Pallas kernels  187 us (37%)
  waiting for transfers between devices  140 us (28%)
  starting transfers between devices  119 us (24%)
  local copies, waits for them, and re-layouts  35.3 us (7%)
  other arithmetic  14.6 us (3%)
    ppermute x97, waiting for transfers between devices, swap(): return lax.ppermute(value, axis, [(j, j ^ bit) for j in range(count)])  140 us
    ppermute x97, starting transfers between devices, swap(): return lax.ppermute(value, axis, [(j, j ^ bit) for j in range(count)])  119 us
    pallas_call x23, Pallas kernels, call(): pl.pallas_call(kernel, out_shape=outs, compiler_params=pltpu.CompilerPara...  62 us
    pallas_call x6, Pallas kernels, weight_grads(): pl.pallas_call(weight_kernel, grid_spec=pltpu.PrefetchScalarGridSpec(num_...  40.2 us
    pallas_call x2, Pallas kernels, mlp(): pl.pallas_call(functools.partial(mlp_kernel, tiles, len(before)), grid_sp...  34 us
    unnamed x189, local copies, waits for them, and re-layouts  22.8 us
    pallas_call x3, Pallas kernels, attention_call(): pl.pallas_call(kernel, grid_spec=pltpu.PrefetchScalarGridSpec(num_scalar_...  20.5 us
    pallas_call x6, Pallas kernels, split_add(): pl.pallas_call(split_kernel, grid_spec=pltpu.PrefetchScalarGridSpec(num_s...  15.8 us
  transfers between devices with their start and end apart: 97, of which 30 were waited for; matrix products, arithmetic and copies ran while one was open for 6% of the time, Pallas kernels for 32%

profile of v1, /device:TPU:0, one launch (start us, length us, event | category | flops | bytes accessed | tf_op | source)
XLA Modules:
  0.0 497.2 jit_solution(8564116125817775710)
XLA Ops:
  13.8 5.3 %collective-permute-done.9 = bf16[128,128]{1,0:T(8,128)(2,1)S(1)} collective-permute-done((bf16[128,128]{1,0:T(8,128)(2,1)}, bf16[128,128]{1,0:T(8,128)(2,1)S(1)}, u32[]{:S(2)}, u32[]{:S(2)}) %collective-permute-start.9) | collective-permute-done | bytes 32800 | tf_op jit(solution)/shard_map/ppermute | solution.py:37
  42.4 4.3 shard_map.289.q_ref
  49.8 6.3 %shard_map.290 = (bf16[512,512]{1,0:T(8,128)(2,1)}, f32[4,512]{1,0:T(4,128)}) custom-call(s32[3,8]{1,0:T(4,128)} %pad_add_fusion.1.meta, bf16[512,512]{1,0:T(8,128)(2,1)} %shard_map.289.q_ref, bf16[8,128,128]{2,1,0:T(8,128)(2,1)} %copy-done.14, bf16[8,128,128]{2,1,0:T(8,128)(2,1)} %copy-done.16, bf16[8,128,128]{2,1,0:T(8,128)(2,1)} %copy-done.15, ...), custom_call_target="tpu_custom_call" | custom-call | flops 1024 | bytes 1024 | tf_op jit(solution)/shard_map/pallas_call | solution.py:542
  59.4 3.5 shard_map.292
  68.3 13.0 %collective-permute-done.16.p2 = bf16[128,2048]{1,0:T(8,128)(2,1)S(1)} collective-permute-done((bf16[128,2048]{1,0:T(8,128)(2,1)}, bf16[128,2048]{1,0:T(8,128)(2,1)S(1)}, u32[]{:S(2)}, u32[]{:S(2)}) %collective-permute-start.16) | collective-permute-done | bytes 524320 | tf_op jit(solution)/shard_map/ppermute | solution.py:37
  93.5 17.0 %shard_map.295 = (bf16[512,512]{1,0:T(8,128)(2,1)}, bf16[512,512]{1,0:T(8,128)(2,1)}, bf16[512,1024]{1,0:T(8,128)(2,1)}, bf16[512,512]{1,0:T(8,128)(2,1)}, bf16[...) custom-call(s32[1]{0:T(128)} %bitcast.42.meta.side, ...), custom_call_target="tpu_custom_call" | custom-call | flops 1024 | bytes 1024 | tf_op jit(solution)/shard_map/pallas_call | solution.py:366
  113.5 17.0 %shard_map.296 = (bf16[512,512]{1,0:T(8,128)(2,1)}, bf16[512,512]{1,0:T(8,128)(2,1)}, bf16[512,1024]{1,0:T(8,128)(2,1)}, bf16[512,512]{1,0:T(8,128)(2,1)}, bf16[...) custom-call(s32[1]{0:T(128)} %bitcast.42.meta.side, ...), custom_call_target="tpu_custom_call", output_to_operand_aliasing={{0}: (8, {}), {1}: (9, {}), {2}: (10, {}), {3}: (11, {}), {... | custom-call | flops 1024 | bytes 1024 | tf_op jit(solution)/shard_map/pallas_call | solution.py:366
  138.7 6.3 %collective-permute-done.26.refs_6_ = bf16[128,2048]{1,0:T(8,128)(2,1)S(1)} collective-permute-done((bf16[128,2048]{1,0:T(8,128)(2,1)}, bf16[128,2048]{1,0:T(8,128)(2,1)S(1)}, u32[]{:S(2)}, u32[]{:S(2)}) %collective-permute-start.26) | collective-permute-done | bytes 524320 | tf_op jit(solution)/shard_map/ppermute | solution.py:37
  149.6 7.2 %shard_map.298 = (bf16[2,512,512]{2,1,0:T(8,128)(2,1)}, bf16[2,512,512]{2,1,0:T(8,128)(2,1)}) custom-call(s32[1]{0:T(128)} %bitcast.41.meta, bf16[128,2048]{1,0:T(8,128)(2,1)} %refs_0_.1, bf16[128,2048]{1,0:T(8,128)(2,1)} %copy-done.10, bf16[128,2048]{1,0:T(8,128)(2,1)} %copy-done.11, bf16[128,2048]{1,0:T(8,128)(2,1)} %copy-done.12, ...), custom_call_target="tpu_custom_call" | custom-call | flops 1024 | bytes 1024 | tf_op jit(solution)/shard_map/pallas_call | solution.py:242
  160.4 4.1 shard_map.299
  166.1 4.3 collective-permute-start.38
  172.2 7.2 %shard_map.300 = (bf16[2,512,512]{2,1,0:T(8,128)(2,1)}, bf16[2,512,512]{2,1,0:T(8,128)(2,1)}) custom-call(s32[1]{0:T(128)} %bitcast.41.meta, bf16[128,2048]{1,0:T(8,128)(2,1)} %refs_0_.1, bf16[128,2048]{1,0:T(8,128)(2,1)} %copy-done.10, bf16[128,2048]{1,0:T(8,128)(2,1)} %copy-done.11, bf16[128,2048]{1,0:T(8,128)(2,1)} %copy-done.12, ...), custom_call_target="tpu_custom_call" | custom-call | flops 1024 | bytes 1024 | tf_op jit(solution)/shard_map/pallas_call | solution.py:242
  183.3 4.3 shard_map.301.refs_11_
  187.7 6.4 %collective-permute-done.21.refs_4_ = bf16[128,2048]{1,0:T(8,128)(2,1)S(1)} collective-permute-done((bf16[128,2048]{1,0:T(8,128)(2,1)S(1)}, bf16[128,2048]{1,0:T(8,128)(2,1)S(1)}, u32[]{:S(2)}, u32[]{:S(2)}) %collective-permute-start.21) | collective-permute-done | bytes 524320 | tf_op jit(solution)/shard_map/ppermute | solution.py:37
  195.3 4.0 collective-permute-start.42
  204.2 5.6 %shard_map.303 = (f32[4,128,512]{2,1,0:T(8,128)}, f32[4,512]{1,0:T(4,128)}, bf16[4,128,256]{2,1,0:T(8,128)(2,1)}, bf16[4,128,256]{2,1,0:T(8,128)(2,1)}, bf16[4,1...) custom-call(s32[3,8]{1,0:T(4,128)} %pad_add_fusion.1.meta, bf16[512,512]{1,0:T(8,128)(2,1)} %shard_map.289.q_ref, ...), custom_call_target="tpu_custom_call" | custom-call | flops 1024 | bytes 1024 | tf_op jit(solution)/shard_map/pallas_call | solution.py:542
  214.6 19.0 %collective-permute-start.53 = (bf16[1,512,512]{2,1,0:T(8,128)(2,1)}, bf16[1,512,512]{2,1,0:T(8,128)(2,1)S(1)}, u32[]{:S(2)}, u32[]{:S(2)}) collective-permute-start(bf16[1,512,512]{2,1,0:T(8,128)(2,1)} %get-tuple-element.236), channel_id=1, source_target_pairs={{0,16},{4,20},{8,24},{12,28},{16,0},{20,4},{24,8},{28,12},{1,17},{... | collective-permute-start | bytes 1572872 | tf_op jit(solution)/shard_map/ppermute | solution.py:37
  235.6 7.2 %shard_map.305 = (bf16[2,512,512]{2,1,0:T(8,128)(2,1)}, bf16[2,512,512]{2,1,0:T(8,128)(2,1)}) custom-call(s32[1]{0:T(128)} %bitcast.41.meta, bf16[128,2048]{1,0:T(8,128)(2,1)} %get-tuple-element.168.x0.refs_0_, bf16[128,2048]{1,0:T(8,128)(2,1)} %copy-done.7, bf16[128,2048]{1,0:T(8,128)(2,1)} %copy-done.8, bf16[128,2048]{1,0:T(8,128)(2,1)} %copy-done.9, ...), custom_call_target="tpu_custom_call" | custom-call | flops 1024 | bytes 1024 | tf_op jit(solution)/shard_map/pallas_call | solution.py:242
  245.6 8.7 %shard_map.307 = (bf16[512,512]{1,0:T(8,128)(2,1)}, f32[1,512]{1,0:T(1,128)}, bf16[4,128,256]{2,1,0:T(8,128)(2,1)}, bf16[4,128,256]{2,1,0:T(8,128)(2,1)}, bf16[4...) custom-call(s32[3,8]{1,0:T(4,128)} %pad_add_fusion.1.meta, bf16[512,512]{1,0:T(8,128)(2,1)} %shard_map.289.q_ref, ...), custom_call_target="tpu_custom_call" | custom-call | flops 1024 | bytes 1024 | tf_op jit(solution)/shard_map/pallas_call | solution.py:542
  254.3 3.5 shard_map.308
  258.4 6.4 %collective-permute-start.61 = (bf16[2,512,512]{2,1,0:T(8,128)(2,1)}, bf16[2,512,512]{2,1,0:T(8,128)(2,1)}, u32[]{:S(2)}, u32[]{:S(2)}) collective-permute-start(bf16[2,512,512]{2,1,0:T(8,128)(2,1)} %get-tuple-element.243), channel_id=1, source_target_pairs={{0,8},{4,12},{8,0},{12,4},{16,24},{20,28},{24,16},{28,20},{1,9},{5... | collective-permute-start | bytes 3145736 | tf_op jit(solution)/shard_map/ppermute | solution.py:37
  279.9 10.1 %collective-permute-done.55.refs_2_ = bf16[4,128,256]{2,1,0:T(8,128)(2,1)S(1)} collective-permute-done((bf16[4,128,256]{2,1,0:T(8,128)(2,1)}, bf16[4,128,256]{2,1,0:T(8,128)(2,1)S(1)}, u32[]{:S(2)}, u32[]{:S(2)}) %collective-permute-start.55) | collective-permute-done | bytes 262176 | tf_op jit(solution)/shard_map/ppermute | solution.py:37
  292.6 7.2 %shard_map.313 = (bf16[2,512,512]{2,1,0:T(8,128)(2,1)}, bf16[2,512,512]{2,1,0:T(8,128)(2,1)}) custom-call(s32[1]{0:T(128)} %bitcast.41.meta, bf16[128,2048]{1,0:T(8,128)(2,1)} %get-tuple-element.168.x0.refs_0_, bf16[128,2048]{1,0:T(8,128)(2,1)} %copy-done.7, bf16[128,2048]{1,0:T(8,128)(2,1)} %copy-done.8, bf16[128,2048]{1,0:T(8,128)(2,1)} %copy-done.9, ...), custom_call_target="tpu_custom_call" | custom-call | flops 1024 | bytes 1024 | tf_op jit(solution)/shard_map/pallas_call | solution.py:242
  310.9 5.8 %shard_map.317 = (bf16[2,256,512]{2,1,0:T(8,128)(2,1)}, bf16[2,256,512]{2,1,0:T(8,128)(2,1)}) custom-call(s32[1]{0:T(128)} %bitcast.41.meta, bf16[128,2048]{1,0:T(8,128)(2,1)} %get-tuple-element.157.r0.refs_0_, bf16[128,2048]{1,0:T(8,128)(2,1)} %copy-done.4, bf16[128,2048]{1,0:T(8,128)(2,1)} %copy-done.3, bf16[128,2048]{1,0:T(8,128)(2,1)} %copy-done.5, ...), custom_call_target="tpu_custom_call" | custom-call | flops 1024 | bytes 1024 | tf_op jit(solution)/shard_map/pallas_call | solution.py:242
  327.7 4.3 shard_map.320
  345.7 16.5 %collective-permute-done.73 = f32[117,128]{1,0:T(8,128)S(1)} collective-permute-done((f32[117,128]{1,0:T(8,128)S(1)}, f32[117,128]{1,0:T(8,128)S(1)}, u32[]{:S(2)}, u32[]{:S(2)}) %collective-permute-start.73) | collective-permute-done | bytes 59936 | tf_op jit(solution)/shard_map/ppermute | solution.py:37
  366.6 15.3 %collective-permute-done.74 = f32[117,128]{1,0:T(8,128)S(1)} collective-permute-done((f32[117,128]{1,0:T(8,128)S(1)}, f32[117,128]{1,0:T(8,128)S(1)}, u32[]{:S(2)}, u32[]{:S(2)}) %collective-permute-start.74) | collective-permute-done | bytes 59936 | tf_op jit(solution)/shard_map/ppermute | solution.py:37
  385.6 5.6 %shard_map.321 = (bf16[2,256,512]{2,1,0:T(8,128)(2,1)}, bf16[2,256,512]{2,1,0:T(8,128)(2,1)}) custom-call(s32[1]{0:T(128)} %bitcast.41.meta, bf16[128,2048]{1,0:T(8,128)(2,1)} %get-tuple-element.231.r0.refs_0_, bf16[128,2048]{1,0:T(8,128)(2,1)} %copy-done.20, bf16[128,2048]{1,0:T(8,128)(2,1)} %copy-done.19, bf16[128,2048]{1,0:T(8,128)(2,1)} %copy-done.21, ...), custom_call_target="tpu_custom_call" | custom-call | flops 1024 | bytes 1024 | tf_op jit(solution)/shard_map/pallas_call | solution.py:242
  404.7 6.9 %collective-permute-done.81.refs_1_ = bf16[256,256]{1,0:T(8,128)(2,1)S(1)} collective-permute-done((bf16[256,256]{1,0:T(8,128)(2,1)}, bf16[256,256]{1,0:T(8,128)(2,1)S(1)}, u32[]{:S(2)}, u32[]{:S(2)}) %collective-permute-start.81) | collective-permute-done | bytes 131104 | tf_op jit(solution)/shard_map/ppermute | solution.py:37
  416.9 17.4 %collective-permute-done.82.refs_1_ = bf16[256,256]{1,0:T(8,128)(2,1)S(1)} collective-permute-done((bf16[256,256]{1,0:T(8,128)(2,1)}, bf16[256,256]{1,0:T(8,128)(2,1)S(1)}, u32[]{:S(2)}, u32[]{:S(2)}) %collective-permute-start.82) | collective-permute-done | bytes 131104 | tf_op jit(solution)/shard_map/ppermute | solution.py:37
  441.3 9.7 %collective-permute-done.89 = bf16[256,256]{1,0:T(8,128)(2,1)S(1)} collective-permute-done((bf16[256,256]{1,0:T(8,128)(2,1)}, bf16[256,256]{1,0:T(8,128)(2,1)S(1)}, u32[]{:S(2)}, u32[]{:S(2)}) %collective-permute-start.89) | collective-permute-done | bytes 131104 | tf_op jit(solution)/shard_map/ppermute | solution.py:37
  475.1 10.2 %collective-permute-done.88 = bf16[256,256]{1,0:T(8,128)(2,1)S(1)} collective-permute-done((bf16[256,256]{1,0:T(8,128)(2,1)}, bf16[256,256]{1,0:T(8,128)(2,1)S(1)}, u32[]{:S(2)}, u32[]{:S(2)}) %collective-permute-start.88) | collective-permute-done | bytes 131104 | tf_op jit(solution)/shard_map/ppermute | solution.py:37
  (453 shorter events, 225.9 us)
Async XLA Ops:
  3.3 35.3 %collective-permute-start.1 = (bf16[128,2048]{1,0:T(8,128)(2,1)}, bf16[128,2048]{1,0:T(8,128)(2,1)S(1)}, u32[]{:S(2)}, u32[]{:S(2)}) collective-permute-start(bf16[128,2048]{1,0:T(8,128)(2,1)} %get-tuple-element.157.r0.refs_0_), channel_id=1, source_target_pairs={{0,2},{1,3},{2,0},{3,1},{4,6},{5,7},{6,4},{7,5},{8,10},{9,11},{10,... | collective-permute-start | bytes 1572872 | tf_op jit(solution)/shard_map/ppermute | solution.py:37
  6.2 35.1 %collective-permute-start = (bf16[128,2048]{1,0:T(8,128)(2,1)}, bf16[128,2048]{1,0:T(8,128)(2,1)S(1)}, u32[]{:S(2)}, u32[]{:S(2)}) collective-permute-start(bf16[128,2048]{1,0:T(8,128)(2,1)} %get-tuple-element.157.r0.refs_0_), channel_id=1, source_target_pairs={{0,1},{1,0},{2,3},{3,2},{4,5},{5,4},{6,7},{7,6},{8,9},{9,8},{10,11... | collective-permute-start | bytes 1572872 | tf_op jit(solution)/shard_map/ppermute | solution.py:37
  67.8 24.7 %collective-permute-start.19 = (bf16[128,2048]{1,0:T(8,128)(2,1)S(1)}, bf16[128,2048]{1,0:T(8,128)(2,1)S(1)}, u32[]{:S(2)}, u32[]{:S(2)}) collective-permute-start(bf16[128,2048]{1,0:T(8,128)(2,1)S(1)} %copy-done.1), channel_id=1, source_target_pairs={{0,1},{1,0},{2,3},{3,2},{4,5},{5,4},{6,7},{7,6},{8,9},{9,8},{10,11... | collective-permute-start | bytes 1572872 | tf_op jit(solution)/shard_map/ppermute | solution.py:37
  67.8 24.7 %collective-permute-start.22 = (bf16[128,2048]{1,0:T(8,128)(2,1)S(1)}, bf16[128,2048]{1,0:T(8,128)(2,1)S(1)}, u32[]{:S(2)}, u32[]{:S(2)}) collective-permute-start(bf16[128,2048]{1,0:T(8,128)(2,1)S(1)} %copy-done.1), channel_id=1, source_target_pairs={{0,2},{1,3},{2,0},{3,1},{4,6},{5,7},{6,4},{7,5},{8,10},{9,11},{10,... | collective-permute-start | bytes 1572872 | tf_op jit(solution)/shard_map/ppermute | solution.py:37
  85.1 25.4 %collective-permute-start.18 = (bf16[128,2048]{1,0:T(8,128)(2,1)}, bf16[128,2048]{1,0:T(8,128)(2,1)S(1)}, u32[]{:S(2)}, u32[]{:S(2)}) collective-permute-start(bf16[128,2048]{1,0:T(8,128)(2,1)} %get-tuple-element.168.x0.refs_0_), channel_id=1, source_target_pairs={{0,2},{1,3},{2,0},{3,1},{4,6},{5,7},{6,4},{7,5},{8,10},{9,11},{10,... | collective-permute-start | bytes 1572872 | tf_op jit(solution)/shard_map/ppermute | solution.py:37
  86.7 24.5 %collective-permute-start.24 = (bf16[128,2048]{1,0:T(8,128)(2,1)S(1)}, bf16[128,2048]{1,0:T(8,128)(2,1)}, u32[]{:S(2)}, u32[]{:S(2)}) collective-permute-start(bf16[128,2048]{1,0:T(8,128)(2,1)S(1)} %copy-done.1), channel_id=1, source_target_pairs={{0,4},{4,0},{8,12},{12,8},{16,20},{20,16},{24,28},{28,24},{1,5},{5... | collective-permute-start | bytes 1572872 | tf_op jit(solution)/shard_map/ppermute | solution.py:37
  166.1 34.9 %collective-permute-start.38 = (bf16[2,512,512]{2,1,0:T(8,128)(2,1)}, bf16[2,512,512]{2,1,0:T(8,128)(2,1)}, u32[]{:S(2)}, u32[]{:S(2)}) collective-permute-start(bf16[2,512,512]{2,1,0:T(8,128)(2,1)} %get-tuple-element.196), channel_id=1, source_target_pairs={{0,8},{4,12},{8,0},{12,4},{16,24},{20,28},{24,16},{28,20},{1,9},{5... | collective-permute-start | bytes 3145736 | tf_op jit(solution)/shard_map/ppermute | solution.py:37
  195.3 47.5 %collective-permute-start.42 = (bf16[2,512,512]{2,1,0:T(8,128)(2,1)}, bf16[2,512,512]{2,1,0:T(8,128)(2,1)}, u32[]{:S(2)}, u32[]{:S(2)}) collective-permute-start(bf16[2,512,512]{2,1,0:T(8,128)(2,1)} %get-tuple-element.212), channel_id=1, source_target_pairs={{0,8},{4,12},{8,0},{12,4},{16,24},{20,28},{24,16},{28,20},{1,9},{5... | collective-permute-start | bytes 3145736 | tf_op jit(solution)/shard_map/ppermute | solution.py:37
  209.8 23.7 %collective-permute-start.39 = (bf16[128,2048]{1,0:T(8,128)(2,1)S(1)}, bf16[128,2048]{1,0:T(8,128)(2,1)S(1)}, u32[]{:S(2)}, u32[]{:S(2)}) collective-permute-start(bf16[128,2048]{1,0:T(8,128)(2,1)S(1)} %collective-permute-done.37.refs_6_), channel_id=1, source_target_pairs={{0,1},{1,0},{2,3},{3,2},{4,5},{5,4},{6,7},{7,6},{8,9},{9,8},{10,11... | collective-permute-start | bytes 1572872 | tf_op jit(solution)/shard_map/ppermute | solution.py:37
  212.5 45.6 %collective-permute-start.57 = (bf16[128,2048]{1,0:T(8,128)(2,1)S(1)}, bf16[128,2048]{1,0:T(8,128)(2,1)S(1)}, u32[]{:S(2)}, u32[]{:S(2)}) collective-permute-start(bf16[128,2048]{1,0:T(8,128)(2,1)S(1)} %copy-done.2), channel_id=1, source_target_pairs={{0,4},{4,0},{8,12},{12,8},{16,20},{20,16},{24,28},{28,24},{1,5},{5... | collective-permute-start | bytes 1572872 | tf_op jit(solution)/shard_map/ppermute | solution.py:37
  214.3 50.5 %collective-permute-start.47 = (bf16[512,512]{1,0:T(8,128)(2,1)}, bf16[512,512]{1,0:T(8,128)(2,1)S(1)}, u32[]{:S(2)}, u32[]{:S(2)}) collective-permute-start(bf16[512,512]{1,0:T(8,128)(2,1)} %get-tuple-element.229), channel_id=1, source_target_pairs={{0,4},{4,0},{8,12},{12,8},{16,20},{20,16},{24,28},{28,24},{1,5},{5... | collective-permute-start | bytes 1572872 | tf_op jit(solution)/shard_map/ppermute | solution.py:37
  214.6 50.8 %collective-permute-start.53 = (bf16[1,512,512]{2,1,0:T(8,128)(2,1)}, bf16[1,512,512]{2,1,0:T(8,128)(2,1)S(1)}, u32[]{:S(2)}, u32[]{:S(2)}) collective-permute-start(bf16[1,512,512]{2,1,0:T(8,128)(2,1)} %get-tuple-element.236), channel_id=1, source_target_pairs={{0,16},{4,20},{8,24},{12,28},{16,0},{20,4},{24,8},{28,12},{1,17},{... | collective-permute-start | bytes 1572872 | tf_op jit(solution)/shard_map/ppermute | solution.py:37
  233.6 24.8 %collective-permute-start.45 = (bf16[4,128,256]{2,1,0:T(8,128)(2,1)}, bf16[4,128,256]{2,1,0:T(8,128)(2,1)}, u32[]{:S(2)}, u32[]{:S(2)}) collective-permute-start(bf16[4,128,256]{2,1,0:T(8,128)(2,1)} %get-tuple-element.226), channel_id=1, source_target_pairs={{0,1},{1,0},{2,3},{3,2},{4,5},{5,4},{6,7},{7,6},{8,9},{9,8},{10,11... | collective-permute-start | bytes 786440 | tf_op jit(solution)/shard_map/ppermute | solution.py:37
  258.4 48.5 %collective-permute-start.61 = (bf16[2,512,512]{2,1,0:T(8,128)(2,1)}, bf16[2,512,512]{2,1,0:T(8,128)(2,1)}, u32[]{:S(2)}, u32[]{:S(2)}) collective-permute-start(bf16[2,512,512]{2,1,0:T(8,128)(2,1)} %get-tuple-element.243), channel_id=1, source_target_pairs={{0,8},{4,12},{8,0},{12,4},{16,24},{20,28},{24,16},{28,20},{1,9},{5... | collective-permute-start | bytes 3145736 | tf_op jit(solution)/shard_map/ppermute | solution.py:37
  265.4 38.7 %collective-permute-start.59 = (bf16[128,2048]{1,0:T(8,128)(2,1)S(1)}, bf16[128,2048]{1,0:T(8,128)(2,1)S(1)}, u32[]{:S(2)}, u32[]{:S(2)}) collective-permute-start(bf16[128,2048]{1,0:T(8,128)(2,1)S(1)} %collective-permute-done.57.refs_4_), channel_id=1, source_target_pairs={{0,2},{1,3},{2,0},{3,1},{4,6},{5,7},{6,4},{7,5},{8,10},{9,11},{10,... | collective-permute-start | bytes 1572872 | tf_op jit(solution)/shard_map/ppermute | solution.py:37
  274.1 30.1 %collective-permute-start.58 = (bf16[128,2048]{1,0:T(8,128)(2,1)S(1)}, bf16[128,2048]{1,0:T(8,128)(2,1)S(1)}, u32[]{:S(2)}, u32[]{:S(2)}) collective-permute-start(bf16[128,2048]{1,0:T(8,128)(2,1)S(1)} %collective-permute-done.57.refs_4_), channel_id=1, source_target_pairs={{0,1},{1,0},{2,3},{3,2},{4,5},{5,4},{6,7},{7,6},{8,9},{9,8},{10,11... | collective-permute-start | bytes 1572872 | tf_op jit(solution)/shard_map/ppermute | solution.py:37
  279.0 23.1 %collective-permute-start.56 = (bf16[4,128,256]{2,1,0:T(8,128)(2,1)}, bf16[4,128,256]{2,1,0:T(8,128)(2,1)}, u32[]{:S(2)}, u32[]{:S(2)}) collective-permute-start(bf16[4,128,256]{2,1,0:T(8,128)(2,1)} %shard_map.312), channel_id=1, source_target_pairs={{0,16},{4,20},{8,24},{12,28},{16,0},{20,4},{24,8},{28,12},{1,17},{... | collective-permute-start | bytes 786440 | tf_op jit(solution)/shard_map/ppermute | solution.py:37
  310.1 30.2 %collective-permute-start.70 = (bf16[128,2048]{1,0:T(8,128)(2,1)}, bf16[128,2048]{1,0:T(8,128)(2,1)}, u32[]{:S(2)}, u32[]{:S(2)}) collective-permute-start(bf16[128,2048]{1,0:T(8,128)(2,1)} %get-tuple-element.266), channel_id=1, source_target_pairs={{0,1},{1,0},{2,3},{3,2},{4,5},{5,4},{6,7},{7,6},{8,9},{9,8},{10,11... | collective-permute-start | bytes 1572872 | tf_op jit(solution)/shard_map/ppermute | solution.py:37
  335.2 47.2 %collective-permute-start.49 = (bf16[128,2048]{1,0:T(8,128)(2,1)}, bf16[128,2048]{1,0:T(8,128)(2,1)S(1)}, u32[]{:S(2)}, u32[]{:S(2)}) collective-permute-start(bf16[128,2048]{1,0:T(8,128)(2,1)} %collective-permute-done.48.refs_4_), channel_id=1, source_target_pairs={{0,1},{1,0},{2,3},{3,2},{4,5},{5,4},{6,7},{7,6},{8,9},{9,8},{10,11... | collective-permute-start | bytes 1572872 | tf_op jit(solution)/shard_map/ppermute | solution.py:37
  335.2 60.1 %collective-permute-start.68 = (bf16[2,512,512]{2,1,0:T(8,128)(2,1)}, bf16[2,512,512]{2,1,0:T(8,128)(2,1)S(1)}, u32[]{:S(2)}, u32[]{:S(2)}) collective-permute-start(bf16[2,512,512]{2,1,0:T(8,128)(2,1)} %get-tuple-element.259), channel_id=1, source_target_pairs={{0,8},{4,12},{8,0},{12,4},{16,24},{20,28},{24,16},{28,20},{1,9},{5... | collective-permute-start | bytes 3145736 | tf_op jit(solution)/shard_map/ppermute | solution.py:37
  337.7 24.6 %collective-permute-start.73 = (f32[117,128]{1,0:T(8,128)S(1)}, f32[117,128]{1,0:T(8,128)S(1)}, u32[]{:S(2)}, u32[]{:S(2)}) collective-permute-start(f32[117,128]{1,0:T(8,128)S(1)} %bitcast_add_fusion), channel_id=1, source_target_pairs={{0,8},{4,12},{8,0},{12,4},{16,24},{20,28},{24,16},{28,20},{1,9},{5... | collective-permute-start | bytes 179720 | tf_op jit(solution)/shard_map/ppermute | solution.py:37
  342.5 39.5 %collective-permute-start.66 = (bf16[512,256]{1,0:T(8,128)(2,1)}, bf16[512,256]{1,0:T(8,128)(2,1)S(1)}, u32[]{:S(2)}, u32[]{:S(2)}) collective-permute-start(bf16[512,256]{1,0:T(8,128)(2,1)} %get-tuple-element.253), channel_id=1, source_target_pairs={{0,4},{4,0},{8,12},{12,8},{16,20},{20,16},{24,28},{28,24},{1,5},{5... | collective-permute-start | bytes 786440 | tf_op jit(solution)/shard_map/ppermute | solution.py:37
  364.3 28.1 %collective-permute-start.67 = (bf16[1,512,512]{2,1,0:T(8,128)(2,1)}, bf16[1,512,512]{2,1,0:T(8,128)(2,1)S(1)}, u32[]{:S(2)}, u32[]{:S(2)}) collective-permute-start(bf16[1,512,512]{2,1,0:T(8,128)(2,1)} %get-tuple-element.256), channel_id=1, source_target_pairs={{0,16},{4,20},{8,24},{12,28},{16,0},{20,4},{24,8},{28,12},{1,17},{... | collective-permute-start | bytes 1572872 | tf_op jit(solution)/shard_map/ppermute | solution.py:37
  383.8 30.7 %collective-permute-start.69 = (bf16[128,2048]{1,0:T(8,128)(2,1)}, bf16[128,2048]{1,0:T(8,128)(2,1)}, u32[]{:S(2)}, u32[]{:S(2)}) collective-permute-start(bf16[128,2048]{1,0:T(8,128)(2,1)} %get-tuple-element.263), channel_id=1, source_target_pairs={{0,1},{1,0},{2,3},{3,2},{4,5},{5,4},{6,7},{7,6},{8,9},{9,8},{10,11... | collective-permute-start | bytes 1572872 | tf_op jit(solution)/shard_map/ppermute | solution.py:37
  384.0 52.6 %collective-permute-start.71 = (bf16[128,2048]{1,0:T(8,128)(2,1)}, bf16[128,2048]{1,0:T(8,128)(2,1)}, u32[]{:S(2)}, u32[]{:S(2)}) collective-permute-start(bf16[128,2048]{1,0:T(8,128)(2,1)} %shard_map.324), channel_id=1, source_target_pairs={{0,2},{1,3},{2,0},{3,1},{4,6},{5,7},{6,4},{7,5},{8,10},{9,11},{10,... | collective-permute-start | bytes 1572872 | tf_op jit(solution)/shard_map/ppermute | solution.py:37
  392.4 45.1 %collective-permute-start.83 = (bf16[2,256,512]{2,1,0:T(8,128)(2,1)}, bf16[2,256,512]{2,1,0:T(8,128)(2,1)S(1)}, u32[]{:S(2)}, u32[]{:S(2)}) collective-permute-start(bf16[2,256,512]{2,1,0:T(8,128)(2,1)} %get-tuple-element.275), channel_id=1, source_target_pairs={{0,8},{4,12},{8,0},{12,4},{16,24},{20,28},{24,16},{28,20},{1,9},{5... | collective-permute-start | bytes 1572872 | tf_op jit(solution)/shard_map/ppermute | solution.py:37
  403.8 57.2 %collective-permute-start.85 = (bf16[1,512,512]{2,1,0:T(8,128)(2,1)}, bf16[1,512,512]{2,1,0:T(8,128)(2,1)S(1)}, u32[]{:S(2)}, u32[]{:S(2)}) collective-permute-start(bf16[1,512,512]{2,1,0:T(8,128)(2,1)} %get-tuple-element.281), channel_id=1, source_target_pairs={{0,16},{4,20},{8,24},{12,28},{16,0},{20,4},{24,8},{28,12},{1,17},{... | collective-permute-start | bytes 1572872 | tf_op jit(solution)/shard_map/ppermute | solution.py:37
  414.5 42.9 %collective-permute-start.84 = (bf16[2,256,512]{2,1,0:T(8,128)(2,1)}, bf16[2,256,512]{2,1,0:T(8,128)(2,1)S(1)}, u32[]{:S(2)}, u32[]{:S(2)}) collective-permute-start(bf16[2,256,512]{2,1,0:T(8,128)(2,1)} %get-tuple-element.278), channel_id=1, source_target_pairs={{0,8},{4,12},{8,0},{12,4},{16,24},{20,28},{24,16},{28,20},{1,9},{5... | collective-permute-start | bytes 1572872 | tf_op jit(solution)/shard_map/ppermute | solution.py:37
  434.3 29.8 %collective-permute-start.86 = (bf16[1,512,512]{2,1,0:T(8,128)(2,1)}, bf16[1,512,512]{2,1,0:T(8,128)(2,1)S(1)}, u32[]{:S(2)}, u32[]{:S(2)}) collective-permute-start(bf16[1,512,512]{2,1,0:T(8,128)(2,1)} %get-tuple-element.284), channel_id=1, source_target_pairs={{0,16},{4,20},{8,24},{12,28},{16,0},{20,4},{24,8},{28,12},{1,17},{... | collective-permute-start | bytes 1572872 | tf_op jit(solution)/shard_map/ppermute | solution.py:37
  436.6 35.5 %collective-permute-start.96 = (bf16[1024,256]{1,0:T(8,128)(2,1)S(1)}, bf16[1024,256]{1,0:T(8,128)(2,1)S(1)}, u32[]{:S(2)}, u32[]{:S(2)}) collective-permute-start(bf16[1024,256]{1,0:T(8,128)(2,1)S(1)} %pad_maximum_fusion.1), channel_id=1, source_target_pairs={{0,4},{4,0},{8,12},{12,8},{16,20},{20,16},{24,28},{28,24},{1,5},{5... | collective-permute-start | bytes 1572872 | tf_op jit(solution)/shard_map/ppermute | solution.py:37
  461.0 28.7 %collective-permute-start.90 = (bf16[2,256,256]{2,1,0:T(8,128)(2,1)}, bf16[2,256,256]{2,1,0:T(8,128)(2,1)S(1)}, u32[]{:S(2)}, u32[]{:S(2)}) collective-permute-start(bf16[2,256,256]{2,1,0:T(8,128)(2,1)} %maximum_select_fusion), channel_id=1, source_target_pairs={{0,1},{1,0},{2,3},{3,2},{4,5},{5,4},{6,7},{7,6},{8,9},{9,8},{10,11... | collective-permute-start | bytes 786440 | tf_op jit(solution)/shard_map/ppermute | solution.py:37
  468.9 26.1 %collective-permute-start.95 = (bf16[1024,256]{1,0:T(8,128)(2,1)}, bf16[1024,256]{1,0:T(8,128)(2,1)S(1)}, u32[]{:S(2)}, u32[]{:S(2)}) collective-permute-start(bf16[1024,256]{1,0:T(8,128)(2,1)} %pad_maximum_fusion), channel_id=1, source_target_pairs={{0,4},{4,0},{8,12},{12,8},{16,20},{20,16},{24,28},{28,24},{1,5},{5... | collective-permute-start | bytes 1572872 | tf_op jit(solution)/shard_map/ppermute | solution.py:37
  (148 other events, 1294.4 us)

commit v2 on v1

--- a/solution.py
+++ b/solution.py
@@ -43,9 +43,37 @@
     return own, beside, across, swap(across, "tp", 1)
 
 
-def gather_other(own, first, second):
-    across = swap(tie(own, first), "tp", 2)
-    return own, swap(tie(own, first), "tp", 1), across, swap(tie(across, second), "tp", 1)
+def touch_kernel(value, out):
+    pass
+
+
+def touch(value, *deps):
+    anywhere = pl.BlockSpec(memory_space=pl.ANY)
+    return pl.pallas_call(
+        touch_kernel,
+        in_specs=[anywhere],
+        out_specs=anywhere,
+        out_shape=struct(value.shape, value.dtype),
+        input_output_aliases={0: 0},
+        cost_estimate=LIGHT,
+    )(tie(value, *deps))
+
+
+def gather_pair(own):
+    seq_count, tp_count = lax.axis_size("seq"), lax.axis_size("tp")
+    wide = 2 * tp_count
+    groups = [[first * wide + j for j in range(wide)] for first in range(seq_count // 2)]
+    return lax.all_gather(own, ("seq", "tp"), axis=0, tiled=True, axis_index_groups=groups)
+
+
+def half_gather(own):
+    return own, swap(own, "tp", 1), swap(own, "tp", 2)
+
+
+def full_gather(blocks, after):
+    own, beside, across = blocks
+    across = tie(across, after)
+    return own, beside, across, swap(across, "tp", 1)
 
 
 def call(kernel, outs, *args):
@@ -65,6 +93,27 @@
     refs[-1][...] = total(*refs[:-1]).astype(jnp.bfloat16)
 
 
+def add_split_kernel(*refs):
+    *parts, low_ref, high_ref = refs
+    both = total(*parts).astype(jnp.bfloat16)
+    half = low_ref.shape[0]
+    low_ref[...] = both[:half]
+    high_ref[...] = both[half:]
+
+
+def add_split(*values):
+    half = struct((values[0].shape[0] // 2, *values[0].shape[1:]), jnp.bfloat16)
+    return call(add_split_kernel, [half, half], *values)
+
+
+def columns_kernel(side, first, second, first_keep, second_keep, send):
+    half = first_keep.shape[1]
+    for index, (ref, keep) in enumerate(((first, first_keep), (second, second_keep))):
+        low, high = ref[:, :half], ref[:, half:]
+        keep[...] = jnp.where(side[0] == 0, low, high)
+        send[:, index * half : (index + 1) * half] = jnp.where(side[0] == 0, high, low)
+
+
 def add_low(*values):
     return call(add_kernel, struct(values[0].shape, jnp.bfloat16), *values)
 
@@ -81,9 +130,10 @@
         keep_ref[...] = both
 
 
-def halves_kernel(side, keep, got, mine, theirs):
+def halves_kernel(side, *refs):
+    *parts, mine, theirs = refs
     half = mine.shape[1]
-    both = total(keep, got).astype(jnp.bfloat16)
+    both = total(*parts).astype(jnp.bfloat16)
     low, high = both[:, :half], both[:, half:]
     mine[...] = jnp.where(side[0] == 0, low, high)
     theirs[...] = jnp.where(side[0] == 0, high, low)
@@ -206,91 +256,106 @@
     value_ref[...] = jnp.sum(pairs_ref[:, hd:].astype(jnp.float32), axis=0, keepdims=True)
 
 
-def turned(own_ref, other_ref, scratch):
-    half = own_ref.shape[0]
-    scratch[:, :half] = own_ref[...].T
-    scratch[:, half:] = other_ref[...].T
-
-
-def weight_kernel(meta, *refs):
-    lefts, own_ref, other_ref = refs[:8], refs[8], refs[9]
-    send_ref, keep_ref, scratch = refs[10:]
+def weight_kernel(counts, meta, *refs):
+    terms, at = [], 0
+    for count in counts:
+        terms.append((refs[at : at + 8], refs[at + 8 : at + 8 + count]))
+        at += 8 + count
+    outs, token, scratch = refs[at : -len(counts) - 1], refs[-len(counts) - 1], refs[-len(counts) :]
+    token[...] = jnp.zeros_like(token)
 
     @pl.when((pl.program_id(0) == 0) & (pl.program_id(1) == 0))
     def _():
-        turned(own_ref, other_ref, scratch)
-
-    rows = jnp.concatenate([ref[...] for ref in lefts], axis=0)
-    part = dot(scratch[...], rows).astype(jnp.bfloat16)
-
-    @pl.when(pl.program_id(1) == 0)
-    def _():
-        send_ref[0] = part
-
-    @pl.when(pl.program_id(1) == 1)
-    def _():
-        keep_ref[0] = part
-
-
-def weight_grads(blocks, lowest, own, piece, other):
-    count, columns = other.shape
-    size, dim = blocks[0].shape
+        for (_, columns), turned in zip(terms, scratch):
+            turn(columns, turned)
+
+    start = 0
+    for (rows, _), turned in zip(terms, scratch):
+        joined = jnp.concatenate([ref[...] for ref in rows], axis=0)
+        part = dot(turned[...], joined).astype(jnp.bfloat16)
+        stop = start + part.shape[0]
+        outs[0][0, start:stop] = part
+        start = stop
+
+
+def turn(refs, scratch):
+    at = 0
+    for ref in refs:
+        scratch[:, at : at + ref.shape[0]] = ref[...].T
+        at += ref.shape[0]
+
+
+def block_width(rows):
+    return (rows if isinstance(rows, jax.Array) else rows[0]).shape[1]
+
+
+def row_blocks(rows, size, tile, column):
+    if isinstance(rows, jax.Array):
+        return [pl.BlockSpec((size, tile), lambda *ids, j=j: (ids[-1][2 + j], column(*ids))) for j in range(8)]
+    return [pl.BlockSpec((size, tile), lambda *ids: (0, column(*ids)))] * 8
+
+
+def weight_grads(meta, *terms):
+    size, dim = terms[0][1][0].shape[0] * len(terms[0][1]) // 8, block_width(terms[0][0])
     parts = lax.axis_size("seq") // 2
     tile = dim // parts
-    block = pl.BlockSpec((size, tile), lambda m, s, meta: (0, 2 * m + (meta[0] + 1 - s) % 2))
-    half = struct((parts // 2, columns, tile), jnp.bfloat16)
+    column = lambda m, s, meta: 2 * m + s
+    specs, args, widths = [], [], []
+    for rows, columns in terms:
+        specs += row_blocks(rows, size, tile, column)
+        specs += [pl.BlockSpec(value.shape, lambda m, s, meta: (0, 0)) for value in columns]
+        args += [*([rows] * 8 if isinstance(rows, jax.Array) else rows), *columns]
+        widths.append(columns[0].shape[1])
+    out = (1, sum(widths), tile)
+    out_specs = [
+        pl.BlockSpec(out, lambda m, s, meta: (2 * m + s, 0, 0)),
+        pl.BlockSpec((8, 128), lambda m, s, meta: (0, 0)),
+    ]
+    outs = [struct((parts, *out[1:]), jnp.bfloat16), struct((8, 128), jnp.float32)]
     return pl.pallas_call(
-        weight_kernel,
+        functools.partial(weight_kernel, [len(columns) for _, columns in terms]),
         grid_spec=pltpu.PrefetchScalarGridSpec(
             num_scalar_prefetch=1,
             grid=(parts // 2, 2),
-            in_specs=[block] * 8
-            + [
-                pl.BlockSpec((count, columns), lambda m, s, meta: (0, piece)),
-                pl.BlockSpec((count, columns), lambda m, s, meta: (0, 0)),
-            ],
-            out_specs=[pl.BlockSpec((1, columns, tile), lambda m, s, meta: (m, 0, 0))] * 2,
-            scratch_shapes=[pltpu.VMEM((columns, 2 * count), jnp.bfloat16)],
+            in_specs=specs,
+            out_specs=out_specs,
+            scratch_shapes=[pltpu.VMEM((width, 8 * size), jnp.bfloat16) for width in widths],
         ),
-        out_shape=[half, half],
+        out_shape=outs,
         compiler_params=pltpu.CompilerParams(vmem_limit_bytes=VMEM_LIMIT),
         cost_estimate=LIGHT,
-    )(lowest, *blocks, own, other)
+    )(meta, *args)
 
 
 def slab_kernel(meta, *refs):
-    lefts, own_ref, other_ref, out_ref, scratch = refs[:8], *refs[8:]
-    turned(own_ref, other_ref, scratch)
-    rows = jnp.concatenate([ref[...] for ref in lefts], axis=0)
+    *columns, out_ref, scratch = refs[8:]
+    turn(columns, scratch)
+    rows = jnp.concatenate([ref[...] for ref in refs[:8]], axis=0)
     out_ref[...] = dot(scratch[...], rows).astype(jnp.bfloat16)
 
 
-def slab_grads(blocks, slab, own, other, parts):
-    count, columns = own.shape
-    size, dim = blocks[0].shape
-    tile = dim // parts
-    block = pl.BlockSpec((size, tile), lambda m, meta: (0, meta[0]))
-    fixed = pl.BlockSpec((count, columns), lambda m, meta: (0, 0))
+def slab_grads(meta, rows, columns, parts):
+    size = columns[0].shape[0] * len(columns) // 8
+    tile = block_width(rows) // parts
+    width = columns[0].shape[1]
     return pl.pallas_call(
         slab_kernel,
         grid_spec=pltpu.PrefetchScalarGridSpec(
             num_scalar_prefetch=1,
             grid=(1,),
-            in_specs=[block] * 8 + [fixed, fixed],
-            out_specs=pl.BlockSpec((columns, tile), lambda m, meta: (0, 0)),
-            scratch_shapes=[pltpu.VMEM((columns, 2 * count), jnp.bfloat16)],
+            in_specs=row_blocks(rows, size, tile, lambda m, meta: meta[1])
+            + [pl.BlockSpec(value.shape, lambda m, meta: (0, 0)) for value in columns],
+            out_specs=pl.BlockSpec((width, tile), lambda m, meta: (0, 0)),
+            scratch_shapes=[pltpu.VMEM((width, 8 * size), jnp.bfloat16)],
         ),
-        out_shape=struct((columns, tile), jnp.bfloat16),
+        out_shape=struct((width, tile), jnp.bfloat16),
         compiler_params=pltpu.CompilerParams(vmem_limit_bytes=VMEM_LIMIT),
         cost_estimate=LIGHT,
-    )(slab, *blocks, own, other)
-
-
-ANYWHERE = pl.BlockSpec(memory_space=pl.ANY)
-
-
-def mlp_kernel(tiles, aliased, meta, x0, x1, g0, g1, fc_ref, proj_ref, bias_ref, *refs):
-    (a0, a1, ak, l0, l1, lk, m0, m1, t0, t1, sum_ref, x_ref, g_ref, macc, tacc) = refs[aliased:]
+    )(meta, *([rows] * 8 if isinstance(rows, jax.Array) else rows), *columns)
+
+
+def mlp_kernel(tiles, meta, x0, x1, g0, g1, fc_ref, proj_ref, bias_ref, *refs):
+    a_send, a_keep, l_send, l_keep, m0, m1, t0, t1, sum_ref, x_ref, g_ref, macc, tacc = refs
     step = pl.program_id(0)
     size = x0.shape[0]
 
@@ -324,20 +389,15 @@
         macc[:, cut] += dot(activated, proj_ref[:, cut])
         tacc[:, cut] += dot_nt(low, fc_ref[cut, :])
 
-    @pl.when(step < tiles // 4)
-    def _():
-        a0[...] = activated
-        l0[...] = low
-
-    @pl.when((step >= tiles // 4) & (step < tiles // 2))
-    def _():
-        a1[...] = activated
-        l1[...] = low
+    @pl.when(step < tiles // 2)
+    def _():
+        a_send[...] = activated
+        l_send[...] = low
 
     @pl.when(step >= tiles // 2)
     def _():
-        ak[...] = activated
-        lk[...] = low
+        a_keep[...] = activated
+        l_keep[...] = low
 
     @pl.when(step == tiles - 1)
     def _():
@@ -349,22 +409,20 @@
         t1[...] = b[size:]
 
 
-def mlp(blocks, ups, side, first, w_fc, w_proj, b_fc, before=()):
+def mlp(blocks, ups, meta, w_fc, w_proj, b_fc):
     size, dim = blocks[0].shape
     hidden = w_fc.shape[1]
     tiles = 4
     width = hidden // tiles
-    tile = lambda n, meta: ((n // (tiles // 2)) ^ (1 - meta[0])) * (tiles // 2) + n % (tiles // 2)
-    within = lambda n, start, count: jnp.clip(n - start, 0, count - 1)
+    tile = lambda n, meta: ((n // (tiles // 2)) ^ (1 - meta[10])) * (tiles // 2) + n % (tiles // 2)
     fixed = pl.BlockSpec((size, dim), lambda n, meta: (0, 0))
-    columns = lambda start, count: pl.BlockSpec(
-        (2 * size, width), lambda n, meta: (first // 2, within(n, start, count))
-    )
-    spread = [columns(0, tiles // 4), columns(tiles // 4, tiles // 4), columns(tiles // 2, tiles // 2)] * 2
-    shapes = [struct((4 * size, hidden // 4), jnp.bfloat16)] * 2 + [struct((4 * size, hidden // 2), jnp.bfloat16)]
+    columns = lambda start: pl.BlockSpec(
+        (2 * size, width), lambda n, meta: (0, jnp.clip(n - start, 0, tiles // 2 - 1))
+    )
+    half = struct((2 * size, hidden // 2), jnp.bfloat16)
     rows = struct((size, dim), jnp.bfloat16)
     return pl.pallas_call(
-        functools.partial(mlp_kernel, tiles, len(before)),
+        functools.partial(mlp_kernel, tiles),
         grid_spec=pltpu.PrefetchScalarGridSpec(
             num_scalar_prefetch=1,
             grid=(tiles,),
@@ -373,16 +431,16 @@
                 pl.BlockSpec((dim, width), lambda n, meta: (0, tile(n, meta))),
                 pl.BlockSpec((width, dim), lambda n, meta: (tile(n, meta), 0)),
                 pl.BlockSpec((1, width), lambda n, meta: (0, tile(n, meta))),
-            ]
-            + [ANYWHERE] * len(before),
-            out_specs=spread + [fixed] * 4 + [pl.BlockSpec((1, width), lambda n, meta: (0, tile(n, meta)))],
+            ],
+            out_specs=[columns(0), columns(tiles // 2)] * 2
+            + [fixed] * 4
+            + [pl.BlockSpec((1, width), lambda n, meta: (0, tile(n, meta)))],
             scratch_shapes=[pltpu.VMEM((2 * size, dim), jnp.bfloat16)] * 2 + [pltpu.VMEM((2 * size, dim), jnp.float32)] * 2,
         ),
-        out_shape=shapes * 2 + [rows] * 4 + [struct((1, hidden), jnp.float32)],
-        input_output_aliases={8 + j: j for j in range(len(before))},
+        out_shape=[half] * 4 + [rows] * 4 + [struct((1, hidden), jnp.float32)],
         compiler_params=pltpu.CompilerParams(vmem_limit_bytes=VMEM_LIMIT),
         cost_estimate=LIGHT,
-    )(side, *blocks, *ups, w_fc, w_proj, b_fc[None, :], *before)
+    )(meta, *blocks, *ups, w_fc, w_proj, b_fc[None, :])
 
 
 def allowed_pairs(slot, masks_ref, rows_ref, keys_ref):
@@ -637,7 +695,9 @@
     meta = jnp.stack([live, clear, key_first - group_first]).astype(jnp.int32)
     side = seq_index % 2
     scalar = lambda value: jnp.stack([value]).astype(jnp.int32)
-    lowest, slab, side_scalar = scalar((seq_index // 2) % 2), scalar(2 * tp_index + side), scalar(side)
+    side_scalar = scalar(side)
+    places = [scalar((seq_index // 2) % 2), scalar(2 * tp_index + side)]
+    places = jnp.concatenate(places + [side * tp_count + order, (1 - side) * tp_count + order, scalar(side)])
     beside = lambda value: swap(value, "seq", 1)
 
     row = lambda vector: vector[None, :]
@@ -660,8 +720,8 @@
     )
     key_across = tie(swap(key_stack, "tp", 2), queries)
     keys = [key_stack, swap(key_stack, "tp", 1), key_across, swap(key_across, "tp", 1)]
-    up_other, one_other = beside(grad_out), beside(normed_one)
     ups_own = gather_rows(tie(grad_out, queries))
+    up_other, one_other = beside(tie(grad_out, queries)), beside(tie(normed_one, queries))
     attended, norm = attention_forward(queries, keys, values, meta, rows_info, keys_info, heads)
 
     def project(value, weight, form):
@@ -680,22 +740,24 @@
 
     two_beside, two_across = swap(normed_two, "tp", 1), swap(normed_two, "tp", 2)
     two_other = beside(normed_two)
-    *kept, mlp0, mlp1, two0, two1, sum_near = mlp(
-        (normed_two, two_beside), ups_own[:2], side_scalar, 0, w_fc, w_proj, b_fc
+    act_send0, act_keep0, low_send0, low_keep0, mlp0, mlp1, two0, two1, sum_near = mlp(
+        (normed_two, tie(two_beside, up_other, one_other)), ups_own[:2], places, w_fc, w_proj, b_fc
     )
     two_across = tie(two_across, two0)
     two_opposite = swap(two_across, "tp", 1)
-    *kept, mlp2, mlp3, two2, two3, sum_far = mlp(
-        (two_across, two_opposite), ups_own[2:], side_scalar, 2, w_fc, w_proj, b_fc, kept
-    )
-    act_send0, act_send1, act_keep, low_send0, low_send1, low_keep = kept
+    ups_other = half_gather(tie(up_other, two0))
+    act_other0 = beside(act_send0)
+    act_send1, act_keep1, low_send1, low_keep1, mlp2, mlp3, two2, two3, sum_far = mlp(
+        (two_across, two_opposite), ups_own[2:], places, w_fc, w_proj, b_fc
+    )
 
     line = list(line_bits())
     line_side = lambda bit: (seq_index // bit) % 2
 
-    def start_sum(blocks, keep, piece, other):
-        send, kept = weight_grads(blocks, lowest, keep, piece, other)
-        return kept, swap(send, "seq", line[0]), line[1:]
+    def group_sum(parts):
+        groups = [list(range(first, seq_count, 2)) for first in range(2)]
+        flat = parts.reshape(-1, parts.shape[2])
+        return lax.psum_scatter(flat, "seq", scatter_dimension=0, tiled=True, axis_index_groups=groups)
 
     def step_sum(state, *deps):
         keep, got, bits = state
@@ -705,104 +767,158 @@
         send, kept = split_add(line_side(bits[0]), keep, got)
         return kept, swap(send, "seq", bits[0]), bits[1:]
 
-    def finish_sum(state, *deps):
-        while state[2]:
-            state = step_sum(state)
-        keep, got = tie(state[0][0], *deps), state[1][0]
-        half = keep.shape[1] // 2
+    def halves(*parts):
+        rows, columns = parts[0].shape
         return pl.pallas_call(
             halves_kernel,
-            in_specs=[pl.BlockSpec(memory_space=pltpu.SMEM), pl.BlockSpec(keep.shape), pl.BlockSpec(keep.shape)],
-            out_shape=[struct((keep.shape[0], half), jnp.bfloat16)] * 2,
+            in_specs=[pl.BlockSpec(memory_space=pltpu.SMEM)] + [pl.BlockSpec((rows, columns))] * len(parts),
+            out_shape=[struct((rows, columns // 2), jnp.bfloat16)] * 2,
             compiler_params=pltpu.CompilerParams(vmem_limit_bytes=VMEM_LIMIT),
             cost_estimate=LIGHT,
-        )(side_scalar, keep, got)
-
-    def exchange(*halves):
-        mine, theirs = joined(*[half[0] for half in halves]), beside(joined(*[half[1] for half in halves]))
-        low_first = jnp.where(side == 0, mine, theirs)
-        high = jnp.where(side == 0, theirs, mine)
-        return joined(low_first, high).astype(jnp.float32)
-
-    act_other0 = beside(act_send0)
-    two_sum0, two_sum1, two_over, two_sum2 = scatter(two0, two1, two2, two3)
-    ups = ups_own + gather_other(up_other, two0, two_over)
-    sum_p0 = start_sum(ups, tie(act_keep, two_over), 0, act_other0)
-    act_other1 = beside(tie(act_send1, sum_p0[0]))
-    middle_grads, middle_low, sums_two = call(
-        middle_back_kernel,
-        [rows_wide, rows_low, struct((4, dim), jnp.float32)],
-        middle, tie(two_sum0, sum_p0[0]), two_sum1, two_sum2, grad_out, row(ln2_gain),
-    )
-    mid_beside, mid_across = swap(middle_low, "tp", 1), swap(middle_low, "tp", 2)
-    sum_p1 = start_sum(ups, tie(act_keep, middle_low), 1, act_other1)
-    low_other0 = beside(tie(low_send0, sum_p1[0]))
-
-    mid_across = tie(mid_across, sum_p1[0])
-    mid_opposite = swap(mid_across, "tp", 1)
+        )(side_scalar, *parts)
+
+    def exchange(mine, theirs):
+        both = [jnp.where(side == 0, mine, theirs), jnp.where(side == 0, theirs, mine)]
+        return joined(*both).astype(jnp.float32)
+
+    act_other1 = beside(act_send1)
+
+    clock = [two2]
+
+    def at(value, *arrived):
+        return tie(value, clock[0], *arrived)
+
+    def mark(results):
+        clock[0] = results[0] if isinstance(results, (list, tuple)) else results
+        return results
+
+    core = lambda value: swap(value, "tp", 1)
+    chip = lambda value: swap(value, "tp", 2)
+
+    two_over = mark(add_low(at(two2, act_other0, two_other, ups_other[2]), core(two3)))
+    two_own, two_got = core(two1), chip(two_over)
+    middle_grads, middle_low, sums_two = mark(
+        call(
+            middle_back_kernel,
+            [rows_wide, rows_low, struct((4, dim), jnp.float32)],
+            middle, two0, two_own, two_got, grad_out, at(row(ln2_gain)),
+        )
+    )
+    mid_beside, mid_across = core(middle_low), chip(middle_low)
+    low_other0, low_other1 = beside(at(low_send0)), beside(at(low_send1))
+    ups = ups_own + full_gather(ups_other, middle_low)
+    part_p, clock[0] = weight_grads(places, (ups, (at(act_keep0), act_keep1, act_other0, act_other1)))
+    mid_opposite = core(at(mid_across))
     mids_own = (middle_low, mid_beside, mid_across, mid_opposite)
-    attended_grads = call(
-        attended_grads_kernel, struct(attended.shape, jnp.bfloat16), *mids_own, w_out
-    )
-    mlp_sum0, mlp_sum1, _, mlp_sum2 = scatter(mlp0, mlp1, mlp2, mlp3, attended_grads)
-    sum_p0 = step_sum(sum_p0, attended_grads)
-    att_keep, att_send = column_halves(attended)
-
-    back = backward_calls(queries, keys, values, meta, rows_info, keys_info, norm, attended, attended_grads, heads)
-    start, delta, *kv_far = back[0](sum_p0[0])
-    low_other1 = beside(tie(low_send1, start))
-    mid_other = beside(tie(middle_low, start))
-    far0, far1, far_over, far2 = scatter(*kv_far, start)
-    twos = (normed_two, two_beside, two_across, two_opposite) + gather_other(two_other, attended_grads, start)
-    sum_f0 = start_sum(twos, tie(low_keep, far_over), 0, low_other0)
-    sum_p1 = step_sum(sum_p1, sum_f0[0])
-    query_low, bias_query, *kv_near = back[1](start, delta, sum_p1[0])
-
-    one = project(query_low, w_query, dot_nt)
-    dq_keep, dq_send = column_halves(query_low)
-    dq_other = beside(dq_send)
-    att_other = beside(tie(att_send, query_low))
-    near0, near1, near_over, near2 = scatter(*kv_near, one[0])
-    one0, one1, one_over, one2 = scatter(*one, near_over)
-    far_sum = add_low(tie(far0, one_over), far1, far2)
+
+    attended_grads = mark(
+        call(attended_grads_kernel, struct(attended.shape, jnp.bfloat16), *mids_own, at(w_out))
+    )
+    sum_p = group_sum(touch(part_p, mid_across))
+    twos_other = half_gather(at(two_other))
+    ones_other = half_gather(at(one_other))
+    first_call, last_call = backward_calls(
+        queries, keys, values, meta, rows_info, keys_info, norm, attended, attended_grads, heads
+    )
+    start, delta, *kv_far = mark(first_call(attended_grads))
+    mid_other = beside(at(middle_low))
+    far_over = mark(add_low(at(kv_far[2], low_other0, low_other1, twos_other[2]), core(kv_far[3])))
+    twos = (normed_two, two_beside, two_across, two_opposite) + full_gather(twos_other, far_over)
+    far_own, far_got = core(kv_far[1]), chip(far_over)
+    query_low, bias_query, *kv_near = mark(last_call(start, delta, far_over))
+
+    one2, one3 = mark(
+        call(
+            functools.partial(project_kernel, 2, dot_nt), [rows_low] * 2,
+            at(query_low, far_got, far_own, mid_other, ones_other[2]), w_query,
+        )
+    )
+    ones = blocks_one + full_gather(ones_other, one2)
+    near_over = mark(add_low(at(kv_near[2]), core(kv_near[3])))
+    mid_others = mid_other, core(at(mid_other)), chip(at(mid_other))
+    near_own, near_got = core(kv_near[1]), chip(near_over)
+    far_sum = mark(add_low(at(kv_far[0]), far_own, far_got))
     far_there = swap(far_sum, "seq", seq_count // 2)
-    sum_f1 = start_sum(twos, tie(low_keep, far_sum), 1, low_other1)
-    done_p0 = finish_sum(sum_p0, sum_f1[0])
-    kv_slots = add_low(tie(near0, done_p0[0]), near1, near2, far_there)
-    sum_f0 = step_sum(sum_f0, kv_slots)
-    ones = blocks_one + gather_other(one_other, start, kv_slots)
-    sum_q = start_sum(ones, tie(dq_keep, sum_f0[0]), 0, dq_other)
-    for bit in seq_bits[-2::-1]:
-        kv_slots = add_low(tie(kv_slots[:bit], sum_q[0]), swap(kv_slots[bit:], "seq", bit))
-    kv_low = kv_slots[0]
-    kv_group = joined(*gather_rows(kv_low))
-    kv_beside = beside(kv_group)
-    grad_in, sums_one, sums_value = call(
-        last_kernel,
-        [rows_wide, struct((2, dim), jnp.float32), struct((1, head_dim), jnp.float32)],
-        hidden_in, one0, one1, one2, kv_low, w_kv, middle_grads, row(ln1_gain),
-    )
-    mids = mids_own + gather_other(mid_other, far_sum, sums_value)
-    sum_o = start_sum(mids, tie(att_keep, sums_value), 0, att_other)
-    done_p1 = finish_sum(sum_p1, sum_o[0])
-    sum_f1 = step_sum(sum_f1, done_p1[0])
-    layer_out = call(layer_kernel, rows_low, tie(middle, sum_f1[0]), mlp_sum0, mlp_sum1, mlp_sum2, row(b_proj))
-
-    vectors = [sums_two.reshape(-1), sums_one.reshape(-1), sums_value[0]]
-    split = [bias_query[0], (sum_near + sum_far)[0]]
-    vectors = jnp.concatenate(vectors + split).reshape(-1, 128)
-    vectors = sum_over(vectors, "seq").reshape(-1)
+    one_over = mark(add_low(at(one2), core(one3)))
+    one_got = chip(one_over)
+    part = struct((group_rows, heads * head_dim // 2), jnp.bfloat16)
+    dq_keep, att_keep, sends = mark(
+        pl.pallas_call(
+            columns_kernel,
+            in_specs=[pl.BlockSpec(memory_space=pltpu.SMEM)] + [pl.BlockSpec(query_low.shape)] * 2,
+            out_shape=[part, part, struct(query_low.shape, jnp.bfloat16)],
+            compiler_params=pltpu.CompilerParams(vmem_limit_bytes=VMEM_LIMIT),
+            cost_estimate=LIGHT,
+        )(side_scalar, at(query_low), attended)
+    )
+    others = beside(sends)
+    part_f, clock[0] = weight_grads(places, (twos, (at(low_keep0), low_keep1, low_other0, low_other1)))
+    kv_slots, there = mark(add_split(at(kv_near[0], others, mid_others[2]), near_own, near_got, far_there))
+    sum_f = group_sum(touch(part_f, far_there))
+    there = swap(there, "seq", seq_bits[-2])
+    mid_others = (*mid_others, core(at(mid_others[2])))
+    one0, one1 = mark(
+        call(functools.partial(project_kernel, 0, dot_nt), [rows_low] * 2, at(query_low), w_query)
+    )
+    one_own = core(one1)
+    width = dq_keep.shape[1]
+    part_qo, clock[0] = weight_grads(
+        places,
+        (ones, (at(dq_keep), others[:, :width])),
+        (mids_own + mid_others, (att_keep, others[:, width:])),
+    )
+    for bit in seq_bits[-3::-1]:
+        kv_slots, send = mark(add_split(at(kv_slots), there))
+        there = swap(send, "seq", bit)
+    kv_low = mark(add_low(at(kv_slots, one_got), there))[0]
+    kv_beside, kv_across = core(kv_low), chip(kv_low)
+    sum_qo = group_sum(touch(part_qo, kv_low))
+    grad_in, sums_one, sums_value = mark(
+        call(
+            last_kernel,
+            [rows_wide, struct((2, dim), jnp.float32), struct((1, head_dim), jnp.float32)],
+            hidden_in, one0, one_own, one_got, kv_low, w_kv, middle_grads, at(row(ln1_gain)),
+        )
+    )
+
     count = 6 * dim + head_dim
-    shared = sum_over(vectors[:count].reshape(-1, 128), "tp").reshape(-1)
-    split = vectors[count:]
-    queries_width = bias_query.shape[1]
-
-    part_kv = slab_grads(ones, slab, tie(kv_group, sum_f1[0]), kv_beside, 2 * tp_count)
-    for bit in seq_bits[1:]:
-        part_kv = add_low(part_kv, swap(part_kv, "seq", bit))
-    got = beside(part_kv)
-    half_kv = jnp.where(side == 0, jnp.stack([part_kv, got]), jnp.stack([got, part_kv]))
-    quarters = gather_rows(half_kv)
+    vectors = [sums_two.reshape(-1), sums_one.reshape(-1), sums_value[0], bias_query[0], (sum_near + sum_far)[0]]
+    vectors = jnp.concatenate(vectors).reshape(-1, 128)
+    got = swap(vectors, "seq", seq_bits[1])
+    kv_group = joined(kv_low, kv_beside, kv_across, core(at(kv_across)))
+    kv_other = beside(kv_group)
+    mine_p, theirs_p = mark(halves(at(sum_p)))
+    theirs_p = beside(theirs_p)
+    mlp_over = mark(add_low(at(mlp2), core(at(mlp3))))
+    mlp_own, mlp_got = core(at(mlp1)), chip(mlp_over)
+    vectors = vectors + at(got)
+    got = swap(vectors, "seq", seq_bits[2])
+    part_kv = mark(slab_grads(places, ones, (at(kv_group), kv_other), 2 * tp_count))
+    got_kv = swap(part_kv, "seq", seq_bits[1])
+    vectors = vectors + at(got)
+    for bit in seq_bits[2:]:
+        part_kv = mark(add_low(at(part_kv), got_kv))
+        got_kv = swap(part_kv, "seq", bit)
+    for bit in seq_bits[3:]:
+        vectors = vectors + swap(vectors, "seq", bit)
+    got = swap(vectors, "seq", 1)
+    part_kv = mark(add_low(at(part_kv), got_kv))
+    got_kv = beside(part_kv)
+    layer_out = mark(call(layer_kernel, rows_low, at(middle), mlp0, mlp_own, mlp_got, row(b_proj)))
+    vectors = (vectors + at(got)).reshape(-1)
+    shared, split = vectors[:count].reshape(-1, 128), vectors[count:]
+    got = chip(shared)
+    grad_proj = exchange(at(mine_p), theirs_p)
+    half_kv = jnp.where(side == 0, jnp.stack([part_kv, got_kv]), jnp.stack([got_kv, part_kv]))
+    half_beside, half_across = core(half_kv), chip(half_kv)
+    mine_f, theirs_f = mark(halves(tie(sum_f, half_kv)))
+    theirs_f = beside(theirs_f)
+    shared = shared + at(got)
+    got = core(shared)
+    half_opposite = core(at(half_across))
+    shared = (shared + at(got)).reshape(-1)
+    grad_fc = exchange(at(mine_f), theirs_f).T
+    quarters = half_kv, half_beside, half_across, half_opposite
     grad_kv = jnp.concatenate(
         [
             jnp.where(tp_index == j, quarters[0], jnp.where(tp_index == j ^ 1, quarters[1], jnp.where(tp_index == j ^ 2, quarters[2], quarters[3])))
@@ -810,17 +926,11 @@
         ]
     )
     grad_kv = jnp.swapaxes(grad_kv.astype(jnp.float32), 1, 2).reshape(dim, 2 * head_dim)
-
-    grad_proj = exchange(done_p0, done_p1)
-    sum_q = step_sum(sum_q, part_kv)
-    sum_o = step_sum(sum_o, sum_q[0])
-    done_f0 = finish_sum(sum_f0, sum_o[0])
-    done_f1 = finish_sum(sum_f1, done_f0[0])
-    done_q = finish_sum(sum_q, done_f1[0])
-    done_o = finish_sum(sum_o, done_q[0])
-    grad_fc = exchange(done_f0, done_f1).T
-    grad_query = exchange(done_q).T
-    grad_out_weight = exchange(done_o)
+    mine_qo, theirs_qo = mark(halves(tie(sum_qo, grad_fc, grad_kv, shared)))
+    theirs_qo = beside(theirs_qo)
+    grad_query = exchange(mine_qo[:width], theirs_qo[:width]).T
+    grad_out_weight = exchange(mine_qo[width:], theirs_qo[width:])
+    queries_width = bias_query.shape[1]
     return (
         layer_out,
         grad_in,

time: 506 us -> 448 us (0.89)
  the two profiles are of different devices: /device:TPU:0 before, /device:TPU:26 now
where the time goes in v2:
time: 448 us; the launch traced here: 440 us
  Pallas kernels  190 us (42%)
  waiting for transfers between devices  135 us (30%)
  starting transfers between devices  50.8 us (11%)
  local copies, waits for them, and re-layouts  36.8 us (8%)
  between operations  15 us (3%)
  other arithmetic  12 us (3%)
    ppermute x83, waiting for transfers between devices, swap(): return lax.ppermute(value, axis, [(j, j ^ bit) for j in range(count)])  135 us
    pallas_call x23, Pallas kernels, call(): pl.pallas_call(kernel, out_shape=outs, compiler_params=pltpu.CompilerPara...  62.6 us
    pallas_call x3, Pallas kernels, attention_call(): pl.pallas_call(kernel, grid_spec=pltpu.PrefetchScalarGridSpec(num_scalar_...  53.3 us
    ppermute x83, starting transfers between devices, swap(): return lax.ppermute(value, axis, [(j, j ^ bit) for j in range(count)])  50.7 us
    pallas_call x2, Pallas kernels, mlp(): pl.pallas_call(functools.partial(mlp_kernel, tiles), grid_spec=pltpu.Pref...  35 us
    pallas_call x3, Pallas kernels, weight_grads(): pl.pallas_call(functools.partial(weight_kernel, [len(columns) for _, colu...  27.8 us
    unnamed x165, local copies, waits for them, and re-layouts  27.5 us
  transfers between devices with their start and end apart: 86, of which 27 were waited for; matrix products, arithmetic and copies ran while one was open for 6% of the time, Pallas kernels for 37%

profile of v2, /device:TPU:26, one launch (start us, length us, event | category | flops | bytes accessed | tf_op | source)
XLA Modules:
  0.0 440.2 jit_solution(14021945260055114736)
XLA Ops:
  16.6 7.8 %collective-permute-done.9 = bf16[128,128]{1,0:T(8,128)(2,1)S(1)} collective-permute-done((bf16[128,128]{1,0:T(8,128)(2,1)}, bf16[128,128]{1,0:T(8,128)(2,1)S(1)}, u32[]{:S(2)}, u32[]{:S(2)}) %collective-permute-start.9) | collective-permute-done | bytes 32800 | tf_op jit(solution)/shard_map/ppermute | solution.py:37
  27.5 3.6 collective-permute-done.10
  32.9 3.2 collective-permute-done.11
  46.5 4.3 shard_map.289.q_ref
  53.9 20.0 %shard_map.290 = (bf16[512,512]{1,0:T(8,128)(2,1)}, f32[4,512]{1,0:T(4,128)}) custom-call(s32[3,8]{1,0:T(4,128)} %pad_add_fusion.1.meta, bf16[512,512]{1,0:T(8,128)(2,1)} %shard_map.289.q_ref, bf16[8,128,128]{2,1,0:T(8,128)(2,1)} %copy-done.5, bf16[8,128,128]{2,1,0:T(8,128)(2,1)} %copy-done.7, bf16[8,128,128]{2,1,0:T(8,128)(2,1)} %copy-done.6, ...), custom_call_target="tpu_custom_call" | custom-call | flops 1024 | bytes 1024 | tf_op jit(solution)/shard_map/pallas_call | solution.py:600
  73.9 3.5 shard_map.291
  77.4 3.5 shard_map.292
  88.4 10.9 %collective-permute-done.16.p2 = bf16[128,2048]{1,0:T(8,128)(2,1)S(1)} collective-permute-done((bf16[128,2048]{1,0:T(8,128)(2,1)}, bf16[128,2048]{1,0:T(8,128)(2,1)S(1)}, u32[]{:S(2)}, u32[]{:S(2)}) %collective-permute-start.16) | collective-permute-done | bytes 524320 | tf_op jit(solution)/shard_map/ppermute | solution.py:37
  100.1 3.0 shard_map.294
  105.8 4.8 %collective-permute-done.24.g0.refs_2_ = bf16[128,2048]{1,0:T(8,128)(2,1)S(1)} collective-permute-done((bf16[128,2048]{1,0:T(8,128)(2,1)S(1)}, bf16[128,2048]{1,0:T(8,128)(2,1)S(1)}, u32[]{:S(2)}, u32[]{:S(2)}) %collective-permute-start.24) | collective-permute-done | bytes 524320 | tf_op jit(solution)/shard_map/ppermute | solution.py:37
  111.6 17.6 %shard_map.295 = (bf16[256,1024]{1,0:T(8,128)(2,1)}, bf16[256,1024]{1,0:T(8,128)(2,1)}, bf16[256,1024]{1,0:T(8,128)(2,1)}, bf16[256,1024]{1,0:T(8,128)(2,1)}, bf...) custom-call(s32[11]{0:T(128)} %concatenate.28.meta, ...), custom_call_target="tpu_custom_call" | custom-call | flops 1024 | bytes 1024 | tf_op jit(solution)/shard_map/pallas_call | solution.py:424
  134.7 17.3 %shard_map.296 = (bf16[256,1024]{1,0:T(8,128)(2,1)}, bf16[256,1024]{1,0:T(8,128)(2,1)}, bf16[256,1024]{1,0:T(8,128)(2,1)}, bf16[256,1024]{1,0:T(8,128)(2,1)}, bf...) custom-call(s32[11]{0:T(128)} %concatenate.28.meta, ...), custom_call_target="tpu_custom_call" | custom-call | flops 1024 | bytes 1024 | tf_op jit(solution)/shard_map/pallas_call | solution.py:424
  159.6 11.8 %collective-permute-done.30.p2 = bf16[128,2048]{1,0:T(8,128)(2,1)S(1)} collective-permute-done((bf16[128,2048]{1,0:T(8,128)(2,1)}, bf16[128,2048]{1,0:T(8,128)(2,1)S(1)}, u32[]{:S(2)}, u32[]{:S(2)}) %collective-permute-start.30) | collective-permute-done | bytes 524320 | tf_op jit(solution)/shard_map/ppermute | solution.py:37
  172.2 4.1 shard_map.298
  179.2 9.9 %shard_map.299 = (bf16[4,1024,512]{2,1,0:T(8,128)(2,1)}, f32[8,128]{1,0:T(8,128)}) custom-call(s32[11]{0:T(128)} %concatenate.28.meta, bf16[128,2048]{1,0:T(8,128)(2,1)} %refs_0_, bf16[128,2048]{1,0:T(8,128)(2,1)} %collective-permute-done.20.g1.refs_1_, bf16[128,2048]{1,0:T(8,128)(2,1)} %copy-done.20, bf16[128,2048]{1,0:T(8,128)(2,1)} %copy-done.23, ...), custom_call_target="tpu_custom_call" | custom-call | flops 1024 | bytes 1024 | tf_op jit(solution)/shard_map/pallas_call | solution.py:315
  196.3 4.8 %shard_map.300.refs_11_ = bf16[512,512]{1,0:T(8,128)(2,1)} custom-call(bf16[128,2048]{1,0:T(8,128)(2,1)} %get-tuple-element.192.r0.refs_10_, bf16[128,2048]{1,0:T(8,128)(2,1)} %copy-done.17, bf16[128,2048]{1,0:T(8,128)(2,1)} %copy-done.16, bf16[128,2048]{1,0:T(8,128)(2,1)} %copy-done.18, bf16[512,2048]{1,0:T(8,128)(2,1)} %w_ref.11), custom_call_target="tpu_custom_call" | custom-call | flops 1024 | bytes 1024 | tf_op jit(solution)/shard_map/pallas_call | solution.py:80
  202.0 16.6 %shard_map.301 = (f32[4,128,512]{2,1,0:T(8,128)}, f32[4,512]{1,0:T(4,128)}, bf16[4,128,256]{2,1,0:T(8,128)(2,1)}, bf16[4,128,256]{2,1,0:T(8,128)(2,1)}, bf16[4,1...) custom-call(s32[3,8]{1,0:T(4,128)} %pad_add_fusion.1.meta, bf16[512,512]{1,0:T(8,128)(2,1)} %shard_map.289.q_ref, ...), custom_call_target="tpu_custom_call" | custom-call | flops 1024 | bytes 1024 | tf_op jit(solution)/shard_map/pallas_call | solution.py:600
  224.1 16.7 %shard_map.303 = (bf16[512,512]{1,0:T(8,128)(2,1)}, f32[1,512]{1,0:T(1,128)}, bf16[4,128,256]{2,1,0:T(8,128)(2,1)}, bf16[4,128,256]{2,1,0:T(8,128)(2,1)}, bf16[4...) custom-call(s32[3,8]{1,0:T(4,128)} %pad_add_fusion.1.meta, bf16[512,512]{1,0:T(8,128)(2,1)} %shard_map.289.q_ref, ...), custom_call_target="tpu_custom_call" | custom-call | flops 1024 | bytes 1024 | tf_op jit(solution)/shard_map/pallas_call | solution.py:600
  240.9 3.9 shard_map.304
  257.9 9.9 %shard_map.321 = (bf16[4,1024,512]{2,1,0:T(8,128)(2,1)}, f32[8,128]{1,0:T(8,128)}) custom-call(s32[11]{0:T(128)} %concatenate.28.meta, bf16[128,2048]{1,0:T(8,128)(2,1)} %get-tuple-element.154.x0.refs_0_, bf16[128,2048]{1,0:T(8,128)(2,1)} %copy-done.11, bf16[128,2048]{1,0:T(8,128)(2,1)} %copy-done.12, bf16[128,2048]{1,0:T(8,128)(2,1)} %copy-done.19, ...), custom_call_target="tpu_custom_call" | custom-call | flops 1024 | bytes 1024 | tf_op jit(solution)/shard_map/pallas_call | solution.py:315
  267.7 9.6 %collective-permute-done.53.refs_3_ = bf16[4,128,256]{2,1,0:T(8,128)(2,1)S(1)} collective-permute-done((bf16[4,128,256]{2,1,0:T(8,128)(2,1)}, bf16[4,128,256]{2,1,0:T(8,128)(2,1)S(1)}, u32[]{:S(2)}, u32[]{:S(2)}) %collective-permute-start.53) | collective-permute-done | bytes 262176 | tf_op jit(solution)/shard_map/ppermute | solution.py:37
  282.2 10.8 %collective-permute-done.50.refs_16_ = bf16[128,2048]{1,0:T(8,128)(2,1)S(1)} collective-permute-done((bf16[128,2048]{1,0:T(8,128)(2,1)S(1)}, bf16[128,2048]{1,0:T(8,128)(2,1)S(1)}, u32[]{:S(2)}, u32[]{:S(2)}) %collective-permute-start.50) | collective-permute-done | bytes 524320 | tf_op jit(solution)/shard_map/ppermute | solution.py:37
  293.3 5.3 %collective-permute-done.52.refs_2_ = bf16[4,128,256]{2,1,0:T(8,128)(2,1)S(1)} collective-permute-done((bf16[4,128,256]{2,1,0:T(8,128)(2,1)S(1)}, bf16[4,128,256]{2,1,0:T(8,128)(2,1)S(1)}, u32[]{:S(2)}, u32[]{:S(2)}) %collective-permute-start.52) | collective-permute-done | bytes 262176 | tf_op jit(solution)/shard_map/ppermute | solution.py:37
  301.9 12.5 %collective-permute-done.54.refs_1_ = bf16[2,128,256]{2,1,0:T(8,128)(2,1)S(1)} collective-permute-done((bf16[2,128,256]{2,1,0:T(8,128)(2,1)}, bf16[2,128,256]{2,1,0:T(8,128)(2,1)S(1)}, u32[]{:S(2)}, u32[]{:S(2)}) %collective-permute-start.54) | collective-permute-done | bytes 131104 | tf_op jit(solution)/shard_map/ppermute | solution.py:37
  318.9 3.5 shard_map.312
  325.6 8.1 %shard_map.324 = (bf16[4,512,512]{2,1,0:T(8,128)(2,1)}, f32[8,128]{1,0:T(8,128)}) custom-call(s32[11]{0:T(128)} %concatenate.28.meta, bf16[128,2048]{1,0:T(8,128)(2,1)} %get-tuple-element.153.r0.refs_0_, bf16[128,2048]{1,0:T(8,128)(2,1)} %copy-done.2, bf16[128,2048]{1,0:T(8,128)(2,1)} %copy-done.1, bf16[128,2048]{1,0:T(8,128)(2,1)} %copy-done.3, ...), custom_call_target="tpu_custom_call" | custom-call | flops 1024 | bytes 1024 | tf_op jit(solution)/shard_map/pallas_call | solution.py:315
  337.6 4.2 shard_map.313
  350.5 3.5 collective-permute-done.62.refs_9_
  370.7 16.0 %collective-permute-done.68 = f32[117,128]{1,0:T(8,128)S(1)} collective-permute-done((f32[117,128]{1,0:T(8,128)S(1)}, f32[117,128]{1,0:T(8,128)S(1)}, u32[]{:S(2)}, u32[]{:S(2)}) %collective-permute-start.68) | collective-permute-done | bytes 59936 | tf_op jit(solution)/shard_map/ppermute | solution.py:37
  391.1 4.0 collective-permute-done.73
  410.5 10.5 %collective-permute-done.77 = bf16[1024,256]{1,0:T(8,128)(2,1)S(1)} collective-permute-done((bf16[1024,256]{1,0:T(8,128)(2,1)}, bf16[1024,256]{1,0:T(8,128)(2,1)S(1)}, u32[]{:S(2)}, u32[]{:S(2)}) %collective-permute-start.77) | collective-permute-done | bytes 524320 | tf_op jit(solution)/shard_map/ppermute | solution.py:37
  426.6 4.7 %collective-permute-done.81 = bf16[512,256]{1,0:T(8,128)(2,1)S(1)} collective-permute-done((bf16[512,256]{1,0:T(8,128)(2,1)}, bf16[512,256]{1,0:T(8,128)(2,1)S(1)}, u32[]{:S(2)}, u32[]{:S(2)}) %collective-permute-start.81) | collective-permute-done | bytes 262176 | tf_op jit(solution)/shard_map/ppermute | solution.py:37
  (396 shorter events, 155.3 us)
Async XLA Ops:
  7.2 335.6 %reduce-scatter.4.cloned.1.call-start = ((), (), s32[]{:S(2)}) async-start(), calls=%async_computation.3 | async-start | bytes 5242880 | tf_op jit(solution)/shard_map/reduce_scatter | solution.py:760
  9.9 32.9 %collective-permute-start.1 = (bf16[128,2048]{1,0:T(8,128)(2,1)}, bf16[128,2048]{1,0:T(8,128)(2,1)S(1)}, u32[]{:S(2)}, u32[]{:S(2)}) collective-permute-start(bf16[128,2048]{1,0:T(8,128)(2,1)} %get-tuple-element.153.r0.refs_0_), channel_id=1, source_target_pairs={{0,2},{1,3},{2,0},{3,1},{4,6},{5,7},{6,4},{7,5},{8,10},{9,11},{10,... | collective-permute-start | bytes 1572872 | tf_op jit(solution)/shard_map/ppermute | solution.py:37
  11.4 34.1 %collective-permute-start = (bf16[128,2048]{1,0:T(8,128)(2,1)}, bf16[128,2048]{1,0:T(8,128)(2,1)S(1)}, u32[]{:S(2)}, u32[]{:S(2)}) collective-permute-start(bf16[128,2048]{1,0:T(8,128)(2,1)} %get-tuple-element.153.r0.refs_0_), channel_id=1, source_target_pairs={{0,1},{1,0},{2,3},{3,2},{4,5},{5,4},{6,7},{7,6},{8,9},{9,8},{10,11... | collective-permute-start | bytes 1572872 | tf_op jit(solution)/shard_map/ppermute | solution.py:37
  85.9 24.9 %collective-permute-start.19 = (bf16[128,2048]{1,0:T(8,128)(2,1)S(1)}, bf16[128,2048]{1,0:T(8,128)(2,1)}, u32[]{:S(2)}, u32[]{:S(2)}) collective-permute-start(bf16[128,2048]{1,0:T(8,128)(2,1)S(1)} %copy-done.4), channel_id=1, source_target_pairs={{0,4},{4,0},{8,12},{12,8},{16,20},{20,16},{24,28},{28,24},{1,5},{5... | collective-permute-start | bytes 1572872 | tf_op jit(solution)/shard_map/ppermute | solution.py:37
  87.9 22.7 %collective-permute-start.24 = (bf16[128,2048]{1,0:T(8,128)(2,1)S(1)}, bf16[128,2048]{1,0:T(8,128)(2,1)S(1)}, u32[]{:S(2)}, u32[]{:S(2)}) collective-permute-start(bf16[128,2048]{1,0:T(8,128)(2,1)S(1)} %copy-done.4), channel_id=1, source_target_pairs={{0,2},{1,3},{2,0},{3,1},{4,6},{5,7},{6,4},{7,5},{8,10},{9,11},{10,... | collective-permute-start | bytes 1572872 | tf_op jit(solution)/shard_map/ppermute | solution.py:37
  103.7 25.5 %collective-permute-start.22 = (bf16[128,2048]{1,0:T(8,128)(2,1)}, bf16[128,2048]{1,0:T(8,128)(2,1)S(1)}, u32[]{:S(2)}, u32[]{:S(2)}) collective-permute-start(bf16[128,2048]{1,0:T(8,128)(2,1)} %get-tuple-element.154.x0.refs_0_), channel_id=1, source_target_pairs={{0,2},{1,3},{2,0},{3,1},{4,6},{5,7},{6,4},{7,5},{8,10},{9,11},{10,... | collective-permute-start | bytes 1572872 | tf_op jit(solution)/shard_map/ppermute | solution.py:37
  110.6 22.6 %collective-permute-start.25 = (bf16[128,2048]{1,0:T(8,128)(2,1)S(1)}, bf16[128,2048]{1,0:T(8,128)(2,1)S(1)}, u32[]{:S(2)}, u32[]{:S(2)}) collective-permute-start(bf16[128,2048]{1,0:T(8,128)(2,1)S(1)} %collective-permute-done.24.g0.refs_2_), channel_id=1, source_target_pairs={{0,1},{1,0},{2,3},{3,2},{4,5},{5,4},{6,7},{7,6},{8,9},{9,8},{10,11... | collective-permute-start | bytes 1572872 | tf_op jit(solution)/shard_map/ppermute | solution.py:37
  129.6 23.1 %collective-permute-start.27 = (bf16[128,2048]{1,0:T(8,128)(2,1)S(1)}, bf16[128,2048]{1,0:T(8,128)(2,1)S(1)}, u32[]{:S(2)}, u32[]{:S(2)}) collective-permute-start(bf16[128,2048]{1,0:T(8,128)(2,1)S(1)} %copy-done.10), channel_id=1, source_target_pairs={{0,4},{4,0},{8,12},{12,8},{16,20},{20,16},{24,28},{28,24},{1,5},{5... | collective-permute-start | bytes 1572872 | tf_op jit(solution)/shard_map/ppermute | solution.py:37
  129.7 23.0 %collective-permute-start.28 = (bf16[128,2048]{1,0:T(8,128)(2,1)}, bf16[128,2048]{1,0:T(8,128)(2,1)}, u32[]{:S(2)}, u32[]{:S(2)}) collective-permute-start(bf16[128,2048]{1,0:T(8,128)(2,1)} %collective-permute-done.19.refs_4_), channel_id=1, source_target_pairs={{0,2},{1,3},{2,0},{3,1},{4,6},{5,7},{6,4},{7,5},{8,10},{9,11},{10,... | collective-permute-start | bytes 1572872 | tf_op jit(solution)/shard_map/ppermute | solution.py:37
  131.1 23.8 %collective-permute-start.26 = (bf16[256,1024]{1,0:T(8,128)(2,1)}, bf16[256,1024]{1,0:T(8,128)(2,1)}, u32[]{:S(2)}, u32[]{:S(2)}) collective-permute-start(bf16[256,1024]{1,0:T(8,128)(2,1)} %get-tuple-element.161), channel_id=1, source_target_pairs={{0,4},{4,0},{8,12},{12,8},{16,20},{20,16},{24,28},{28,24},{1,5},{5... | collective-permute-start | bytes 1572872 | tf_op jit(solution)/shard_map/ppermute | solution.py:37
  159.3 18.2 %collective-permute-start.33 = (bf16[128,2048]{1,0:T(8,128)(2,1)}, bf16[128,2048]{1,0:T(8,128)(2,1)S(1)}, u32[]{:S(2)}, u32[]{:S(2)}) collective-permute-start(bf16[128,2048]{1,0:T(8,128)(2,1)} %collective-permute-done.19.refs_4_), channel_id=1, source_target_pairs={{0,1},{1,0},{2,3},{3,2},{4,5},{5,4},{6,7},{7,6},{8,9},{9,8},{10,11... | collective-permute-start | bytes 1572872 | tf_op jit(solution)/shard_map/ppermute | solution.py:37
  159.3 18.2 %collective-permute-start.35 = (bf16[256,1024]{1,0:T(8,128)(2,1)}, bf16[256,1024]{1,0:T(8,128)(2,1)S(1)}, u32[]{:S(2)}, u32[]{:S(2)}) collective-permute-start(bf16[256,1024]{1,0:T(8,128)(2,1)} %get-tuple-element.172), channel_id=1, source_target_pairs={{0,4},{4,0},{8,12},{12,8},{16,20},{20,16},{24,28},{28,24},{1,5},{5... | collective-permute-start | bytes 1572872 | tf_op jit(solution)/shard_map/ppermute | solution.py:37
  190.9 213.3 %reduce-scatter.6.cloned.1.call-start = ((), (), s32[]{:S(2)}) async-start(), calls=%async_computation.4 | async-start | bytes 5242880 | tf_op jit(solution)/shard_map/reduce_scatter | solution.py:760
  192.6 26.2 %collective-permute-start.40 = (bf16[256,1024]{1,0:T(8,128)(2,1)}, bf16[256,1024]{1,0:T(8,128)(2,1)S(1)}, u32[]{:S(2)}, u32[]{:S(2)}) collective-permute-start(bf16[256,1024]{1,0:T(8,128)(2,1)} %get-tuple-element.184), channel_id=1, source_target_pairs={{0,4},{4,0},{8,12},{12,8},{16,20},{20,16},{24,28},{28,24},{1,5},{5... | collective-permute-start | bytes 1572872 | tf_op jit(solution)/shard_map/ppermute | solution.py:37
  193.2 26.8 %collective-permute-start.39 = (bf16[256,1024]{1,0:T(8,128)(2,1)}, bf16[256,1024]{1,0:T(8,128)(2,1)}, u32[]{:S(2)}, u32[]{:S(2)}) collective-permute-start(bf16[256,1024]{1,0:T(8,128)(2,1)} %get-tuple-element.182), channel_id=1, source_target_pairs={{0,4},{4,0},{8,12},{12,8},{16,20},{20,16},{24,28},{28,24},{1,5},{5... | collective-permute-start | bytes 1572872 | tf_op jit(solution)/shard_map/ppermute | solution.py:37
  201.0 19.1 %collective-permute-start.41 = (bf16[128,2048]{1,0:T(8,128)(2,1)S(1)}, bf16[128,2048]{1,0:T(8,128)(2,1)S(1)}, u32[]{:S(2)}, u32[]{:S(2)}) collective-permute-start(bf16[128,2048]{1,0:T(8,128)(2,1)S(1)} %collective-permute-done.27.refs_4_), channel_id=1, source_target_pairs={{0,2},{1,3},{2,0},{3,1},{4,6},{5,7},{6,4},{7,5},{8,10},{9,11},{10,... | collective-permute-start | bytes 1572872 | tf_op jit(solution)/shard_map/ppermute | solution.py:37
  218.6 22.2 %collective-permute-start.45 = (bf16[128,2048]{1,0:T(8,128)(2,1)S(1)}, bf16[128,2048]{1,0:T(8,128)(2,1)S(1)}, u32[]{:S(2)}, u32[]{:S(2)}) collective-permute-start(bf16[128,2048]{1,0:T(8,128)(2,1)S(1)} %copy-done.15), channel_id=1, source_target_pairs={{0,4},{4,0},{8,12},{12,8},{16,20},{20,16},{24,28},{28,24},{1,5},{5... | collective-permute-start | bytes 1572872 | tf_op jit(solution)/shard_map/ppermute | solution.py:37
  218.8 22.0 %collective-permute-start.38 = (bf16[128,2048]{1,0:T(8,128)(2,1)S(1)}, bf16[128,2048]{1,0:T(8,128)(2,1)S(1)}, u32[]{:S(2)}, u32[]{:S(2)}) collective-permute-start(bf16[128,2048]{1,0:T(8,128)(2,1)S(1)} %collective-permute-done.17.refs_4_), channel_id=1, source_target_pairs={{0,2},{1,3},{2,0},{3,1},{4,6},{5,7},{6,4},{7,5},{8,10},{9,11},{10,... | collective-permute-start | bytes 1572872 | tf_op jit(solution)/shard_map/ppermute | solution.py:37
  220.0 20.8 %collective-permute-start.44 = (bf16[4,128,256]{2,1,0:T(8,128)(2,1)}, bf16[4,128,256]{2,1,0:T(8,128)(2,1)}, u32[]{:S(2)}, u32[]{:S(2)}) collective-permute-start(bf16[4,128,256]{2,1,0:T(8,128)(2,1)} %get-tuple-element.191), channel_id=1, source_target_pairs={{0,1},{1,0},{2,3},{3,2},{4,5},{5,4},{6,7},{7,6},{8,9},{9,8},{10,11... | collective-permute-start | bytes 786440 | tf_op jit(solution)/shard_map/ppermute | solution.py:37
  223.0 17.8 %collective-permute-start.43 = (bf16[4,128,256]{2,1,0:T(8,128)(2,1)}, bf16[4,128,256]{2,1,0:T(8,128)(2,1)S(1)}, u32[]{:S(2)}, u32[]{:S(2)}) collective-permute-start(bf16[4,128,256]{2,1,0:T(8,128)(2,1)} %shard_map.302), channel_id=1, source_target_pairs={{0,2},{1,3},{2,0},{3,1},{4,6},{5,7},{6,4},{7,5},{8,10},{9,11},{10,... | collective-permute-start | bytes 786440 | tf_op jit(solution)/shard_map/ppermute | solution.py:37
  252.5 24.8 %collective-permute-start.53 = (bf16[4,128,256]{2,1,0:T(8,128)(2,1)}, bf16[4,128,256]{2,1,0:T(8,128)(2,1)S(1)}, u32[]{:S(2)}, u32[]{:S(2)}) collective-permute-start(bf16[4,128,256]{2,1,0:T(8,128)(2,1)} %shard_map.306), channel_id=1, source_target_pairs={{0,16},{4,20},{8,24},{12,28},{16,0},{20,4},{24,8},{28,12},{1,17},{... | collective-permute-start | bytes 786440 | tf_op jit(solution)/shard_map/ppermute | solution.py:37
  278.1 143.2 %reduce-scatter.8.cloned.1.call-start = ((), (), s32[]{:S(2)}) async-start(), calls=%async_computation.5 | async-start | bytes 2621440 | tf_op jit(solution)/shard_map/reduce_scatter | solution.py:760
  280.2 18.4 %collective-permute-start.52 = (bf16[4,128,256]{2,1,0:T(8,128)(2,1)S(1)}, bf16[4,128,256]{2,1,0:T(8,128)(2,1)S(1)}, u32[]{:S(2)}, u32[]{:S(2)}) collective-permute-start(bf16[4,128,256]{2,1,0:T(8,128)(2,1)S(1)} %copy-done.52), channel_id=1, source_target_pairs={{0,2},{1,3},{2,0},{3,1},{4,6},{5,7},{6,4},{7,5},{8,10},{9,11},{10,... | collective-permute-start | bytes 786440 | tf_op jit(solution)/shard_map/ppermute | solution.py:37
  281.1 35.6 %collective-permute-start.55 = (bf16[128,2048]{1,0:T(8,128)(2,1)S(1)}, bf16[128,2048]{1,0:T(8,128)(2,1)}, u32[]{:S(2)}, u32[]{:S(2)}) collective-permute-start(bf16[128,2048]{1,0:T(8,128)(2,1)S(1)} %copy-done.33), channel_id=1, source_target_pairs={{0,2},{1,3},{2,0},{3,1},{4,6},{5,7},{6,4},{7,5},{8,10},{9,11},{10,... | collective-permute-start | bytes 1572872 | tf_op jit(solution)/shard_map/ppermute | solution.py:37
  301.3 23.3 %collective-permute-start.37 = (bf16[128,2048]{1,0:T(8,128)(2,1)S(1)}, bf16[128,2048]{1,0:T(8,128)(2,1)S(1)}, u32[]{:S(2)}, u32[]{:S(2)}) collective-permute-start(bf16[128,2048]{1,0:T(8,128)(2,1)S(1)} %collective-permute-done.17.refs_4_), channel_id=1, source_target_pairs={{0,1},{1,0},{2,3},{3,2},{4,5},{5,4},{6,7},{7,6},{8,9},{9,8},{10,11... | collective-permute-start | bytes 1572872 | tf_op jit(solution)/shard_map/ppermute | solution.py:37
  301.4 23.2 %collective-permute-start.75 = (bf16[128,2048]{1,0:T(8,128)(2,1)S(1)}, bf16[128,2048]{1,0:T(8,128)(2,1)}, u32[]{:S(2)}, u32[]{:S(2)}) collective-permute-start(bf16[128,2048]{1,0:T(8,128)(2,1)S(1)} %collective-permute-done.45.refs_14_), channel_id=1, source_target_pairs={{0,1},{1,0},{2,3},{3,2},{4,5},{5,4},{6,7},{7,6},{8,9},{9,8},{10,11... | collective-permute-start | bytes 1572872 | tf_op jit(solution)/shard_map/ppermute | solution.py:37
  301.9 22.7 %collective-permute-start.46 = (bf16[128,2048]{1,0:T(8,128)(2,1)S(1)}, bf16[128,2048]{1,0:T(8,128)(2,1)S(1)}, u32[]{:S(2)}, u32[]{:S(2)}) collective-permute-start(bf16[128,2048]{1,0:T(8,128)(2,1)S(1)} %collective-permute-done.38.refs_6_), channel_id=1, source_target_pairs={{0,1},{1,0},{2,3},{3,2},{4,5},{5,4},{6,7},{7,6},{8,9},{9,8},{10,11... | collective-permute-start | bytes 1572872 | tf_op jit(solution)/shard_map/ppermute | solution.py:37
  359.7 42.3 %collective-permute-start.82 = (bf16[1024,256]{1,0:T(8,128)(2,1)}, bf16[1024,256]{1,0:T(8,128)(2,1)S(1)}, u32[]{:S(2)}, u32[]{:S(2)}) collective-permute-start(bf16[1024,256]{1,0:T(8,128)(2,1)} %get-tuple-element.267), channel_id=1, source_target_pairs={{0,4},{4,0},{8,12},{12,8},{16,20},{20,16},{24,28},{28,24},{1,5},{5... | collective-permute-start | bytes 1572872 | tf_op jit(solution)/shard_map/ppermute | solution.py:37
  361.1 35.4 %collective-permute-start.66 = (bf16[128,2048]{1,0:T(8,128)(2,1)S(1)}, bf16[128,2048]{1,0:T(8,128)(2,1)S(1)}, u32[]{:S(2)}, u32[]{:S(2)}) collective-permute-start(bf16[128,2048]{1,0:T(8,128)(2,1)S(1)} %copy-done.35), channel_id=1, source_target_pairs={{0,2},{1,3},{2,0},{3,1},{4,6},{5,7},{6,4},{7,5},{8,10},{9,11},{10,... | collective-permute-start | bytes 1572872 | tf_op jit(solution)/shard_map/ppermute | solution.py:37
  362.4 34.1 %collective-permute-start.65 = (bf16[128,2048]{1,0:T(8,128)(2,1)}, bf16[128,2048]{1,0:T(8,128)(2,1)S(1)}, u32[]{:S(2)}, u32[]{:S(2)}) collective-permute-start(bf16[128,2048]{1,0:T(8,128)(2,1)} %get-tuple-element.234), channel_id=1, source_target_pairs={{0,1},{1,0},{2,3},{3,2},{4,5},{5,4},{6,7},{7,6},{8,9},{9,8},{10,11... | collective-permute-start | bytes 1572872 | tf_op jit(solution)/shard_map/ppermute | solution.py:37
  367.7 19.0 %collective-permute-start.64 = (bf16[256,256]{1,0:T(8,128)(2,1)}, bf16[256,256]{1,0:T(8,128)(2,1)S(1)}, u32[]{:S(2)}, u32[]{:S(2)}) collective-permute-start(bf16[256,256]{1,0:T(8,128)(2,1)} %shard_map.318.refs_0_), channel_id=1, source_target_pairs={{0,16},{4,20},{8,24},{12,28},{16,0},{20,4},{24,8},{28,12},{1,17},{... | collective-permute-start | bytes 393224 | tf_op jit(solution)/shard_map/ppermute | solution.py:37
  367.7 19.0 %collective-permute-start.68 = (f32[117,128]{1,0:T(8,128)S(1)}, f32[117,128]{1,0:T(8,128)S(1)}, u32[]{:S(2)}, u32[]{:S(2)}) collective-permute-start(f32[117,128]{1,0:T(8,128)S(1)} %bitcast_add_fusion), channel_id=1, source_target_pairs={{0,16},{4,20},{8,24},{12,28},{16,0},{20,4},{24,8},{28,12},{1,17},{... | collective-permute-start | bytes 179720 | tf_op jit(solution)/shard_map/ppermute | solution.py:37
  (126 other events, 1163.8 us)
Sparse Core Ops, SparseCore 0:
  191.0 82.5 reduce-scatter.3
  278.2 85.6 reduce-scatter.5
  366.8 45.9 reduce-scatter.7

commit v3 on v2

--- a/solution.py
+++ b/solution.py
@@ -814,7 +814,7 @@
     attended_grads = mark(
         call(attended_grads_kernel, struct(attended.shape, jnp.bfloat16), *mids_own, at(w_out))
     )
-    sum_p = group_sum(touch(part_p, mid_across))
+    sum_p = group_sum(touch(part_p, mid_beside))
     twos_other = half_gather(at(two_other))
     ones_other = half_gather(at(one_other))
     first_call, last_call = backward_calls(
@@ -854,7 +854,7 @@
     others = beside(sends)
     part_f, clock[0] = weight_grads(places, (twos, (at(low_keep0), low_keep1, low_other0, low_other1)))
     kv_slots, there = mark(add_split(at(kv_near[0], others, mid_others[2]), near_own, near_got, far_there))
-    sum_f = group_sum(touch(part_f, far_there))
+    sum_f = group_sum(touch(part_f, far_sum))
     there = swap(there, "seq", seq_bits[-2])
     mid_others = (*mid_others, core(at(mid_others[2])))
     one0, one1 = mark(

time: 448 us -> 459 us (1.025)
  the two profiles are of different devices: /device:TPU:26 before, /device:TPU:0 now
where the time goes in v3:
time: 459 us; the launch traced here: 451 us
  Pallas kernels  158 us (34%)
  waiting for transfers between devices  124 us (27%)
  starting transfers between devices  104 us (23%)
  local copies, waits for them, and re-layouts  36.4 us (8%)
  between operations  15.1 us (3%)
  other arithmetic  13 us (3%)
    ppermute x83, waiting for transfers between devices, swap(): return lax.ppermute(value, axis, [(j, j ^ bit) for j in range(count)])  124 us
    ppermute x83, starting transfers between devices, swap(): return lax.ppermute(value, axis, [(j, j ^ bit) for j in range(count)])  104 us
    pallas_call x23, Pallas kernels, call(): pl.pallas_call(kernel, out_shape=outs, compiler_params=pltpu.CompilerPara...  62.7 us
    pallas_call x2, Pallas kernels, mlp(): pl.pallas_call(functools.partial(mlp_kernel, tiles), grid_spec=pltpu.Pref...  35.1 us
    pallas_call x3, Pallas kernels, weight_grads(): pl.pallas_call(functools.partial(weight_kernel, [len(columns) for _, colu...  27.8 us
    unnamed x169, local copies, waits for them, and re-layouts  27.2 us
    pallas_call x3, Pallas kernels, attention_call(): pl.pallas_call(kernel, grid_spec=pltpu.PrefetchScalarGridSpec(num_scalar_...  21.1 us
  transfers between devices with their start and end apart: 86, of which 25 were waited for; matrix products, arithmetic and copies ran while one was open for 6% of the time, Pallas kernels for 32%

profile of v3, /device:TPU:0, one launch (start us, length us, event | category | flops | bytes accessed | tf_op | source)
XLA Modules:
  0.0 450.8 jit_solution(9469654137492286323)
XLA Ops:
  20.4 5.3 %collective-permute-done.9 = bf16[128,128]{1,0:T(8,128)(2,1)S(1)} collective-permute-done((bf16[128,128]{1,0:T(8,128)(2,1)}, bf16[128,128]{1,0:T(8,128)(2,1)S(1)}, u32[]{:S(2)}, u32[]{:S(2)}) %collective-permute-start.9) | collective-permute-done | bytes 32800 | tf_op jit(solution)/shard_map/ppermute | solution.py:37
  48.9 4.3 shard_map.289.q_ref
  56.3 6.6 %shard_map.290 = (bf16[512,512]{1,0:T(8,128)(2,1)}, f32[4,512]{1,0:T(4,128)}) custom-call(s32[3,8]{1,0:T(4,128)} %pad_add_fusion.1.meta, bf16[512,512]{1,0:T(8,128)(2,1)} %shard_map.289.q_ref, bf16[8,128,128]{2,1,0:T(8,128)(2,1)} %copy-done.5, bf16[8,128,128]{2,1,0:T(8,128)(2,1)} %copy-done.7, bf16[8,128,128]{2,1,0:T(8,128)(2,1)} %copy-done.6, ...), custom_call_target="tpu_custom_call" | custom-call | flops 1024 | bytes 1024 | tf_op jit(solution)/shard_map/pallas_call | solution.py:600
  62.9 3.5 shard_map.291
  66.4 3.5 shard_map.292
  74.9 3.4 collective-permute-start.17
  78.9 9.5 %collective-permute-done.16.p2 = bf16[128,2048]{1,0:T(8,128)(2,1)S(1)} collective-permute-done((bf16[128,2048]{1,0:T(8,128)(2,1)}, bf16[128,2048]{1,0:T(8,128)(2,1)S(1)}, u32[]{:S(2)}, u32[]{:S(2)}) %collective-permute-start.16) | collective-permute-done | bytes 524320 | tf_op jit(solution)/shard_map/ppermute | solution.py:37
  94.8 4.8 %collective-permute-done.24.g0.refs_2_ = bf16[128,2048]{1,0:T(8,128)(2,1)} collective-permute-done((bf16[128,2048]{1,0:T(8,128)(2,1)S(1)}, bf16[128,2048]{1,0:T(8,128)(2,1)}, u32[]{:S(2)}, u32[]{:S(2)}) %collective-permute-start.24) | collective-permute-done | bytes 524320 | tf_op jit(solution)/shard_map/ppermute | solution.py:37
  102.4 17.6 %shard_map.295 = (bf16[256,1024]{1,0:T(8,128)(2,1)}, bf16[256,1024]{1,0:T(8,128)(2,1)}, bf16[256,1024]{1,0:T(8,128)(2,1)}, bf16[256,1024]{1,0:T(8,128)(2,1)}, bf...) custom-call(s32[11]{0:T(128)} %concatenate.28.meta, ...), custom_call_target="tpu_custom_call" | custom-call | flops 1024 | bytes 1024 | tf_op jit(solution)/shard_map/pallas_call | solution.py:424
  125.5 17.4 %shard_map.296 = (bf16[256,1024]{1,0:T(8,128)(2,1)}, bf16[256,1024]{1,0:T(8,128)(2,1)}, bf16[256,1024]{1,0:T(8,128)(2,1)}, bf16[256,1024]{1,0:T(8,128)(2,1)}, bf...) custom-call(s32[11]{0:T(128)} %concatenate.28.meta, ...), custom_call_target="tpu_custom_call" | custom-call | flops 1024 | bytes 1024 | tf_op jit(solution)/shard_map/pallas_call | solution.py:424
  152.1 10.3 %collective-permute-done.30.p2 = bf16[128,2048]{1,0:T(8,128)(2,1)S(1)} collective-permute-done((bf16[128,2048]{1,0:T(8,128)(2,1)}, bf16[128,2048]{1,0:T(8,128)(2,1)S(1)}, u32[]{:S(2)}, u32[]{:S(2)}) %collective-permute-start.30) | collective-permute-done | bytes 524320 | tf_op jit(solution)/shard_map/ppermute | solution.py:37
  163.2 4.1 shard_map.298
  170.2 9.9 %shard_map.299 = (bf16[4,1024,512]{2,1,0:T(8,128)(2,1)}, f32[8,128]{1,0:T(8,128)}) custom-call(s32[11]{0:T(128)} %concatenate.28.meta, bf16[128,2048]{1,0:T(8,128)(2,1)} %refs_0_, bf16[128,2048]{1,0:T(8,128)(2,1)} %copy-done.20, bf16[128,2048]{1,0:T(8,128)(2,1)} %collective-permute-done.24.g0.refs_2_, bf16[128,2048]{1,0:T(8,128)(2,1)} %copy-done.23, ...), custom_call_target="tpu_custom_call" | custom-call | flops 1024 | bytes 1024 | tf_op jit(solution)/shard_map/pallas_call | solution.py:315
  183.5 12.4 %collective-permute-done.32.r2.refs_12_ = bf16[128,2048]{1,0:T(8,128)(2,1)S(1)} collective-permute-done((bf16[128,2048]{1,0:T(8,128)(2,1)S(1)}, bf16[128,2048]{1,0:T(8,128)(2,1)S(1)}, u32[]{:S(2)}, u32[]{:S(2)}) %collective-permute-start.32) | collective-permute-done | bytes 524320 | tf_op jit(solution)/shard_map/ppermute | solution.py:37
  198.7 4.6 %shard_map.300.refs_11_ = bf16[512,512]{1,0:T(8,128)(2,1)} custom-call(bf16[128,2048]{1,0:T(8,128)(2,1)} %get-tuple-element.192.r0.refs_10_, bf16[128,2048]{1,0:T(8,128)(2,1)} %copy-done.16, bf16[128,2048]{1,0:T(8,128)(2,1)} %copy-done.17, bf16[128,2048]{1,0:T(8,128)(2,1)} %copy-done.18, bf16[512,2048]{1,0:T(8,128)(2,1)} %w_ref.11), custom_call_target="tpu_custom_call" | custom-call | flops 1024 | bytes 1024 | tf_op jit(solution)/shard_map/pallas_call | solution.py:80
  205.0 5.7 %shard_map.301 = (f32[4,128,512]{2,1,0:T(8,128)}, f32[4,512]{1,0:T(4,128)}, bf16[4,128,256]{2,1,0:T(8,128)(2,1)}, bf16[4,128,256]{2,1,0:T(8,128)(2,1)}, bf16[4,1...) custom-call(s32[3,8]{1,0:T(4,128)} %pad_add_fusion.1.meta, bf16[512,512]{1,0:T(8,128)(2,1)} %shard_map.289.q_ref, ...), custom_call_target="tpu_custom_call" | custom-call | flops 1024 | bytes 1024 | tf_op jit(solution)/shard_map/pallas_call | solution.py:600
  213.1 9.1 %collective-permute-done.39.refs_10_ = bf16[256,1024]{1,0:T(8,128)(2,1)S(1)} collective-permute-done((bf16[256,1024]{1,0:T(8,128)(2,1)}, bf16[256,1024]{1,0:T(8,128)(2,1)S(1)}, u32[]{:S(2)}, u32[]{:S(2)}) %collective-permute-start.39) | collective-permute-done | bytes 524320 | tf_op jit(solution)/shard_map/ppermute | solution.py:37
  226.2 8.9 %shard_map.303 = (bf16[512,512]{1,0:T(8,128)(2,1)}, f32[1,512]{1,0:T(1,128)}, bf16[4,128,256]{2,1,0:T(8,128)(2,1)}, bf16[4,128,256]{2,1,0:T(8,128)(2,1)}, bf16[4...) custom-call(s32[3,8]{1,0:T(4,128)} %pad_add_fusion.1.meta, bf16[512,512]{1,0:T(8,128)(2,1)} %shard_map.289.q_ref, ...), custom_call_target="tpu_custom_call" | custom-call | flops 1024 | bytes 1024 | tf_op jit(solution)/shard_map/pallas_call | solution.py:600
  235.2 3.9 shard_map.304
  253.7 9.9 %shard_map.321 = (bf16[4,1024,512]{2,1,0:T(8,128)(2,1)}, f32[8,128]{1,0:T(8,128)}) custom-call(s32[11]{0:T(128)} %concatenate.28.meta, bf16[128,2048]{1,0:T(8,128)(2,1)} %get-tuple-element.154.x0.refs_0_, bf16[128,2048]{1,0:T(8,128)(2,1)} %copy-done.11, bf16[128,2048]{1,0:T(8,128)(2,1)} %copy-done.13, bf16[128,2048]{1,0:T(8,128)(2,1)} %copy-done.19, ...), custom_call_target="tpu_custom_call" | custom-call | flops 1024 | bytes 1024 | tf_op jit(solution)/shard_map/pallas_call | solution.py:315
  264.3 4.4 collective-permute-start.49
  268.7 10.1 %collective-permute-start.53 = (bf16[4,128,256]{2,1,0:T(8,128)(2,1)}, bf16[4,128,256]{2,1,0:T(8,128)(2,1)S(1)}, u32[]{:S(2)}, u32[]{:S(2)}) collective-permute-start(bf16[4,128,256]{2,1,0:T(8,128)(2,1)} %shard_map.306), channel_id=1, source_target_pairs={{0,16},{4,20},{8,24},{12,28},{16,0},{20,4},{24,8},{28,12},{1,17},{... | collective-permute-start | bytes 786440 | tf_op jit(solution)/shard_map/ppermute | solution.py:37
  281.0 5.1 %collective-permute-done.53.refs_3_ = bf16[4,128,256]{2,1,0:T(8,128)(2,1)S(1)} collective-permute-done((bf16[4,128,256]{2,1,0:T(8,128)(2,1)}, bf16[4,128,256]{2,1,0:T(8,128)(2,1)S(1)}, u32[]{:S(2)}, u32[]{:S(2)}) %collective-permute-start.53) | collective-permute-done | bytes 262176 | tf_op jit(solution)/shard_map/ppermute | solution.py:37
  290.3 21.6 %collective-permute-start.54 = (bf16[2,128,256]{2,1,0:T(8,128)(2,1)}, bf16[2,128,256]{2,1,0:T(8,128)(2,1)S(1)}, u32[]{:S(2)}, u32[]{:S(2)}) collective-permute-start(bf16[2,128,256]{2,1,0:T(8,128)(2,1)} %get-tuple-element.210), channel_id=1, source_target_pairs={{0,8},{4,12},{8,0},{12,4},{16,24},{20,28},{24,16},{28,20},{1,9},{5... | collective-permute-start | bytes 393224 | tf_op jit(solution)/shard_map/ppermute | solution.py:37
  312.5 7.8 %collective-permute-done.54.refs_1_ = bf16[2,128,256]{2,1,0:T(8,128)(2,1)S(1)} collective-permute-done((bf16[2,128,256]{2,1,0:T(8,128)(2,1)}, bf16[2,128,256]{2,1,0:T(8,128)(2,1)S(1)}, u32[]{:S(2)}, u32[]{:S(2)}) %collective-permute-start.54) | collective-permute-done | bytes 131104 | tf_op jit(solution)/shard_map/ppermute | solution.py:37
  324.5 3.4 shard_map.312
  331.0 8.0 %shard_map.324 = (bf16[4,512,512]{2,1,0:T(8,128)(2,1)}, f32[8,128]{1,0:T(8,128)}) custom-call(s32[11]{0:T(128)} %concatenate.28.meta, bf16[128,2048]{1,0:T(8,128)(2,1)} %get-tuple-element.153.r0.refs_0_, bf16[128,2048]{1,0:T(8,128)(2,1)} %copy-done.2, bf16[128,2048]{1,0:T(8,128)(2,1)} %copy-done.1, bf16[128,2048]{1,0:T(8,128)(2,1)} %copy-done.3, ...), custom_call_target="tpu_custom_call" | custom-call | flops 1024 | bytes 1024 | tf_op jit(solution)/shard_map/pallas_call | solution.py:315
  342.8 4.2 shard_map.313
  371.9 5.2 %collective-permute-start.64 = (bf16[256,256]{1,0:T(8,128)(2,1)}, bf16[256,256]{1,0:T(8,128)(2,1)S(1)}, u32[]{:S(2)}, u32[]{:S(2)}) collective-permute-start(bf16[256,256]{1,0:T(8,128)(2,1)} %shard_map.318.refs_0_), channel_id=1, source_target_pairs={{0,16},{4,20},{8,24},{12,28},{16,0},{20,4},{24,8},{28,12},{1,17},{... | collective-permute-start | bytes 393224 | tf_op jit(solution)/shard_map/ppermute | solution.py:37
  377.2 21.0 %collective-permute-done.68 = f32[117,128]{1,0:T(8,128)S(1)} collective-permute-done((f32[117,128]{1,0:T(8,128)S(1)}, f32[117,128]{1,0:T(8,128)S(1)}, u32[]{:S(2)}, u32[]{:S(2)}) %collective-permute-start.68) | collective-permute-done | bytes 59936 | tf_op jit(solution)/shard_map/ppermute | solution.py:37
  422.5 9.1 %collective-permute-done.77 = bf16[1024,256]{1,0:T(8,128)(2,1)S(1)} collective-permute-done((bf16[1024,256]{1,0:T(8,128)(2,1)}, bf16[1024,256]{1,0:T(8,128)(2,1)S(1)}, u32[]{:S(2)}, u32[]{:S(2)}) %collective-permute-start.77) | collective-permute-done | bytes 524320 | tf_op jit(solution)/shard_map/ppermute | solution.py:37
  437.6 4.3 collective-permute-done.81
  (400 shorter events, 176.8 us)
Async XLA Ops:
  7.2 340.8 %reduce-scatter.4.cloned.1.call-start = ((), (), s32[]{:S(2)}) async-start(), calls=%async_computation.3 | async-start | bytes 5242880 | tf_op jit(solution)/shard_map/reduce_scatter | solution.py:760
  9.9 35.3 %collective-permute-start.1 = (bf16[128,2048]{1,0:T(8,128)(2,1)}, bf16[128,2048]{1,0:T(8,128)(2,1)S(1)}, u32[]{:S(2)}, u32[]{:S(2)}) collective-permute-start(bf16[128,2048]{1,0:T(8,128)(2,1)} %get-tuple-element.153.r0.refs_0_), channel_id=1, source_target_pairs={{0,2},{1,3},{2,0},{3,1},{4,6},{5,7},{6,4},{7,5},{8,10},{9,11},{10,... | collective-permute-start | bytes 1572872 | tf_op jit(solution)/shard_map/ppermute | solution.py:37
  12.8 35.1 %collective-permute-start = (bf16[128,2048]{1,0:T(8,128)(2,1)}, bf16[128,2048]{1,0:T(8,128)(2,1)S(1)}, u32[]{:S(2)}, u32[]{:S(2)}) collective-permute-start(bf16[128,2048]{1,0:T(8,128)(2,1)} %get-tuple-element.153.r0.refs_0_), channel_id=1, source_target_pairs={{0,1},{1,0},{2,3},{3,2},{4,5},{5,4},{6,7},{7,6},{8,9},{9,8},{10,11... | collective-permute-start | bytes 1572872 | tf_op jit(solution)/shard_map/ppermute | solution.py:37
  74.9 17.8 %collective-permute-start.17 = (bf16[128,2048]{1,0:T(8,128)(2,1)S(1)}, bf16[128,2048]{1,0:T(8,128)(2,1)S(1)}, u32[]{:S(2)}, u32[]{:S(2)}) collective-permute-start(bf16[128,2048]{1,0:T(8,128)(2,1)S(1)} %copy-done), channel_id=1, source_target_pairs={{0,4},{4,0},{8,12},{12,8},{16,20},{20,16},{24,28},{28,24},{1,5},{5... | collective-permute-start | bytes 1572872 | tf_op jit(solution)/shard_map/ppermute | solution.py:37
  78.3 23.1 %collective-permute-start.19 = (bf16[128,2048]{1,0:T(8,128)(2,1)S(1)}, bf16[128,2048]{1,0:T(8,128)(2,1)S(1)}, u32[]{:S(2)}, u32[]{:S(2)}) collective-permute-start(bf16[128,2048]{1,0:T(8,128)(2,1)S(1)} %copy-done.4), channel_id=1, source_target_pairs={{0,4},{4,0},{8,12},{12,8},{16,20},{20,16},{24,28},{28,24},{1,5},{5... | collective-permute-start | bytes 1572872 | tf_op jit(solution)/shard_map/ppermute | solution.py:37
  78.3 21.3 %collective-permute-start.24 = (bf16[128,2048]{1,0:T(8,128)(2,1)S(1)}, bf16[128,2048]{1,0:T(8,128)(2,1)}, u32[]{:S(2)}, u32[]{:S(2)}) collective-permute-start(bf16[128,2048]{1,0:T(8,128)(2,1)S(1)} %copy-done.4), channel_id=1, source_target_pairs={{0,2},{1,3},{2,0},{3,1},{4,6},{5,7},{6,4},{7,5},{8,10},{9,11},{10,... | collective-permute-start | bytes 1572872 | tf_op jit(solution)/shard_map/ppermute | solution.py:37
  92.7 27.3 %collective-permute-start.22 = (bf16[128,2048]{1,0:T(8,128)(2,1)}, bf16[128,2048]{1,0:T(8,128)(2,1)S(1)}, u32[]{:S(2)}, u32[]{:S(2)}) collective-permute-start(bf16[128,2048]{1,0:T(8,128)(2,1)} %get-tuple-element.154.x0.refs_0_), channel_id=1, source_target_pairs={{0,2},{1,3},{2,0},{3,1},{4,6},{5,7},{6,4},{7,5},{8,10},{9,11},{10,... | collective-permute-start | bytes 1572872 | tf_op jit(solution)/shard_map/ppermute | solution.py:37
  99.7 24.2 %collective-permute-start.25 = (bf16[128,2048]{1,0:T(8,128)(2,1)}, bf16[128,2048]{1,0:T(8,128)(2,1)S(1)}, u32[]{:S(2)}, u32[]{:S(2)}) collective-permute-start(bf16[128,2048]{1,0:T(8,128)(2,1)} %collective-permute-done.24.g0.refs_2_), channel_id=1, source_target_pairs={{0,1},{1,0},{2,3},{3,2},{4,5},{5,4},{6,7},{7,6},{8,9},{9,8},{10,11... | collective-permute-start | bytes 1572872 | tf_op jit(solution)/shard_map/ppermute | solution.py:37
  120.1 23.4 %collective-permute-start.27 = (bf16[128,2048]{1,0:T(8,128)(2,1)S(1)}, bf16[128,2048]{1,0:T(8,128)(2,1)S(1)}, u32[]{:S(2)}, u32[]{:S(2)}) collective-permute-start(bf16[128,2048]{1,0:T(8,128)(2,1)S(1)} %copy-done.10), channel_id=1, source_target_pairs={{0,4},{4,0},{8,12},{12,8},{16,20},{20,16},{24,28},{28,24},{1,5},{5... | collective-permute-start | bytes 1572872 | tf_op jit(solution)/shard_map/ppermute | solution.py:37
  122.3 21.2 %collective-permute-start.28 = (bf16[128,2048]{1,0:T(8,128)(2,1)S(1)}, bf16[128,2048]{1,0:T(8,128)(2,1)}, u32[]{:S(2)}, u32[]{:S(2)}) collective-permute-start(bf16[128,2048]{1,0:T(8,128)(2,1)S(1)} %collective-permute-done.19.refs_4_), channel_id=1, source_target_pairs={{0,2},{1,3},{2,0},{3,1},{4,6},{5,7},{6,4},{7,5},{8,10},{9,11},{10,... | collective-permute-start | bytes 1572872 | tf_op jit(solution)/shard_map/ppermute | solution.py:37
  123.9 22.0 %collective-permute-start.26 = (bf16[256,1024]{1,0:T(8,128)(2,1)}, bf16[256,1024]{1,0:T(8,128)(2,1)}, u32[]{:S(2)}, u32[]{:S(2)}) collective-permute-start(bf16[256,1024]{1,0:T(8,128)(2,1)} %get-tuple-element.161), channel_id=1, source_target_pairs={{0,4},{4,0},{8,12},{12,8},{16,20},{20,16},{24,28},{28,24},{1,5},{5... | collective-permute-start | bytes 1572872 | tf_op jit(solution)/shard_map/ppermute | solution.py:37
  150.3 17.5 %collective-permute-start.33 = (bf16[128,2048]{1,0:T(8,128)(2,1)S(1)}, bf16[128,2048]{1,0:T(8,128)(2,1)S(1)}, u32[]{:S(2)}, u32[]{:S(2)}) collective-permute-start(bf16[128,2048]{1,0:T(8,128)(2,1)S(1)} %collective-permute-done.19.refs_4_), channel_id=1, source_target_pairs={{0,1},{1,0},{2,3},{3,2},{4,5},{5,4},{6,7},{7,6},{8,9},{9,8},{10,11... | collective-permute-start | bytes 1572872 | tf_op jit(solution)/shard_map/ppermute | solution.py:37
  150.3 17.5 %collective-permute-start.35 = (bf16[256,1024]{1,0:T(8,128)(2,1)}, bf16[256,1024]{1,0:T(8,128)(2,1)S(1)}, u32[]{:S(2)}, u32[]{:S(2)}) collective-permute-start(bf16[256,1024]{1,0:T(8,128)(2,1)} %get-tuple-element.172), channel_id=1, source_target_pairs={{0,4},{4,0},{8,12},{12,8},{16,20},{20,16},{24,28},{28,24},{1,5},{5... | collective-permute-start | bytes 1572872 | tf_op jit(solution)/shard_map/ppermute | solution.py:37
  180.9 233.9 %reduce-scatter.6.cloned.1.call-start = ((), (), s32[]{:S(2)}) async-start(), calls=%async_computation.4 | async-start | bytes 5242880 | tf_op jit(solution)/shard_map/reduce_scatter | solution.py:760
  197.8 24.4 %collective-permute-start.39 = (bf16[256,1024]{1,0:T(8,128)(2,1)}, bf16[256,1024]{1,0:T(8,128)(2,1)S(1)}, u32[]{:S(2)}, u32[]{:S(2)}) collective-permute-start(bf16[256,1024]{1,0:T(8,128)(2,1)} %get-tuple-element.182), channel_id=1, source_target_pairs={{0,4},{4,0},{8,12},{12,8},{16,20},{20,16},{24,28},{28,24},{1,5},{5... | collective-permute-start | bytes 1572872 | tf_op jit(solution)/shard_map/ppermute | solution.py:37
  203.3 18.8 %collective-permute-start.41 = (bf16[128,2048]{1,0:T(8,128)(2,1)S(1)}, bf16[128,2048]{1,0:T(8,128)(2,1)}, u32[]{:S(2)}, u32[]{:S(2)}) collective-permute-start(bf16[128,2048]{1,0:T(8,128)(2,1)S(1)} %collective-permute-done.27.refs_4_), channel_id=1, source_target_pairs={{0,2},{1,3},{2,0},{3,1},{4,6},{5,7},{6,4},{7,5},{8,10},{9,11},{10,... | collective-permute-start | bytes 1572872 | tf_op jit(solution)/shard_map/ppermute | solution.py:37
  210.7 24.5 %collective-permute-start.45 = (bf16[128,2048]{1,0:T(8,128)(2,1)S(1)}, bf16[128,2048]{1,0:T(8,128)(2,1)S(1)}, u32[]{:S(2)}, u32[]{:S(2)}) collective-permute-start(bf16[128,2048]{1,0:T(8,128)(2,1)S(1)} %copy-done.15), channel_id=1, source_target_pairs={{0,4},{4,0},{8,12},{12,8},{16,20},{20,16},{24,28},{28,24},{1,5},{5... | collective-permute-start | bytes 1572872 | tf_op jit(solution)/shard_map/ppermute | solution.py:37
  212.2 23.0 %collective-permute-start.38 = (bf16[128,2048]{1,0:T(8,128)(2,1)S(1)}, bf16[128,2048]{1,0:T(8,128)(2,1)S(1)}, u32[]{:S(2)}, u32[]{:S(2)}) collective-permute-start(bf16[128,2048]{1,0:T(8,128)(2,1)S(1)} %collective-permute-done.17.refs_4_), channel_id=1, source_target_pairs={{0,2},{1,3},{2,0},{3,1},{4,6},{5,7},{6,4},{7,5},{8,10},{9,11},{10,... | collective-permute-start | bytes 1572872 | tf_op jit(solution)/shard_map/ppermute | solution.py:37
  263.7 168.2 %reduce-scatter.8.cloned.1.call-start = ((), (), s32[]{:S(2)}) async-start(), calls=%async_computation.5 | async-start | bytes 2621440 | tf_op jit(solution)/shard_map/reduce_scatter | solution.py:760
  263.7 16.6 %collective-permute-start.50 = (bf16[128,2048]{1,0:T(8,128)(2,1)S(1)}, bf16[128,2048]{1,0:T(8,128)(2,1)S(1)}, u32[]{:S(2)}, u32[]{:S(2)}) collective-permute-start(bf16[128,2048]{1,0:T(8,128)(2,1)S(1)} %collective-permute-done.45.refs_14_), channel_id=1, source_target_pairs={{0,2},{1,3},{2,0},{3,1},{4,6},{5,7},{6,4},{7,5},{8,10},{9,11},{10,... | collective-permute-start | bytes 1572872 | tf_op jit(solution)/shard_map/ppermute | solution.py:37
  264.3 16.6 %collective-permute-start.49 = (bf16[512,512]{1,0:T(8,128)(2,1)}, bf16[512,512]{1,0:T(8,128)(2,1)S(1)}, u32[]{:S(2)}, u32[]{:S(2)}) collective-permute-start(bf16[512,512]{1,0:T(8,128)(2,1)} %get-tuple-element.205), channel_id=1, source_target_pairs={{0,4},{4,0},{8,12},{12,8},{16,20},{20,16},{24,28},{28,24},{1,5},{5... | collective-permute-start | bytes 1572872 | tf_op jit(solution)/shard_map/ppermute | solution.py:37
  268.7 17.3 %collective-permute-start.53 = (bf16[4,128,256]{2,1,0:T(8,128)(2,1)}, bf16[4,128,256]{2,1,0:T(8,128)(2,1)S(1)}, u32[]{:S(2)}, u32[]{:S(2)}) collective-permute-start(bf16[4,128,256]{2,1,0:T(8,128)(2,1)} %shard_map.306), channel_id=1, source_target_pairs={{0,16},{4,20},{8,24},{12,28},{16,0},{20,4},{24,8},{28,12},{1,17},{... | collective-permute-start | bytes 786440 | tf_op jit(solution)/shard_map/ppermute | solution.py:37
  280.3 42.3 %collective-permute-start.55 = (bf16[128,2048]{1,0:T(8,128)(2,1)S(1)}, bf16[128,2048]{1,0:T(8,128)(2,1)}, u32[]{:S(2)}, u32[]{:S(2)}) collective-permute-start(bf16[128,2048]{1,0:T(8,128)(2,1)S(1)} %copy-done.35), channel_id=1, source_target_pairs={{0,2},{1,3},{2,0},{3,1},{4,6},{5,7},{6,4},{7,5},{8,10},{9,11},{10,... | collective-permute-start | bytes 1572872 | tf_op jit(solution)/shard_map/ppermute | solution.py:37
  290.3 30.0 %collective-permute-start.54 = (bf16[2,128,256]{2,1,0:T(8,128)(2,1)}, bf16[2,128,256]{2,1,0:T(8,128)(2,1)S(1)}, u32[]{:S(2)}, u32[]{:S(2)}) collective-permute-start(bf16[2,128,256]{2,1,0:T(8,128)(2,1)} %get-tuple-element.210), channel_id=1, source_target_pairs={{0,8},{4,12},{8,0},{12,4},{16,24},{20,28},{24,16},{28,20},{1,9},{5... | collective-permute-start | bytes 393224 | tf_op jit(solution)/shard_map/ppermute | solution.py:37
  311.9 18.2 %collective-permute-start.37 = (bf16[128,2048]{1,0:T(8,128)(2,1)S(1)}, bf16[128,2048]{1,0:T(8,128)(2,1)S(1)}, u32[]{:S(2)}, u32[]{:S(2)}) collective-permute-start(bf16[128,2048]{1,0:T(8,128)(2,1)S(1)} %collective-permute-done.17.refs_4_), channel_id=1, source_target_pairs={{0,1},{1,0},{2,3},{3,2},{4,5},{5,4},{6,7},{7,6},{8,9},{9,8},{10,11... | collective-permute-start | bytes 1572872 | tf_op jit(solution)/shard_map/ppermute | solution.py:37
  311.9 18.2 %collective-permute-start.75 = (bf16[128,2048]{1,0:T(8,128)(2,1)S(1)}, bf16[128,2048]{1,0:T(8,128)(2,1)}, u32[]{:S(2)}, u32[]{:S(2)}) collective-permute-start(bf16[128,2048]{1,0:T(8,128)(2,1)S(1)} %collective-permute-done.45.refs_14_), channel_id=1, source_target_pairs={{0,1},{1,0},{2,3},{3,2},{4,5},{5,4},{6,7},{7,6},{8,9},{9,8},{10,11... | collective-permute-start | bytes 1572872 | tf_op jit(solution)/shard_map/ppermute | solution.py:37
  312.4 17.6 %collective-permute-start.46 = (bf16[128,2048]{1,0:T(8,128)(2,1)S(1)}, bf16[128,2048]{1,0:T(8,128)(2,1)S(1)}, u32[]{:S(2)}, u32[]{:S(2)}) collective-permute-start(bf16[128,2048]{1,0:T(8,128)(2,1)S(1)} %collective-permute-done.38.refs_6_), channel_id=1, source_target_pairs={{0,1},{1,0},{2,3},{3,2},{4,5},{5,4},{6,7},{7,6},{8,9},{9,8},{10,11... | collective-permute-start | bytes 1572872 | tf_op jit(solution)/shard_map/ppermute | solution.py:37
  365.1 47.5 %collective-permute-start.82 = (bf16[1024,256]{1,0:T(8,128)(2,1)}, bf16[1024,256]{1,0:T(8,128)(2,1)S(1)}, u32[]{:S(2)}, u32[]{:S(2)}) collective-permute-start(bf16[1024,256]{1,0:T(8,128)(2,1)} %get-tuple-element.267), channel_id=1, source_target_pairs={{0,4},{4,0},{8,12},{12,8},{16,20},{20,16},{24,28},{28,24},{1,5},{5... | collective-permute-start | bytes 1572872 | tf_op jit(solution)/shard_map/ppermute | solution.py:37
  366.8 41.0 %collective-permute-start.66 = (bf16[128,2048]{1,0:T(8,128)(2,1)S(1)}, bf16[128,2048]{1,0:T(8,128)(2,1)S(1)}, u32[]{:S(2)}, u32[]{:S(2)}) collective-permute-start(bf16[128,2048]{1,0:T(8,128)(2,1)S(1)} %copy-done.36), channel_id=1, source_target_pairs={{0,2},{1,3},{2,0},{3,1},{4,6},{5,7},{6,4},{7,5},{8,10},{9,11},{10,... | collective-permute-start | bytes 1572872 | tf_op jit(solution)/shard_map/ppermute | solution.py:37
  367.9 39.9 %collective-permute-start.65 = (bf16[128,2048]{1,0:T(8,128)(2,1)S(1)}, bf16[128,2048]{1,0:T(8,128)(2,1)S(1)}, u32[]{:S(2)}, u32[]{:S(2)}) collective-permute-start(bf16[128,2048]{1,0:T(8,128)(2,1)S(1)} %copy-done.71), channel_id=1, source_target_pairs={{0,1},{1,0},{2,3},{3,2},{4,5},{5,4},{6,7},{7,6},{8,9},{9,8},{10,11... | collective-permute-start | bytes 1572872 | tf_op jit(solution)/shard_map/ppermute | solution.py:37
  371.9 26.3 %collective-permute-start.64 = (bf16[256,256]{1,0:T(8,128)(2,1)}, bf16[256,256]{1,0:T(8,128)(2,1)S(1)}, u32[]{:S(2)}, u32[]{:S(2)}) collective-permute-start(bf16[256,256]{1,0:T(8,128)(2,1)} %shard_map.318.refs_0_), channel_id=1, source_target_pairs={{0,16},{4,20},{8,24},{12,28},{16,0},{20,4},{24,8},{28,12},{1,17},{... | collective-permute-start | bytes 393224 | tf_op jit(solution)/shard_map/ppermute | solution.py:37
  377.1 21.1 %collective-permute-start.68 = (f32[117,128]{1,0:T(8,128)S(1)}, f32[117,128]{1,0:T(8,128)S(1)}, u32[]{:S(2)}, u32[]{:S(2)}) collective-permute-start(f32[117,128]{1,0:T(8,128)S(1)} %bitcast_add_fusion), channel_id=1, source_target_pairs={{0,16},{4,20},{8,24},{12,28},{16,0},{20,4},{24,8},{28,12},{1,17},{... | collective-permute-start | bytes 179720 | tf_op jit(solution)/shard_map/ppermute | solution.py:37
  (128 other events, 1336.3 us)
Sparse Core Ops, SparseCore 0:
  181.0 88.4 reduce-scatter.3
  271.9 92.8 reduce-scatter.5
  367.7 49.7 reduce-scatter.7
